TPU v7x, 32 devices: a whole 2x2x4 slice. The times are simulated.
32 devices in a mesh: lat: 4 (over y, x), lon: 8 (over z, core).
Axes of the slice: x: 2, y: 2, z: 4, core: 2. Of those that a mesh axis runs over, the one named last changes fastest.
Arguments:
- conc: bfloat16 [128, 64, 2048], P('lat', None, 'lon'), may hold values from -6 to 6
- dep_owner: int32 [8, 128, 4], P('lon', 'lat'), may hold values from 0 to 14, all different within a row; in each aligned block of 32 rows (0 to 31, 32 to 63, ..., all dimensions but the last counted through in order) at most 17 rows name the same one
- dep_row: int32 [8, 128, 4], P('lon', 'lat'), may hold values from 0 to 31
- dep_weight: float32 [8, 128, 4], P('lon', 'lat'), may hold values from 0.05 to 0.5
- dep_count: int32 [8, 128], P('lon', 'lat'), may hold values from 1 to 4
- zonal_offset: int32 [128], P('lat'), may hold values from -2 to 2
- agg_rates: float32 [4, 128, 2048], P(None, 'lat', 'lon'), may hold values from 0.1 to 1
- toeplitz: bfloat16 [4, 127], replicated, may hold values from -0.75 to 0.75
- settle: float32 [64], replicated, may hold values from 0.05 to 0.5
- kappa: float32 [128, 2048], P('lat', 'lon'), may hold values from 0.02 to 0.2
Outputs:
- updated: float32 [128, 64, 2048], P('lat', None, 'lon')
Inputs may be any that keep to these rules, and one draw needn't show every extreme that they name: `dep_owner`: the 4 entries of a row name different neighbour blocks; among the rows of one device no neighbour block is named by more than 17 entries, and in some device's rows one is named exactly 17 times; every value is named somewhere. `dep_count`: entries of a row at or past its count are padding.
All inputs are finite; a program needn't handle non-finite values.
Results may differ from a plain program's by a relative error of at most 0.00092.
Values may be sent and summed in bfloat16 or wider, within the bound.
No kernel may reach another device: no remote copies, remote signals or barrier semaphores. Data moves between devices by JAX's collectives and lax.ppermute only.
A program may use at most 64 MiB of HBM per device.

v0:
```python
import functools

import jax
import jax.numpy as jnp
from jax import lax
from jax.experimental import pallas as pl
from jax.experimental.pallas import tpu as pltpu
from jax.sharding import PartitionSpec as P

REACH = 2
NEAR_LON = 5
UNROLL = 4
VMEM_BYTES = 12 * 1024 * 1024
MOST_BYTES = 60 * 1024 * 1024
TABLE_BYTES = 20 * 1024 * 1024
QUICK = 2
FIELDS = ((0, 0), (0, 128), (8, 0), (8, 128), (16, 0))


def exchange(value, axis, pairs):
    return lax.ppermute(value, axis, [(i, j) for i, j in pairs] + [(j, i) for i, j in pairs])


def swap_core(value):
    return exchange(value, "lon", [(i, i + 1) for i in range(0, lax.axis_size("lon"), 2)])


def swap_across(value):
    count = lax.axis_size("lon")
    return exchange(value, "lon", [(i, (i + 1) % count) for i in range(1, count, 2)])


def swap_chip(value, second):
    count = lax.axis_size("lon")
    firsts = [i for i in range(count) if (i // 2) % 2 == second]
    return exchange(value, "lon", [(i, (i + 2) % count) for i in firsts])


def swap_lat(value, second):
    count = lax.axis_size("lat")
    return exchange(value, "lat", [(i, i + 1) for i in range(second, count - 1, 2)])


def in_smem():
    return pl.BlockSpec(memory_space=pltpu.SMEM)


def in_place():
    return pl.BlockSpec(memory_space=pl.ANY)


def for_rows(count, one):
    def some(g, carry):
        stores = []
        for u in range(UNROLL):
            stores += one(g * UNROLL + u)
        for ref, at, value in stores:
            ref[at] = value.astype(ref.dtype)
        return carry

    lax.fori_loop(0, count // UNROLL, some, 0)


def growth_kernel(flip_ref, settle_ref, conc_ref, rates_ref, out_ref, mat_ref):
    ranks, rows_step = rates_ref.shape[0], conc_ref.shape[0]
    bins, width = conc_ref.shape[1:]

    @pl.when(pl.program_id(0) == 0)
    def _():
        for q in range(ranks):
            spread = jnp.broadcast_to(flip_ref[q : q + 1, :], (bins, 2 * bins))
            turned = pltpu.roll(spread, bins + 1, 1, stride=1, stride_axis=0)
            mat_ref[q * bins : (q + 1) * bins, :] = turned[:, :bins].astype(jnp.bfloat16)

    settle = jnp.broadcast_to(settle_ref[...], (bins, width))
    for r in range(rows_step):
        cells = conc_ref[r]
        product = jnp.dot(mat_ref[...], cells, preferred_element_type=jnp.float32)
        total = -settle * cells.astype(jnp.float32)
        for q in range(ranks):
            total = total + rates_ref[q, r : r + 1, :] * product[q * bins : (q + 1) * bins]
        out_ref[r] = total


def local_terms(conc, agg_rates, toeplitz, settle):
    rows, bins, width = conc.shape
    ranks = agg_rates.shape[0]
    step = 8
    flipped = jnp.pad(toeplitz[:, ::-1].astype(jnp.float32), ((0, 0), (0, 1)))
    return pl.pallas_call(
        growth_kernel,
        grid=(rows // step,),
        in_specs=[
            pl.BlockSpec((ranks, 2 * bins), lambda i: (0, 0)),
            pl.BlockSpec((bins, 1), lambda i: (0, 0)),
            pl.BlockSpec((step, bins, width), lambda i: (i, 0, 0)),
            pl.BlockSpec((ranks, step, width), lambda i: (0, i, 0)),
        ],
        out_specs=pl.BlockSpec((step, bins, width), lambda i: (i, 0, 0)),
        out_shape=jax.ShapeDtypeStruct(conc.shape, jnp.float32),
        scratch_shapes=[pltpu.VMEM((ranks * bins, bins), jnp.bfloat16)],
        compiler_params=pltpu.CompilerParams(vmem_limit_bytes=VMEM_BYTES),
        cost_estimate=pl.CostEstimate(
            flops=2 * ranks * bins * bins * rows * width, bytes_accessed=8 * conc.size, transcendentals=0
        ),
        name="growth",
    )(flipped, settle[:, None], conc, agg_rates)


def messages_kernel(
    conc_ref, owner_hbm, source_hbm, weight_hbm, count_hbm, low_ref, high_ref, meta_ref,
    owner_ref, source_ref, weight_ref, count_ref, sems,
):
    rows = conc_ref.shape[0]
    half = low_ref.shape[1]
    entries = owner_ref.shape[0]
    small = [
        pltpu.make_async_copy(hbm, ref, sems.at[2 + i])
        for i, (hbm, ref) in enumerate(
            ((owner_hbm, owner_ref), (source_hbm, source_ref), (weight_hbm, weight_ref), (count_hbm, count_ref))
        )
    ]
    large = [
        pltpu.make_async_copy(conc_ref.at[:, pl.ds(i * half, half), :], ref.at[pl.ds(0, rows)], sems.at[i])
        for i, ref in enumerate((low_ref, high_ref))
    ]
    for copy in small + large:
        copy.start()
    meta_ref[...] = jnp.zeros(meta_ref.shape, meta_ref.dtype)
    for copy in small:
        copy.wait()
    wide = lambda value: value.astype(jnp.float32)
    entry = lax.broadcasted_iota(jnp.int32, owner_ref.shape, 0)
    live = jnp.where(entry < count_ref[...], weight_ref[...], 0.0)
    top = live.astype(jnp.bfloat16)
    middle = (live - wide(top)).astype(jnp.bfloat16)
    bottom = (live - wide(top) - wide(middle)).astype(jnp.bfloat16)
    fields = (wide(owner_ref[...]), wide(source_ref[...]), wide(top), wide(middle), wide(bottom))
    for field, (at, lane) in zip(fields, FIELDS):
        meta_ref[0, at : at + entries, lane : lane + rows] = field.astype(jnp.bfloat16)
    low_ref[rows] = meta_ref[0]
    high_ref[rows] = meta_ref[0]
    for copy in large:
        copy.wait()


def messages(conc, owner, source, weight, count):
    rows, bins, width = conc.shape
    half = bins // 2
    return pl.pallas_call(
        messages_kernel,
        in_specs=[in_place()] * 5,
        out_specs=[pl.BlockSpec(memory_space=pltpu.VMEM)] * 3,
        out_shape=[
            jax.ShapeDtypeStruct((rows + 1, half, width), conc.dtype),
            jax.ShapeDtypeStruct((rows + 1, half, width), conc.dtype),
            jax.ShapeDtypeStruct((1, half, width), conc.dtype),
        ],
        scratch_shapes=[pltpu.VMEM(small.shape, small.dtype) for small in (owner, source, weight, count)]
        + [pltpu.SemaphoreType.DMA((6,))],
        compiler_params=pltpu.CompilerParams(vmem_limit_bytes=MOST_BYTES),
        cost_estimate=pl.CostEstimate(flops=0, bytes_accessed=4 * conc.size, transcendentals=0),
        name="messages",
    )(conc, owner, source, weight, count)


def signs(flags):
    return [1.0 - 2.0 * ref[0].astype(jnp.float32) for ref in flags]


def lat_slots(rows, group, lat_step, lon_step, flags):
    core, chip, lat = signs(flags)
    far = jnp.where(core * chip < 0.0, 4.0, 5.0)
    slot = jnp.where(
        lon_step == 0.0,
        0.0,
        jnp.where(
            lon_step == 2.0 * chip, 2.0, jnp.where(lon_step == -2.0 * chip, 3.0, jnp.where(lon_step == core, 1.0, far))
        ),
    )
    return lat_step == (group - 1.0) * lat, slot * rows


def lon_slots(rows, group, lat_step, lon_step, flags):
    core, chip, lat = signs(flags)
    lon_from = 2.0 * (1.0 - group) * chip + lon_step
    slot = jnp.where(lon_from == 0.0, 1.0, 4.0) - lat_step * lat
    return (lon_from == 0.0) | (lon_from == core), slot * rows


def decode(slots, rows, entries, flags, meta_ref, index_ref, weight_ref):
    for g in range(3):
        owner, source, top, middle, bottom = [
            meta_ref[g, at : at + entries, lane : lane + 128].astype(jnp.float32) for at, lane in FIELDS
        ]
        weight = top + middle + bottom
        band = jnp.where(owner >= NEAR_LON, 1.0, 0.0) + jnp.where(owner >= 2 * NEAR_LON, 1.0, 0.0)
        here, base = slots(rows, float(g), band - 1.0, owner - NEAR_LON * band - REACH, flags)
        here = jnp.where(here & (weight != 0.0), 1.0, 0.0)
        index = base + source
        packed = [[jnp.zeros((1, 128), jnp.float32)] * 2 for _ in range(entries)]
        rank = jnp.zeros((1, 128), jnp.float32)
        for k in range(entries):
            taken = here[k : k + 1]
            for place in range(k + 1):
                spot = (taken > 0.0) & (rank == place)
                packed[place] = [
                    jnp.where(spot, index[k : k + 1], packed[place][0]),
                    jnp.where(spot, weight[k : k + 1], packed[place][1]),
                ]
            rank = rank + taken
        for place in range(entries):
            at = g * entries + place
            index_ref[at : at + 1, :] = packed[place][0].astype(jnp.int32)
            weight_ref[at : at + 1, :] = packed[place][1]
        at = 3 * entries + g
        index_ref[at : at + 1, :] = rank.astype(jnp.int32)


def read_metas(asked, meta_ref, sems, first):
    return [
        pltpu.make_async_copy(ref.at[pl.ds(ref.shape[0] - 1, 1)], meta_ref.at[pl.ds(g, 1)], sems.at[first + g])
        for g, ref in enumerate(asked)
    ]


def decode_kernel(slots, rows, entries, *refs):
    flags, asked, (index_ref, weight_ref, meta_ref, sems) = refs[:3], refs[3:6], refs[6:]
    copies = read_metas(asked, meta_ref, sems, 0)
    for copy in copies:
        copy.start()
    for copy in copies:
        copy.wait()
    decode(slots, rows, entries, flags, meta_ref, index_ref, weight_ref)


def decoded(flags, asked, slots, rows, half, entries):
    width = asked[1].shape[2]
    vectors = -(-3 * (entries + 1) // 8) * 8
    return pl.pallas_call(
        functools.partial(decode_kernel, slots, rows, entries),
        in_specs=[in_smem()] * 3 + [in_place()] * 3,
        out_specs=[pl.BlockSpec(memory_space=pltpu.VMEM)] * 2,
        out_shape=[
            jax.ShapeDtypeStruct((vectors, 128), jnp.int32),
            jax.ShapeDtypeStruct((vectors, 128), jnp.float32),
        ],
        scratch_shapes=[pltpu.VMEM((3, half, width), jnp.bfloat16), pltpu.SemaphoreType.DMA((3,))],
        compiler_params=pltpu.CompilerParams(vmem_limit_bytes=VMEM_BYTES),
        cost_estimate=pl.CostEstimate(flops=0, bytes_accessed=6 * half * width, transcendentals=0),
        name="decode",
    )(*flags, *asked)


def table_copies(bases, rows, sources, table, sems):
    half = table.shape[1]
    return [
        pltpu.make_async_copy(
            source.at[pl.ds(0, rows), pl.ds(base, half), :], table.at[pl.ds(i * rows, rows)], sems.at[i]
        )
        for i, (source, base) in enumerate(zip(sources, bases))
    ]


def add_terms(rows, entries, index_ref, weight_ref, table, outs):
    half, width = table.shape[1:]
    for group, out in enumerate(outs):

        def some(g, carry, group=group, out=out):
            def sums(terms):
                totals = []
                for u in range(UNROLL):
                    r = g * UNROLL + u
                    total = jnp.zeros((half, width), jnp.float32)
                    for k in range(terms):
                        row = group * entries + k
                        total = total + weight_ref[row, r] * table[index_ref[row, r]].astype(jnp.float32)
                    totals.append(total)
                for u in range(UNROLL):
                    out[g * UNROLL + u] = totals[u].astype(out.dtype)

            most = index_ref[3 * entries + group, g * UNROLL]
            for u in range(1, UNROLL):
                most = jnp.maximum(most, index_ref[3 * entries + group, g * UNROLL + u])
            sums(min(QUICK, entries))

            @pl.when(most > QUICK)
            def _():
                sums(entries)

            return carry

        lax.fori_loop(0, rows // UNROLL, some, 0)


def lat_sums_kernel(bases, entries, core_ref, chip_ref, index_ref, weight_ref, *refs):
    tables = len(bases)
    sources, outs = refs[:tables], refs[tables : tables + 3]
    table, sems = refs[tables + 3 :]
    rows = table.shape[0] // tables
    copies = table_copies(bases, rows, sources, table, sems)
    first = core_ref[0] != chip_ref[0]
    for copy in copies[:-2]:
        copy.start()
    pl.when(first)(copies[-2].start)
    pl.when(jnp.logical_not(first))(copies[-1].start)
    for copy in copies[:-2]:
        copy.wait()
    pl.when(first)(copies[-2].wait)
    pl.when(jnp.logical_not(first))(copies[-1].wait)
    add_terms(rows, entries, index_ref, weight_ref, table, outs)


def lon_sums_kernel(bases, slots, entries, *refs):
    tables = len(bases)
    flags, refs = refs[:3], refs[3:]
    asked, sources, outs = refs[:3], refs[3 : 3 + tables], refs[3 + tables : 6 + tables]
    table, meta_ref, index_vec, weight_vec, index_ref, weight_ref, sems = refs[6 + tables :]
    rows = table.shape[0] // tables
    metas = read_metas(asked, meta_ref, sems, tables)
    copies = table_copies(bases, rows, sources, table, sems)
    for copy in metas + copies:
        copy.start()
    for copy in metas:
        copy.wait()
    decode(slots, rows, entries, flags, meta_ref, index_vec, weight_vec)
    to_scalar = [
        pltpu.make_async_copy(index_vec, index_ref, sems.at[tables + 3]),
        pltpu.make_async_copy(weight_vec, weight_ref, sems.at[tables + 4]),
    ]
    for copy in to_scalar:
        copy.start()
    for copy in to_scalar + copies:
        copy.wait()
    add_terms(rows, entries, index_ref, weight_ref, table, outs)


def sums_call(kernel, operands, smem, sources, scratch, rows, half, entries, name):
    tables = len(sources)
    width = sources[0][0].shape[2]
    return pl.pallas_call(
        kernel,
        in_specs=[in_smem()] * smem + [in_place()] * (len(operands) - smem + tables),
        out_specs=[pl.BlockSpec(memory_space=pltpu.VMEM)] * 3,
        out_shape=[
            jax.ShapeDtypeStruct((rows, half, width), dtype) for dtype in (jnp.bfloat16, jnp.float32, jnp.bfloat16)
        ],
        scratch_shapes=[pltpu.VMEM((tables * rows, half, width), jnp.bfloat16)] + scratch,
        compiler_params=pltpu.CompilerParams(vmem_limit_bytes=TABLE_BYTES),
        cost_estimate=pl.CostEstimate(
            flops=6 * rows * entries * half * width,
            bytes_accessed=2 * (tables + 3) * rows * half * width,
            transcendentals=0,
        ),
        name=name,
    )(*operands, *[source for source, _ in sources])


def lat_sums(flags, terms, sources, rows, half, entries):
    kernel = functools.partial(lat_sums_kernel, tuple(base for _, base in sources), entries)
    scratch = [pltpu.SemaphoreType.DMA((len(sources),))]
    return sums_call(kernel, [*flags[:2], *terms], 4, sources, scratch, rows, half, entries, "lat_sums")


def lon_sums(flags, asked, slots, sources, rows, half, entries):
    kernel = functools.partial(lon_sums_kernel, tuple(base for _, base in sources), slots, entries)
    vectors = -(-3 * (entries + 1) // 8) * 8
    scratch = [pltpu.VMEM((3, half, asked[1].shape[2]), jnp.bfloat16)]
    scratch += [space((vectors, 128), dtype) for space in (pltpu.VMEM, pltpu.SMEM) for dtype in (jnp.int32, jnp.float32)]
    scratch += [pltpu.SemaphoreType.DMA((len(sources) + 5,))]
    return sums_call(kernel, [*flags, *asked], 3, sources, scratch, rows, half, entries, "lon_sums")


def edges_kernel(core_ref, *refs):
    rows, half = refs[0].shape[:2]
    per = 128 // 8
    lane = lax.broadcasted_iota(jnp.int32, (half, 128), 1)
    odd = core_ref[0] == 1
    for earlier_ref, out_ref in zip(refs[6:-2], refs[-2:]):
        out_ref[:, half:] = earlier_ref[...]
    for j in range(rows // per):
        ends = []
        for side in range(2):
            parts = refs[3 * side : 3 * side + 3]
            packed = jnp.zeros((half, 128), jnp.float32)
            for i in range(per):
                r = j * per + i
                cells = parts[0][r] + parts[1][r].astype(jnp.float32) + parts[2][r].astype(jnp.float32)
                at = 8 * i + 3 * (1 - side)
                spot = (lane >= at) & (lane < at + 3)
                packed = jnp.where(spot, pltpu.roll(cells, 8 * i + 3, 1), packed)
            ends.append(packed)
        for out_ref, value in zip(refs[-2:], (jnp.where(odd, *ends), jnp.where(odd, *ends[::-1]))):
            out_ref[j, :half] = value.astype(out_ref.dtype)


def edges(core, parts, earlier):
    rows, half, width = parts[0].shape
    specs = [
        pl.BlockSpec((rows, half, 128), lambda t, at=at: (0, 0, at)) for at in (0, width // 128 - 1) for _ in parts
    ]
    whole = lambda shape: pl.BlockSpec(shape, lambda t: (0,) * len(shape))
    packed = (rows // 16, half + sum(array.shape[1] for array in earlier[:1]), 128)
    return pl.pallas_call(
        edges_kernel,
        grid=(1,),
        in_specs=[in_smem()] + specs + [whole(array.shape) for array in earlier],
        out_specs=[whole(packed)] * 2,
        out_shape=[jax.ShapeDtypeStruct(packed, jnp.bfloat16)] * 2,
        compiler_params=pltpu.CompilerParams(vmem_limit_bytes=VMEM_BYTES),
        cost_estimate=pl.CostEstimate(flops=8 * half * 256 * rows, bytes_accessed=16 * half * 256 * rows, transcendentals=0),
        name="edges",
    )(core, *parts, *parts, *earlier)


def combine_kernel(own0, a0, b0, own1, a1, b1, out_ref):
    rows, half = own0.shape[:2]
    for r in range(rows):
        out_ref[r, :half] = own0[r] + a0[r].astype(jnp.float32) + b0[r].astype(jnp.float32)
        out_ref[r, half:] = own1[r] + a1[r].astype(jnp.float32) + b1[r].astype(jnp.float32)


def combine(parts0, parts1):
    rows, half, width = parts0[0].shape
    step = 8
    return pl.pallas_call(
        combine_kernel,
        grid=(rows // step,),
        in_specs=[pl.BlockSpec((step, half, width), lambda t: (t, 0, 0))] * 6,
        out_specs=pl.BlockSpec((step, 2 * half, width), lambda t: (t, 0, 0)),
        out_shape=jax.ShapeDtypeStruct((rows, 2 * half, width), jnp.float32),
        compiler_params=pltpu.CompilerParams(vmem_limit_bytes=VMEM_BYTES),
        cost_estimate=pl.CostEstimate(
            flops=4 * rows * half * width, bytes_accessed=24 * rows * half * width, transcendentals=0
        ),
        name="combine",
    )(*parts0, *parts1)


def shifted_by(row, edge, amount, lane):
    count = len(row)
    if amount == 0:
        return row
    if amount > 0:
        row = row[:-1] + [jnp.where(lane >= 128 - amount, edge, row[-1])]
        turned = [pltpu.roll(tile, amount, 1) for tile in row]
        return [jnp.where(lane < amount, turned[t - 1], turned[t]) for t in range(count)]
    row = [jnp.where(lane < -amount, edge, row[0])] + row[1:]
    turned = [pltpu.roll(tile, 128 + amount, 1) for tile in row]
    return [jnp.where(lane >= 128 + amount, turned[(t + 1) % count], turned[t]) for t in range(count)]


def edge_tile(west_ref, east_ref, r):
    per = 128 // 8
    both = west_ref[r // per].astype(jnp.float32) + east_ref[r // per].astype(jnp.float32)
    return pltpu.roll(both, (125 - 8 * (r % per)) % 128, 1)


def rows_kernel(lat_ref, offset_ref, first_row, last_row, one_ref, other_ref, *outs):
    bins, width = first_row.shape[1:]
    lane = lax.broadcasted_iota(jnp.int32, (bins, 128), 1)
    spots = [slice(128 * t, 128 * t + 128) for t in range(width // 128)]
    end = offset_ref.shape[0] - 1
    odd = lat_ref[0] == 1
    for out_ref, first in ((outs[0], odd), (outs[1], jnp.logical_not(odd))):
        offset = jnp.where(first, offset_ref[0], offset_ref[end])
        row = [jnp.where(first, first_row[0, :, at], last_row[0, :, at]) for at in spots]
        edge = jnp.where(first, edge_tile(one_ref, other_ref, 0), edge_tile(one_ref, other_ref, end))
        for amount in range(-REACH, REACH + 1):

            @pl.when(offset == amount)
            def _(out_ref=out_ref, row=row, edge=edge, amount=amount):
                for at, tile in zip(spots, shifted_by(row, edge, amount, lane)):
                    out_ref[0, :, at] = tile.astype(out_ref.dtype)


def outer_rows(lat, offset, remapped, one, other):
    rows, bins, width = remapped.shape
    row = lambda at: pl.BlockSpec((1, bins, width), lambda t: (at, 0, 0))
    whole = pl.BlockSpec(one.shape, lambda t: (0, 0, 0))
    return pl.pallas_call(
        rows_kernel,
        grid=(1,),
        in_specs=[in_smem()] * 2 + [row(0), row(rows - 1), whole, whole],
        out_specs=[row(0), row(0)],
        out_shape=[jax.ShapeDtypeStruct((1, bins, width), jnp.bfloat16)] * 2,
        compiler_params=pltpu.CompilerParams(vmem_limit_bytes=VMEM_BYTES),
        cost_estimate=pl.CostEstimate(flops=20 * bins * width, bytes_accessed=12 * bins * width, transcendentals=0),
        name="outer_rows",
    )(lat, offset, remapped, remapped, one, other)


def final_kernel(offset_ref, remap_ref, west_ref, east_ref, kappa_ref, local_ref, out_ref, outer_ref, edge_ref):
    rows, bins, width = remap_ref.shape
    count = width // 128
    lane = lax.broadcasted_iota(jnp.int32, (8, 128), 1)
    spots = [slice(128 * t, 128 * t + 128) for t in range(count)]
    for r in range(rows):
        edge_ref[r] = edge_tile(west_ref, east_ref, r)

    def moved(row, edge, amount):
        row = [jnp.where(lane < -amount, edge, row[0])] + row[1:]
        row = row[:-1] + [jnp.where(lane >= 128 - amount, edge, row[-1])]
        turned = [pltpu.roll(tile, (amount + 128) & 127, 1) for tile in row]
        before, after = lane < amount, lane >= 128 + amount
        return [
            jnp.where(before, turned[t - 1], jnp.where(after, turned[(t + 1) % count], turned[t])) for t in range(count)
        ]

    pieces = [slice(8 * b, 8 * b + 8) for b in range(bins // 8)]
    before, now, base = {}, {}, {}
    stores = []
    for r in range(rows):
        amount = offset_ref[r]
        kappa = [kappa_ref[r, :, spot] for spot in spots]
        above = [kappa_ref[max(r - 1, 0), :, spot] for spot in spots]
        for at in pieces:
            row = [remap_ref[r, at, spot] for spot in spots]
            edge = edge_ref[r, at]
            center = moved(row, edge, amount)
            east = moved(row, edge, amount - 1)
            west = moved(row, edge, amount + 1)
            key = at.start
            fresh = []
            for t, spot in enumerate(spots):
                around = kappa[t] * (east[t] + west[t] - 4.0 * center[t])
                fresh.append(local_ref[r, at, spot] + center[t] + around)
                if r == 1:
                    stores.append((r - 1, at, spot, base[key][t] + above[t] * center[t]))
                elif r:
                    stores.append((r - 1, at, spot, base[key][t] + above[t] * (before[key][t] + center[t])))
            if r:
                before[key] = now[key]
            now[key], base[key] = center, fresh
        if r % 2:
            for which, at, spot, value in stores:
                if which:
                    out_ref[which, at, spot] = value
                else:
                    outer_ref[0, at, spot] = value
            stores = []
    for at in pieces:
        for t, spot in enumerate(spots):
            outer_ref[1, at, spot] = base[at.start][t] + kappa_ref[rows - 1, :, spot] * before[at.start][t]


def final(offset, remapped, west, east, kappa, local):
    rows, bins, width = remapped.shape
    tile = bins // 2
    block = pl.BlockSpec((rows, tile, width), lambda t: (0, t, 0))
    packed = pl.BlockSpec((west.shape[0], tile, 128), lambda t: (0, t, 0))
    return pl.pallas_call(
        final_kernel,
        grid=(bins // tile,),
        in_specs=[in_smem(), block, packed, packed, pl.BlockSpec(kappa.shape, lambda t: (0, 0, 0)), block],
        out_specs=[block, pl.BlockSpec((2, tile, width), lambda t: (0, t, 0))],
        out_shape=[
            jax.ShapeDtypeStruct(local.shape, jnp.float32),
            jax.ShapeDtypeStruct((2, bins, width), jnp.float32),
        ],
        scratch_shapes=[pltpu.VMEM((rows, tile, 128), jnp.float32)],
        compiler_params=pltpu.CompilerParams(vmem_limit_bytes=VMEM_BYTES),
        cost_estimate=pl.CostEstimate(flops=30 * remapped.size, bytes_accessed=12 * remapped.size, transcendentals=0),
        name="final",
    )(offset, remapped, west, east, kappa, local)


def halo_kernel(lat_ref, one_ref, other_ref, kappa_ref, outer_ref, _, out_ref, sums_ref, sems):
    odd = lat_ref[0] == 1
    rows = out_ref.shape[0]
    copies = []
    for side, (first, at) in enumerate(((odd, 0), (jnp.logical_not(odd), rows - 1))):
        value = jnp.where(first, one_ref[0].astype(jnp.float32), other_ref[0].astype(jnp.float32))
        sums_ref[side] = outer_ref[side] + kappa_ref[at] * value
        copy = pltpu.make_async_copy(sums_ref.at[pl.ds(side, 1)], out_ref.at[pl.ds(at, 1)], sems.at[side])
        copy.start()
        copies.append(copy)
    for copy in copies:
        copy.wait()


def add_halo(lat, one, other, kappa, outer, partial):
    vmem = pl.BlockSpec(memory_space=pltpu.VMEM)
    return pl.pallas_call(
        halo_kernel,
        in_specs=[in_smem()] + [vmem] * 4 + [in_place()],
        out_specs=in_place(),
        out_shape=jax.ShapeDtypeStruct(partial.shape, jnp.float32),
        scratch_shapes=[pltpu.VMEM(outer.shape, jnp.float32), pltpu.SemaphoreType.DMA((2,))],
        input_output_aliases={5: 0},
        compiler_params=pltpu.CompilerParams(vmem_limit_bytes=VMEM_BYTES),
        cost_estimate=pl.CostEstimate(flops=4 * outer.size, bytes_accessed=20 * outer.size, transcendentals=0),
        name="add_halo",
    )(lat, one, other, kappa, outer, partial)


def body(
    conc,
    dep_owner,
    dep_row,
    dep_weight,
    dep_count,
    zonal_offset,
    agg_rates,
    toeplitz,
    settle,
    kappa,
):
    rows, bins, width = conc.shape
    entries = dep_owner.shape[2]
    my_lat, my_lon = lax.axis_index("lat"), lax.axis_index("lon")
    flags = [(value % 2).astype(jnp.int32).reshape(1) for value in (my_lon, my_lon // 2, my_lat)]
    half = bins // 2
    low, high, meta = messages(conc, dep_owner[0].T, dep_row[0].T, dep_weight[0].T, dep_count)
    lat1, lat2 = swap_lat(high, 0), swap_lat(high, 1)
    lon1, lon2 = swap_chip(low, 0), swap_chip(low, 1)
    beside = swap_core(conc)
    rates, meta = lax.optimization_barrier((agg_rates, meta))
    local = local_terms(conc, rates, toeplitz, settle)
    terms = decoded(flags, [lat1, meta, lat2], lat_slots, rows, half, entries)
    lat1, lat2, local, terms = lax.optimization_barrier((lat1, lat2, local, terms))

    to_lon1, own1, to_lon2 = lon_sums(
        flags,
        [lon1, meta, lon2],
        lon_slots,
        [(lat1, 0), (conc, half), (lat2, 0), (swap_core(lat1), 0), (beside, half), (swap_core(lat2), 0)],
        rows,
        half,
        entries,
    )
    parts1 = [swap_chip(to_lon1, 0), swap_chip(to_lon2, 1)]
    own1, later = lax.optimization_barrier((own1, flags))
    parts1 = [own1] + parts1

    to_lat1, own0, to_lat2 = lat_sums(
        later,
        terms,
        [(conc, 0), (beside, 0), (lon1, 0), (lon2, 0), (swap_core(lon1), 0), (swap_core(lon2), 0)],
        rows,
        half,
        entries,
    )
    parts0 = [own0, swap_lat(to_lat1, 0), swap_lat(to_lat2, 1)]

    kappa = kappa[:, None, :]

    earlier = edges(flags[0], parts1, [])
    parts0, earlier = lax.optimization_barrier((parts0, earlier))
    to_core, to_across = edges(flags[0], parts0, earlier)
    one, other = swap_core(to_core), swap_across(to_across)
    remapped = combine(parts0, parts1)
    row1, row2 = outer_rows(flags[2], zonal_offset, remapped, one, other)
    row1, row2 = swap_lat(row1, 0), swap_lat(row2, 1)
    partial, outer = final(zonal_offset, remapped, one, other, kappa, local)
    return add_halo(flags[2], row1, row2, kappa, outer, partial)


def solution(mesh):
    return jax.shard_map(
        body,
        mesh=mesh,
        in_specs=(
            P("lat", None, "lon"),
            P("lon", "lat", None),
            P("lon", "lat", None),
            P("lon", "lat", None),
            P("lon", "lat"),
            P("lat"),
            P(None, "lat", "lon"),
            P(),
            P(),
            P("lat", "lon"),
        ),
        out_specs=P("lat", None, "lon"),
        check_vma=False,
    )
```

profile of v0, /device:TPU:0, one launch (start us, length us, event | category | flops | bytes accessed | tf_op | source)
XLA Modules:
  0.0 81.1 jit_solution(1010693223064876014)
XLA Ops:
  0.0 2.3 %messages.1 = (bf16[33,32,256]{2,1,0:T(8,128)(2,1)}, bf16[33,32,256]{2,1,0:T(8,128)(2,1)}, bf16[1,32,256]{2,1,0:T(8,128)(2,1)}) custom-call(bf16[32,64,256]{2,1,0:T(8,128)(2,1)} %refs_0_.1, s32[4,32]{1,0:T(4,128)} %bitcast.13, s32[4,32]{1,0:T(4,128)} %bitcast.14, f32[4,32]{1,0:T(4,128)} %bitcast.15, s32[1,32]{1,0:T(1,128)} %count_hbm.1), custom_call_target="tpu_custom_call" | custom-call | bytes 2097152 | tf_op jit(solution)/shard_map/messages/pallas_call | solution.py:150
  2.3 3.0 %collective-permute-start.2 = (bf16[33,32,256]{2,1,0:T(8,128)(2,1)}, bf16[33,32,256]{2,1,0:T(8,128)(2,1)S(1)}, u32[]{:S(2)}, u32[]{:S(2)}) collective-permute-start(bf16[33,32,256]{2,1,0:T(8,128)(2,1)} %get-tuple-element.42), channel_id=1, source_target_pairs={{0,8},{16,24},{8,0},{24,16},{1,9},{17,25},{9,1},{25,17},{2,10},{18... | collective-permute-start | bytes 1622024 | tf_op jit(solution)/shard_map/ppermute | solution.py:21
  5.3 0.7 collective-permute-start.3
  6.0 1.6 %collective-permute-start = (bf16[33,32,256]{2,1,0:T(8,128)(2,1)}, bf16[33,32,256]{2,1,0:T(8,128)(2,1)S(1)}, u32[]{:S(2)}, u32[]{:S(2)}) collective-permute-start(bf16[33,32,256]{2,1,0:T(8,128)(2,1)} %get-tuple-element.39), channel_id=1, source_target_pairs={{0,2},{1,3},{4,6},{5,7},{2,0},{3,1},{6,4},{7,5},{8,10},{9,11},{12,... | collective-permute-start | bytes 1622024 | tf_op jit(solution)/shard_map/ppermute | solution.py:21
  7.6 2.5 %collective-permute-start.1 = (bf16[33,32,256]{2,1,0:T(8,128)(2,1)}, bf16[33,32,256]{2,1,0:T(8,128)(2,1)S(1)}, u32[]{:S(2)}, u32[]{:S(2)}) collective-permute-start(bf16[33,32,256]{2,1,0:T(8,128)(2,1)} %get-tuple-element.39), channel_id=1, source_target_pairs={{2,4},{3,5},{6,0},{7,1},{4,2},{5,3},{0,6},{1,7},{10,12},{11,13},{1... | collective-permute-start | bytes 1622024 | tf_op jit(solution)/shard_map/ppermute | solution.py:21
  10.1 0.8 rev.3
  10.9 0.7 copy.12.settle_ref
  11.7 1.2 %copy-done = bf16[32,64,256]{2,1,0:T(8,128)(2,1)S(1)} copy-done((bf16[32,64,256]{2,1,0:T(8,128)(2,1)S(1)}, bf16[32,64,256]{2,1,0:T(8,128)(2,1)}, u32[]{:S(2)}) %copy-start) | copy-done | bytes 1048600
  12.9 0.9 %copy-done.2 = f32[4,32,256]{2,1,0:T(8,128)S(1)} copy-done((f32[4,32,256]{2,1,0:T(8,128)S(1)}, f32[4,32,256]{2,1,0:T(8,128)}, u32[]{:S(2)}) %copy-start.2) | copy-done | bytes 131096
  13.8 1.8 %growth.1.local_ref = f32[32,64,256]{2,1,0:T(8,128)S(1)} custom-call(f32[4,128]{1,0:T(4,128)S(1)} %pad_convert_fusion.flip_ref, f32[64,1]{1,0:T(8,128)S(1)} %copy.12.settle_ref, bf16[32,64,256]{2,1,0:T(8,128)(2,1)S(1)} %copy-done, f32[4,32,256]{2,1,0:T(8,128)S(1)} %copy-done.2), custom_call_target="tpu_custom_call" | custom-call | flops 268435456 | bytes 4194304 | tf_op jit(solution)/shard_map/growth/pallas_call | solution.py:90
  15.6 3.0 %collective-permute-done.2.refs_3_.refs_6_ = bf16[33,32,256]{2,1,0:T(8,128)(2,1)S(1)} collective-permute-done((bf16[33,32,256]{2,1,0:T(8,128)(2,1)}, bf16[33,32,256]{2,1,0:T(8,128)(2,1)S(1)}, u32[]{:S(2)}, u32[]{:S(2)}) %collective-permute-start.2) | collective-permute-done | bytes 540704 | tf_op jit(solution)/shard_map/ppermute | solution.py:21
  19.4 1.3 %collective-permute-done.refs_3_.refs_2_ = bf16[33,32,256]{2,1,0:T(8,128)(2,1)S(1)} collective-permute-done((bf16[33,32,256]{2,1,0:T(8,128)(2,1)}, bf16[33,32,256]{2,1,0:T(8,128)(2,1)S(1)}, u32[]{:S(2)}, u32[]{:S(2)}) %collective-permute-start) | collective-permute-done | bytes 540704 | tf_op jit(solution)/shard_map/ppermute | solution.py:21
  20.7 13.0 %collective-permute-done.1.refs_5_.refs_3_ = bf16[33,32,256]{2,1,0:T(8,128)(2,1)S(1)} collective-permute-done((bf16[33,32,256]{2,1,0:T(8,128)(2,1)}, bf16[33,32,256]{2,1,0:T(8,128)(2,1)S(1)}, u32[]{:S(2)}, u32[]{:S(2)}) %collective-permute-start.1) | collective-permute-done | bytes 540704 | tf_op jit(solution)/shard_map/ppermute | solution.py:21
  33.8 2.3 %lon_sums.1 = (bf16[32,32,256]{2,1,0:T(8,128)(2,1)S(1)}, f32[32,32,256]{2,1,0:T(8,128)S(1)}, bf16[32,32,256]{2,1,0:T(8,128)(2,1)S(1)}) custom-call(s32[1]{0:T(128)} %bitcast.1.refs_0_.core_ref, s32[1]{0:T(128)} %bitcast.2.refs_1_.chip_ref, s32[1]{0:T(128)} %bitcast.refs_2_.lat_ref, bf16[33,32,256]{2,1,0:T(8,128)(2,1)S(1)} %collective-permute-done.refs_3_.refs_2_, ...), custom_call_target="tpu_custom_call" | custom-call | flops 6291456 | bytes 4718592 | tf_op jit(solution)/shard_map/lon_sums/pallas_call | solution.py:341
  36.7 2.6 %collective-permute-start.12 = (bf16[32,32,256]{2,1,0:T(8,128)(2,1)S(1)}, bf16[32,32,256]{2,1,0:T(8,128)(2,1)S(1)}, u32[]{:S(2)}, u32[]{:S(2)}) collective-permute-start(bf16[32,32,256]{2,1,0:T(8,128)(2,1)S(1)} %get-tuple-element.58), channel_id=1, source_target_pairs={{2,4},{3,5},{6,0},{7,1},{4,2},{5,3},{0,6},{1,7},{10,12},{11,13},{1... | collective-permute-start | bytes 1572872 | tf_op jit(solution)/shard_map/ppermute | solution.py:21
  39.4 2.1 %lat_sums.1 = (bf16[32,32,256]{2,1,0:T(8,128)(2,1)S(1)}, f32[32,32,256]{2,1,0:T(8,128)S(1)}, bf16[32,32,256]{2,1,0:T(8,128)(2,1)S(1)}) custom-call(s32[1]{0:T(128)} %bitcast.1.refs_0_.core_ref, s32[1]{0:T(128)} %bitcast.2.refs_1_.chip_ref, s32[16,128]{1,0:T(8,128)S(1)} %get-tuple-element.51.index_ref, f32[16,128]{1,0:T(8,128)S(1)} %get-tuple-element.52.weight_ref, ...), custom_call_target="tpu_custom_call" | custom-call | flops 6291456 | bytes 4718592 | tf_op jit(solution)/shard_map/lat_sums/pallas_call | solution.py:341
  41.5 4.0 %collective-permute-start.9 = (bf16[32,32,256]{2,1,0:T(8,128)(2,1)S(1)}, bf16[32,32,256]{2,1,0:T(8,128)(2,1)S(1)}, u32[]{:S(2)}, u32[]{:S(2)}) collective-permute-start(bf16[32,32,256]{2,1,0:T(8,128)(2,1)S(1)} %get-tuple-element.54), channel_id=1, source_target_pairs={{0,8},{16,24},{8,0},{24,16},{1,9},{17,25},{9,1},{25,17},{2,10},{18... | collective-permute-start | bytes 1572872 | tf_op jit(solution)/shard_map/ppermute | solution.py:21
  46.1 4.3 %collective-permute-done.11.refs_1_.refs_4_.a1 = bf16[32,32,256]{2,1,0:T(8,128)(2,1)S(1)} collective-permute-done((bf16[32,32,256]{2,1,0:T(8,128)(2,1)S(1)}, bf16[32,32,256]{2,1,0:T(8,128)(2,1)S(1)}, u32[]{:S(2)}, u32[]{:S(2)}) %collective-permute-start.11) | collective-permute-done | bytes 524320 | tf_op jit(solution)/shard_map/ppermute | solution.py:21
  50.5 12.4 %collective-permute-done.12.refs_2_.refs_5_.b1 = bf16[32,32,256]{2,1,0:T(8,128)(2,1)S(1)} collective-permute-done((bf16[32,32,256]{2,1,0:T(8,128)(2,1)S(1)}, bf16[32,32,256]{2,1,0:T(8,128)(2,1)S(1)}, u32[]{:S(2)}, u32[]{:S(2)}) %collective-permute-start.12) | collective-permute-done | bytes 524320 | tf_op jit(solution)/shard_map/ppermute | solution.py:21
  63.8 1.4 %collective-permute-start.14 = (bf16[2,64,128]{2,1,0:T(8,128)(2,1)S(1)}, bf16[2,64,128]{2,1,0:T(8,128)(2,1)S(1)}, u32[]{:S(2)}, u32[]{:S(2)}) collective-permute-start(bf16[2,64,128]{2,1,0:T(8,128)(2,1)S(1)} %get-tuple-element.67), channel_id=1, source_target_pairs={{1,2},{3,4},{5,6},{7,0},{2,1},{4,3},{6,5},{0,7},{9,10},{11,12},{13... | collective-permute-start | bytes 98312 | tf_op jit(solution)/shard_map/ppermute | solution.py:21
  65.6 3.4 %collective-permute-done.14.other_ref.east_ref = bf16[2,64,128]{2,1,0:T(8,128)(2,1)S(1)} collective-permute-done((bf16[2,64,128]{2,1,0:T(8,128)(2,1)S(1)}, bf16[2,64,128]{2,1,0:T(8,128)(2,1)S(1)}, u32[]{:S(2)}, u32[]{:S(2)}) %collective-permute-start.14) | collective-permute-done | bytes 32800 | tf_op jit(solution)/shard_map/ppermute | solution.py:21
  69.0 0.9 %outer_rows.1 = (bf16[1,64,256]{2,1,0:T(8,128)(2,1)S(1)}, bf16[1,64,256]{2,1,0:T(8,128)(2,1)S(1)}) custom-call(s32[1]{0:T(128)} %bitcast.refs_2_.lat_ref, s32[32]{0:T(128)S(1)} %copy-done.4, f32[32,64,256]{2,1,0:T(8,128)S(1)} %combine.1.first_row.last_row.remap_ref, f32[32,64,256]{2,1,0:T(8,128)S(1)} %combine.1.first_row.last_row.remap_ref, ...), custom_call_target="tpu_custom_call" | custom-call | flops 327680 | bytes 196608 | tf_op jit(solution)/shard_map/outer_rows/pallas_call | solution.py:481
  69.9 6.0 %collective-permute-start.15 = (bf16[1,64,256]{2,1,0:T(8,128)(2,1)S(1)}, bf16[1,64,256]{2,1,0:T(8,128)(2,1)S(1)}, u32[]{:S(2)}, u32[]{:S(2)}) collective-permute-start(bf16[1,64,256]{2,1,0:T(8,128)(2,1)S(1)} %get-tuple-element.68), channel_id=1, source_target_pairs={{0,8},{16,24},{8,0},{24,16},{1,9},{17,25},{9,1},{25,17},{2,10},{18... | collective-permute-start | bytes 98312 | tf_op jit(solution)/shard_map/ppermute | solution.py:21
  76.6 3.8 %final.1 = (f32[32,64,256]{2,1,0:T(8,128)}, f32[2,64,256]{2,1,0:T(8,128)S(1)}) custom-call(s32[32]{0:T(128)S(1)} %copy-done.4, f32[32,64,256]{2,1,0:T(8,128)S(1)} %combine.1.first_row.last_row.remap_ref, bf16[2,64,128]{2,1,0:T(8,128)(2,1)S(1)} %collective-permute-done.13.one_ref.west_ref, bf16[2,64,128]{2,1,0:T(8,128)(2,1)S(1)} %collective-permute-done.14.other_ref.east_ref, ...), custom_call_target="tpu_custom_call" | custom-call | flops 15728640 | bytes 6291456 | tf_op jit(solution)/shard_map/final/pallas_call | solution.py:552
  (37 shorter events, 4.7 us)
Async XLA Ops:
  2.3 16.3 %copy-start.3 = (bf16[1,32,256]{2,1,0:T(8,128)(2,1)S(1)}, bf16[1,32,256]{2,1,0:T(8,128)(2,1)}, u32[]{:S(2)}) copy-start(bf16[1,32,256]{2,1,0:T(8,128)(2,1)} %get-tuple-element.41.refs_4_) | copy-start | bytes 49156
  2.3 16.3 %collective-permute-start.2 = (bf16[33,32,256]{2,1,0:T(8,128)(2,1)}, bf16[33,32,256]{2,1,0:T(8,128)(2,1)S(1)}, u32[]{:S(2)}, u32[]{:S(2)}) collective-permute-start(bf16[33,32,256]{2,1,0:T(8,128)(2,1)} %get-tuple-element.42), channel_id=1, source_target_pairs={{0,8},{16,24},{8,0},{24,16},{1,9},{17,25},{9,1},{25,17},{2,10},{18... | collective-permute-start | bytes 1622024 | tf_op jit(solution)/shard_map/ppermute | solution.py:21
  5.3 13.3 %collective-permute-start.3 = (bf16[33,32,256]{2,1,0:T(8,128)(2,1)}, bf16[33,32,256]{2,1,0:T(8,128)(2,1)S(1)}, u32[]{:S(2)}, u32[]{:S(2)}) collective-permute-start(bf16[33,32,256]{2,1,0:T(8,128)(2,1)} %get-tuple-element.42), channel_id=1, source_target_pairs={{8,16},{16,8},{9,17},{17,9},{10,18},{18,10},{11,19},{19,11},{12,20... | collective-permute-start | bytes 1622024 | tf_op jit(solution)/shard_map/ppermute | solution.py:21
  6.0 14.7 %collective-permute-start = (bf16[33,32,256]{2,1,0:T(8,128)(2,1)}, bf16[33,32,256]{2,1,0:T(8,128)(2,1)S(1)}, u32[]{:S(2)}, u32[]{:S(2)}) collective-permute-start(bf16[33,32,256]{2,1,0:T(8,128)(2,1)} %get-tuple-element.39), channel_id=1, source_target_pairs={{0,2},{1,3},{4,6},{5,7},{2,0},{3,1},{6,4},{7,5},{8,10},{9,11},{12,... | collective-permute-start | bytes 1622024 | tf_op jit(solution)/shard_map/ppermute | solution.py:21
  7.6 26.1 %collective-permute-start.1 = (bf16[33,32,256]{2,1,0:T(8,128)(2,1)}, bf16[33,32,256]{2,1,0:T(8,128)(2,1)S(1)}, u32[]{:S(2)}, u32[]{:S(2)}) collective-permute-start(bf16[33,32,256]{2,1,0:T(8,128)(2,1)} %get-tuple-element.39), channel_id=1, source_target_pairs={{2,4},{3,5},{6,0},{7,1},{4,2},{5,3},{0,6},{1,7},{10,12},{11,13},{1... | collective-permute-start | bytes 1622024 | tf_op jit(solution)/shard_map/ppermute | solution.py:21
  10.1 23.6 %collective-permute-start.5 = (bf16[32,64,256]{2,1,0:T(8,128)(2,1)}, bf16[32,64,256]{2,1,0:T(8,128)(2,1)S(1)}, u32[]{:S(2)}, u32[]{:S(2)}) collective-permute-start(bf16[32,64,256]{2,1,0:T(8,128)(2,1)} %refs_0_.1), channel_id=1, source_target_pairs={{0,1},{2,3},{4,5},{6,7},{1,0},{3,2},{5,4},{7,6},{8,9},{10,11},{12,... | collective-permute-start | bytes 3145736 | tf_op jit(solution)/shard_map/ppermute | solution.py:21
  11.6 1.2 %copy-start = (bf16[32,64,256]{2,1,0:T(8,128)(2,1)S(1)}, bf16[32,64,256]{2,1,0:T(8,128)(2,1)}, u32[]{:S(2)}) copy-start(bf16[32,64,256]{2,1,0:T(8,128)(2,1)} %refs_0_.1) | copy-start | bytes 3145732
  12.9 0.9 %copy-start.2 = (f32[4,32,256]{2,1,0:T(8,128)S(1)}, f32[4,32,256]{2,1,0:T(8,128)}, u32[]{:S(2)}) copy-start(f32[4,32,256]{2,1,0:T(8,128)} %rates_ref) | copy-start | bytes 393220
  13.8 20.0 %copy-start.1 = (bf16[32,64,256]{2,1,0:T(8,128)(2,1)S(1)}, bf16[32,64,256]{2,1,0:T(8,128)(2,1)}, u32[]{:S(2)}) copy-start(bf16[32,64,256]{2,1,0:T(8,128)(2,1)} %refs_0_.1) | copy-start | bytes 3145732
  18.8 15.0 %collective-permute-start.4 = (bf16[33,32,256]{2,1,0:T(8,128)(2,1)S(1)}, bf16[33,32,256]{2,1,0:T(8,128)(2,1)S(1)}, u32[]{:S(2)}, u32[]{:S(2)}) collective-permute-start(bf16[33,32,256]{2,1,0:T(8,128)(2,1)S(1)} %collective-permute-done.2.refs_3_.refs_6_), channel_id=1, source_target_pairs={{0,1},{2,3},{4,5},{6,7},{1,0},{3,2},{5,4},{7,6},{8,9},{10,11},{12,... | collective-permute-start | bytes 1622024 | tf_op jit(solution)/shard_map/ppermute | solution.py:21
  18.9 14.9 %collective-permute-start.6 = (bf16[33,32,256]{2,1,0:T(8,128)(2,1)S(1)}, bf16[33,32,256]{2,1,0:T(8,128)(2,1)S(1)}, u32[]{:S(2)}, u32[]{:S(2)}) collective-permute-start(bf16[33,32,256]{2,1,0:T(8,128)(2,1)S(1)} %collective-permute-done.3.refs_5_.refs_8_), channel_id=1, source_target_pairs={{0,1},{2,3},{4,5},{6,7},{1,0},{3,2},{5,4},{7,6},{8,9},{10,11},{12,... | collective-permute-start | bytes 1622024 | tf_op jit(solution)/shard_map/ppermute | solution.py:21
  20.7 18.7 %collective-permute-start.7 = (bf16[33,32,256]{2,1,0:T(8,128)(2,1)S(1)}, bf16[33,32,256]{2,1,0:T(8,128)(2,1)S(1)}, u32[]{:S(2)}, u32[]{:S(2)}) collective-permute-start(bf16[33,32,256]{2,1,0:T(8,128)(2,1)S(1)} %collective-permute-done.refs_3_.refs_2_), channel_id=1, source_target_pairs={{0,1},{2,3},{4,5},{6,7},{1,0},{3,2},{5,4},{7,6},{8,9},{10,11},{12,... | collective-permute-start | bytes 1622024 | tf_op jit(solution)/shard_map/ppermute | solution.py:21
  33.7 5.6 %collective-permute-start.8 = (bf16[33,32,256]{2,1,0:T(8,128)(2,1)S(1)}, bf16[33,32,256]{2,1,0:T(8,128)(2,1)S(1)}, u32[]{:S(2)}, u32[]{:S(2)}) collective-permute-start(bf16[33,32,256]{2,1,0:T(8,128)(2,1)S(1)} %collective-permute-done.1.refs_5_.refs_3_), channel_id=1, source_target_pairs={{0,1},{2,3},{4,5},{6,7},{1,0},{3,2},{5,4},{7,6},{8,9},{10,11},{12,... | collective-permute-start | bytes 1622024 | tf_op jit(solution)/shard_map/ppermute | solution.py:21
  36.1 14.4 %collective-permute-start.11 = (bf16[32,32,256]{2,1,0:T(8,128)(2,1)S(1)}, bf16[32,32,256]{2,1,0:T(8,128)(2,1)S(1)}, u32[]{:S(2)}, u32[]{:S(2)}) collective-permute-start(bf16[32,32,256]{2,1,0:T(8,128)(2,1)S(1)} %get-tuple-element.57), channel_id=1, source_target_pairs={{0,2},{1,3},{4,6},{5,7},{2,0},{3,1},{6,4},{7,5},{8,10},{9,11},{12,... | collective-permute-start | bytes 1572872 | tf_op jit(solution)/shard_map/ppermute | solution.py:21
  36.7 26.1 %collective-permute-start.12 = (bf16[32,32,256]{2,1,0:T(8,128)(2,1)S(1)}, bf16[32,32,256]{2,1,0:T(8,128)(2,1)S(1)}, u32[]{:S(2)}, u32[]{:S(2)}) collective-permute-start(bf16[32,32,256]{2,1,0:T(8,128)(2,1)S(1)} %get-tuple-element.58), channel_id=1, source_target_pairs={{2,4},{3,5},{6,0},{7,1},{4,2},{5,3},{0,6},{1,7},{10,12},{11,13},{1... | collective-permute-start | bytes 1572872 | tf_op jit(solution)/shard_map/ppermute | solution.py:21
  41.5 21.8 %collective-permute-start.9 = (bf16[32,32,256]{2,1,0:T(8,128)(2,1)S(1)}, bf16[32,32,256]{2,1,0:T(8,128)(2,1)S(1)}, u32[]{:S(2)}, u32[]{:S(2)}) collective-permute-start(bf16[32,32,256]{2,1,0:T(8,128)(2,1)S(1)} %get-tuple-element.54), channel_id=1, source_target_pairs={{0,8},{16,24},{8,0},{24,16},{1,9},{17,25},{9,1},{25,17},{2,10},{18... | collective-permute-start | bytes 1572872 | tf_op jit(solution)/shard_map/ppermute | solution.py:21
  45.5 17.9 %collective-permute-start.10 = (bf16[32,32,256]{2,1,0:T(8,128)(2,1)S(1)}, bf16[32,32,256]{2,1,0:T(8,128)(2,1)S(1)}, u32[]{:S(2)}, u32[]{:S(2)}) collective-permute-start(bf16[32,32,256]{2,1,0:T(8,128)(2,1)S(1)} %get-tuple-element.55), channel_id=1, source_target_pairs={{8,16},{16,8},{9,17},{17,9},{10,18},{18,10},{11,19},{19,11},{12,20... | collective-permute-start | bytes 1572872 | tf_op jit(solution)/shard_map/ppermute | solution.py:21
  63.7 1.9 %collective-permute-start.13 = (bf16[2,64,128]{2,1,0:T(8,128)(2,1)S(1)}, bf16[2,64,128]{2,1,0:T(8,128)(2,1)S(1)}, u32[]{:S(2)}, u32[]{:S(2)}) collective-permute-start(bf16[2,64,128]{2,1,0:T(8,128)(2,1)S(1)} %get-tuple-element.66), channel_id=1, source_target_pairs={{0,1},{2,3},{4,5},{6,7},{1,0},{3,2},{5,4},{7,6},{8,9},{10,11},{12,... | collective-permute-start | bytes 98312 | tf_op jit(solution)/shard_map/ppermute | solution.py:21
  63.8 5.2 %copy-start.4 = (s32[32]{0:T(128)S(1)}, s32[32]{0:T(128)}, u32[]{:S(2)}) copy-start(s32[32]{0:T(128)} %offset_ref.3) | copy-start | bytes 388
  63.8 5.2 %collective-permute-start.14 = (bf16[2,64,128]{2,1,0:T(8,128)(2,1)S(1)}, bf16[2,64,128]{2,1,0:T(8,128)(2,1)S(1)}, u32[]{:S(2)}, u32[]{:S(2)}) collective-permute-start(bf16[2,64,128]{2,1,0:T(8,128)(2,1)S(1)} %get-tuple-element.67), channel_id=1, source_target_pairs={{1,2},{3,4},{5,6},{7,0},{2,1},{4,3},{6,5},{0,7},{9,10},{11,12},{13... | collective-permute-start | bytes 98312 | tf_op jit(solution)/shard_map/ppermute | solution.py:21
  65.6 11.0 %copy-start.5 = (f32[32,256]{1,0:T(8,128)S(1)}, f32[32,256]{1,0:T(8,128)}, u32[]{:S(2)}) copy-start(f32[32,256]{1,0:T(8,128)} %param.19) | copy-start | bytes 98308
  69.9 10.5 %collective-permute-start.15 = (bf16[1,64,256]{2,1,0:T(8,128)(2,1)S(1)}, bf16[1,64,256]{2,1,0:T(8,128)(2,1)S(1)}, u32[]{:S(2)}, u32[]{:S(2)}) collective-permute-start(bf16[1,64,256]{2,1,0:T(8,128)(2,1)S(1)} %get-tuple-element.68), channel_id=1, source_target_pairs={{0,8},{16,24},{8,0},{24,16},{1,9},{17,25},{9,1},{25,17},{2,10},{18... | collective-permute-start | bytes 98312 | tf_op jit(solution)/shard_map/ppermute | solution.py:21
  75.9 4.5 %collective-permute-start.16 = (bf16[1,64,256]{2,1,0:T(8,128)(2,1)S(1)}, bf16[1,64,256]{2,1,0:T(8,128)(2,1)S(1)}, u32[]{:S(2)}, u32[]{:S(2)}) collective-permute-start(bf16[1,64,256]{2,1,0:T(8,128)(2,1)S(1)} %get-tuple-element.69), channel_id=1, source_target_pairs={{8,16},{16,8},{9,17},{17,9},{10,18},{18,10},{11,19},{19,11},{12,20... | collective-permute-start | bytes 98312 | tf_op jit(solution)/shard_map/ppermute | solution.py:21
where the time goes:
time: 82.1 us; the launch traced here: 81.1 us
  waiting for transfers between devices  37.6 us (46%)
  starting transfers between devices  24.5 us (30%)
  Pallas kernels  15.1 us (18%)
  local copies, waits for them, and re-layouts  3.68 us (4%)
    ppermute x17, waiting for transfers between devices, exchange(): lax.ppermute(value, axis, [(i, j) for i, j in pairs] + [(j, i) for i, j i...  37.6 us
    ppermute x17, starting transfers between devices, exchange(): lax.ppermute(value, axis, [(i, j) for i, j in pairs] + [(j, i) for i, j i...  24.5 us
    pallas_call x2, Pallas kernels, sums_call(): pl.pallas_call(kernel, in_specs=[in_smem()] * smem + [in_place()] * (len(...  4.4 us
    pallas_call x1, Pallas kernels, final(): pl.pallas_call(final_kernel, grid=(bins // tile,), in_specs=[in_smem(), b...  3.77 us
    pallas_call x1, Pallas kernels, messages(): pl.pallas_call(messages_kernel, in_specs=[in_place()] * 5, out_specs=[pl....  2.29 us
    unnamed x12, local copies, waits for them, and re-layouts  2.14 us
    pallas_call x1, Pallas kernels, local_terms(): pl.pallas_call(growth_kernel, grid=(rows // step,), in_specs=[pl.BlockSpe...  1.81 us
  transfers between devices with their start and end apart: 17, of which 6 were waited for; matrix products, arithmetic and copies ran while one was open for 2% of the time, Pallas kernels for 13%

commit v1 on v0

--- a/solution.py
+++ b/solution.py
@@ -32,13 +32,13 @@
 
 def swap_chip(value, second):
     count = lax.axis_size("lon")
-    firsts = [i for i in range(count) if (i // 2) % 2 == second]
+    firsts = [i for i in range(count) if (i // 2) % 2 != second]
     return exchange(value, "lon", [(i, (i + 2) % count) for i in firsts])
 
 
 def swap_lat(value, second):
     count = lax.axis_size("lat")
-    return exchange(value, "lat", [(i, i + 1) for i in range(second, count - 1, 2)])
+    return exchange(value, "lat", [(i, i + 1) for i in range(1 - second, count - 1, 2)])
 
 
 def in_smem():
@@ -609,7 +609,7 @@
     rows, bins, width = conc.shape
     entries = dep_owner.shape[2]
     my_lat, my_lon = lax.axis_index("lat"), lax.axis_index("lon")
-    flags = [(value % 2).astype(jnp.int32).reshape(1) for value in (my_lon, my_lon // 2, my_lat)]
+    flags = [(value % 2).astype(jnp.int32).reshape(1) for value in (my_lon, my_lon // 2 + 1, my_lat + 1)]
     half = bins // 2
     low, high, meta = messages(conc, dep_owner[0].T, dep_row[0].T, dep_weight[0].T, dep_count)
     lat1, lat2 = swap_lat(high, 0), swap_lat(high, 1)

time: 82.1 us -> 83.9 us (1.022)
  waiting for transfers between devices: 37.6 us -> 42.2 us
  starting transfers between devices: 24.5 us -> 22.3 us
    ppermute x17, waiting for transfers between devices: 37.6 us -> 42.2 us  [exchange(): lax.ppermute(value, axis, [(i, j) for i, j in pairs] + [(j, i) for i, j i...]
    ppermute x17, starting transfers between devices: 24.5 us -> 22.3 us  [exchange(): lax.ppermute(value, axis, [(i, j) for i, j in pairs] + [(j, i) for i, j i...]
where the time goes in v1:
time: 83.9 us; the launch traced here: 83.7 us
  waiting for transfers between devices  42.2 us (50%)
  starting transfers between devices  22.3 us (27%)
  Pallas kernels  15.3 us (18%)
  local copies, waits for them, and re-layouts  3.68 us (4%)
    ppermute x17, waiting for transfers between devices, exchange(): lax.ppermute(value, axis, [(i, j) for i, j in pairs] + [(j, i) for i, j i...  42.2 us
    ppermute x17, starting transfers between devices, exchange(): lax.ppermute(value, axis, [(i, j) for i, j in pairs] + [(j, i) for i, j i...  22.3 us
    pallas_call x2, Pallas kernels, sums_call(): pl.pallas_call(kernel, in_specs=[in_smem()] * smem + [in_place()] * (len(...  4.65 us
    pallas_call x1, Pallas kernels, final(): pl.pallas_call(final_kernel, grid=(bins // tile,), in_specs=[in_smem(), b...  3.77 us
    pallas_call x1, Pallas kernels, messages(): pl.pallas_call(messages_kernel, in_specs=[in_place()] * 5, out_specs=[pl....  2.29 us
    unnamed x12, local copies, waits for them, and re-layouts  2.14 us
    pallas_call x1, Pallas kernels, local_terms(): pl.pallas_call(growth_kernel, grid=(rows // step,), in_specs=[pl.BlockSpe...  1.81 us
  transfers between devices with their start and end apart: 17, of which 6 were waited for; matrix products, arithmetic and copies ran while one was open for 2% of the time, Pallas kernels for 13%

profile of v1, /device:TPU:0, one launch (start us, length us, event | category | flops | bytes accessed | tf_op | source)
XLA Modules:
  0.0 83.7 jit_solution(2209803247736379513)
XLA Ops:
  0.0 2.3 %messages.1 = (bf16[33,32,256]{2,1,0:T(8,128)(2,1)}, bf16[33,32,256]{2,1,0:T(8,128)(2,1)}, bf16[1,32,256]{2,1,0:T(8,128)(2,1)}) custom-call(bf16[32,64,256]{2,1,0:T(8,128)(2,1)} %refs_0_.1, s32[4,32]{1,0:T(4,128)} %bitcast.13, s32[4,32]{1,0:T(4,128)} %bitcast.14, f32[4,32]{1,0:T(4,128)} %bitcast.15, s32[1,32]{1,0:T(1,128)} %count_hbm.1), custom_call_target="tpu_custom_call" | custom-call | bytes 2097152 | tf_op jit(solution)/shard_map/messages/pallas_call | solution.py:150
  2.3 0.7 collective-permute-start.2
  3.0 5.7 %collective-permute-start.3 = (bf16[33,32,256]{2,1,0:T(8,128)(2,1)}, bf16[33,32,256]{2,1,0:T(8,128)(2,1)S(1)}, u32[]{:S(2)}, u32[]{:S(2)}) collective-permute-start(bf16[33,32,256]{2,1,0:T(8,128)(2,1)} %get-tuple-element.42), channel_id=1, source_target_pairs={{0,8},{16,24},{8,0},{24,16},{1,9},{17,25},{9,1},{25,17},{2,10},{18... | collective-permute-start | bytes 1622024 | tf_op jit(solution)/shard_map/ppermute | solution.py:21
  8.7 3.6 %collective-permute-start = (bf16[33,32,256]{2,1,0:T(8,128)(2,1)}, bf16[33,32,256]{2,1,0:T(8,128)(2,1)S(1)}, u32[]{:S(2)}, u32[]{:S(2)}) collective-permute-start(bf16[33,32,256]{2,1,0:T(8,128)(2,1)} %get-tuple-element.39), channel_id=1, source_target_pairs={{2,4},{3,5},{6,0},{7,1},{4,2},{5,3},{0,6},{1,7},{10,12},{11,13},{1... | collective-permute-start | bytes 1622024 | tf_op jit(solution)/shard_map/ppermute | solution.py:21
  12.3 0.8 rev.3
  13.1 0.7 copy.12.settle_ref
  13.9 1.2 %copy-done = bf16[32,64,256]{2,1,0:T(8,128)(2,1)S(1)} copy-done((bf16[32,64,256]{2,1,0:T(8,128)(2,1)S(1)}, bf16[32,64,256]{2,1,0:T(8,128)(2,1)}, u32[]{:S(2)}) %copy-start) | copy-done | bytes 1048600
  15.1 0.9 %copy-done.2 = f32[4,32,256]{2,1,0:T(8,128)S(1)} copy-done((f32[4,32,256]{2,1,0:T(8,128)S(1)}, f32[4,32,256]{2,1,0:T(8,128)}, u32[]{:S(2)}) %copy-start.2) | copy-done | bytes 131096
  16.0 1.8 %growth.1.local_ref = f32[32,64,256]{2,1,0:T(8,128)S(1)} custom-call(f32[4,128]{1,0:T(4,128)S(1)} %pad_convert_fusion.flip_ref, f32[64,1]{1,0:T(8,128)S(1)} %copy.12.settle_ref, bf16[32,64,256]{2,1,0:T(8,128)(2,1)S(1)} %copy-done, f32[4,32,256]{2,1,0:T(8,128)S(1)} %copy-done.2), custom_call_target="tpu_custom_call" | custom-call | flops 268435456 | bytes 4194304 | tf_op jit(solution)/shard_map/growth/pallas_call | solution.py:90
  17.8 14.6 %collective-permute-done.3.refs_5_.refs_8_ = bf16[33,32,256]{2,1,0:T(8,128)(2,1)S(1)} collective-permute-done((bf16[33,32,256]{2,1,0:T(8,128)(2,1)}, bf16[33,32,256]{2,1,0:T(8,128)(2,1)S(1)}, u32[]{:S(2)}, u32[]{:S(2)}) %collective-permute-start.3) | collective-permute-done | bytes 540704 | tf_op jit(solution)/shard_map/ppermute | solution.py:21
  33.2 2.7 %collective-permute-done.1.refs_5_.refs_3_ = bf16[33,32,256]{2,1,0:T(8,128)(2,1)S(1)} collective-permute-done((bf16[33,32,256]{2,1,0:T(8,128)(2,1)}, bf16[33,32,256]{2,1,0:T(8,128)(2,1)S(1)}, u32[]{:S(2)}, u32[]{:S(2)}) %collective-permute-start.1) | collective-permute-done | bytes 540704 | tf_op jit(solution)/shard_map/ppermute | solution.py:21
  36.0 2.5 %lon_sums.1 = (bf16[32,32,256]{2,1,0:T(8,128)(2,1)S(1)}, f32[32,32,256]{2,1,0:T(8,128)S(1)}, bf16[32,32,256]{2,1,0:T(8,128)(2,1)S(1)}) custom-call(s32[1]{0:T(128)} %bitcast.1.refs_0_.core_ref, s32[1]{0:T(128)} %bitcast.2.refs_1_.chip_ref, s32[1]{0:T(128)} %bitcast.refs_2_.lat_ref, bf16[33,32,256]{2,1,0:T(8,128)(2,1)S(1)} %collective-permute-done.refs_3_.refs_2_, ...), custom_call_target="tpu_custom_call" | custom-call | flops 6291456 | bytes 4718592 | tf_op jit(solution)/shard_map/lon_sums/pallas_call | solution.py:341
  38.5 2.9 %collective-permute-start.11 = (bf16[32,32,256]{2,1,0:T(8,128)(2,1)S(1)}, bf16[32,32,256]{2,1,0:T(8,128)(2,1)S(1)}, u32[]{:S(2)}, u32[]{:S(2)}) collective-permute-start(bf16[32,32,256]{2,1,0:T(8,128)(2,1)S(1)} %get-tuple-element.57), channel_id=1, source_target_pairs={{2,4},{3,5},{6,0},{7,1},{4,2},{5,3},{0,6},{1,7},{10,12},{11,13},{1... | collective-permute-start | bytes 1572872 | tf_op jit(solution)/shard_map/ppermute | solution.py:21
  41.4 2.1 %lat_sums.1 = (bf16[32,32,256]{2,1,0:T(8,128)(2,1)S(1)}, f32[32,32,256]{2,1,0:T(8,128)S(1)}, bf16[32,32,256]{2,1,0:T(8,128)(2,1)S(1)}) custom-call(s32[1]{0:T(128)} %bitcast.1.refs_0_.core_ref, s32[1]{0:T(128)} %bitcast.2.refs_1_.chip_ref, s32[16,128]{1,0:T(8,128)S(1)} %get-tuple-element.51.index_ref, f32[16,128]{1,0:T(8,128)S(1)} %get-tuple-element.52.weight_ref, ...), custom_call_target="tpu_custom_call" | custom-call | flops 6291456 | bytes 4718592 | tf_op jit(solution)/shard_map/lat_sums/pallas_call | solution.py:341
  43.6 0.7 collective-permute-start.9
  44.3 2.3 %collective-permute-start.10 = (bf16[32,32,256]{2,1,0:T(8,128)(2,1)S(1)}, bf16[32,32,256]{2,1,0:T(8,128)(2,1)S(1)}, u32[]{:S(2)}, u32[]{:S(2)}) collective-permute-start(bf16[32,32,256]{2,1,0:T(8,128)(2,1)S(1)} %get-tuple-element.55), channel_id=1, source_target_pairs={{0,8},{16,24},{8,0},{24,16},{1,9},{17,25},{9,1},{25,17},{2,10},{18... | collective-permute-start | bytes 1572872 | tf_op jit(solution)/shard_map/ppermute | solution.py:21
  46.6 8.6 %collective-permute-done.11.refs_1_.refs_4_.a1 = bf16[32,32,256]{2,1,0:T(8,128)(2,1)S(1)} collective-permute-done((bf16[32,32,256]{2,1,0:T(8,128)(2,1)S(1)}, bf16[32,32,256]{2,1,0:T(8,128)(2,1)S(1)}, u32[]{:S(2)}, u32[]{:S(2)}) %collective-permute-start.11) | collective-permute-done | bytes 524320 | tf_op jit(solution)/shard_map/ppermute | solution.py:21
  55.2 10.8 %collective-permute-done.12.refs_2_.refs_5_.b1 = bf16[32,32,256]{2,1,0:T(8,128)(2,1)S(1)} collective-permute-done((bf16[32,32,256]{2,1,0:T(8,128)(2,1)S(1)}, bf16[32,32,256]{2,1,0:T(8,128)(2,1)S(1)}, u32[]{:S(2)}, u32[]{:S(2)}) %collective-permute-start.12) | collective-permute-done | bytes 524320 | tf_op jit(solution)/shard_map/ppermute | solution.py:21
  66.4 3.1 %collective-permute-done.10.b0.refs_2_.refs_5_ = bf16[32,32,256]{2,1,0:T(8,128)(2,1)S(1)} collective-permute-done((bf16[32,32,256]{2,1,0:T(8,128)(2,1)S(1)}, bf16[32,32,256]{2,1,0:T(8,128)(2,1)S(1)}, u32[]{:S(2)}, u32[]{:S(2)}) %collective-permute-start.10) | collective-permute-done | bytes 524320 | tf_op jit(solution)/shard_map/ppermute | solution.py:21
  70.0 2.6 %collective-permute-start.14 = (bf16[2,64,128]{2,1,0:T(8,128)(2,1)S(1)}, bf16[2,64,128]{2,1,0:T(8,128)(2,1)S(1)}, u32[]{:S(2)}, u32[]{:S(2)}) collective-permute-start(bf16[2,64,128]{2,1,0:T(8,128)(2,1)S(1)} %get-tuple-element.67), channel_id=1, source_target_pairs={{1,2},{3,4},{5,6},{7,0},{2,1},{4,3},{6,5},{0,7},{9,10},{11,12},{13... | collective-permute-start | bytes 98312 | tf_op jit(solution)/shard_map/ppermute | solution.py:21
  73.0 2.3 %collective-permute-done.14.other_ref.east_ref = bf16[2,64,128]{2,1,0:T(8,128)(2,1)S(1)} collective-permute-done((bf16[2,64,128]{2,1,0:T(8,128)(2,1)S(1)}, bf16[2,64,128]{2,1,0:T(8,128)(2,1)S(1)}, u32[]{:S(2)}, u32[]{:S(2)}) %collective-permute-start.14) | collective-permute-done | bytes 32800 | tf_op jit(solution)/shard_map/ppermute | solution.py:21
  75.3 0.8 outer_rows.1
  76.8 2.4 %collective-permute-start.16 = (bf16[1,64,256]{2,1,0:T(8,128)(2,1)S(1)}, bf16[1,64,256]{2,1,0:T(8,128)(2,1)S(1)}, u32[]{:S(2)}, u32[]{:S(2)}) collective-permute-start(bf16[1,64,256]{2,1,0:T(8,128)(2,1)S(1)} %get-tuple-element.69), channel_id=1, source_target_pairs={{0,8},{16,24},{8,0},{24,16},{1,9},{17,25},{9,1},{25,17},{2,10},{18... | collective-permute-start | bytes 98312 | tf_op jit(solution)/shard_map/ppermute | solution.py:21
  79.2 3.8 %final.1 = (f32[32,64,256]{2,1,0:T(8,128)}, f32[2,64,256]{2,1,0:T(8,128)S(1)}) custom-call(s32[32]{0:T(128)S(1)} %copy-done.4, f32[32,64,256]{2,1,0:T(8,128)S(1)} %combine.1.first_row.last_row.remap_ref, bf16[2,64,128]{2,1,0:T(8,128)(2,1)S(1)} %collective-permute-done.13.one_ref.west_ref, bf16[2,64,128]{2,1,0:T(8,128)(2,1)S(1)} %collective-permute-done.14.other_ref.east_ref, ...), custom_call_target="tpu_custom_call" | custom-call | flops 15728640 | bytes 6291456 | tf_op jit(solution)/shard_map/final/pallas_call | solution.py:552
  (37 shorter events, 3.5 us)
Async XLA Ops:
  2.3 30.1 %copy-start.3 = (bf16[1,32,256]{2,1,0:T(8,128)(2,1)S(1)}, bf16[1,32,256]{2,1,0:T(8,128)(2,1)}, u32[]{:S(2)}) copy-start(bf16[1,32,256]{2,1,0:T(8,128)(2,1)} %get-tuple-element.41.refs_4_) | copy-start | bytes 49156
  2.3 15.5 %collective-permute-start.2 = (bf16[33,32,256]{2,1,0:T(8,128)(2,1)}, bf16[33,32,256]{2,1,0:T(8,128)(2,1)S(1)}, u32[]{:S(2)}, u32[]{:S(2)}) collective-permute-start(bf16[33,32,256]{2,1,0:T(8,128)(2,1)} %get-tuple-element.42), channel_id=1, source_target_pairs={{8,16},{16,8},{9,17},{17,9},{10,18},{18,10},{11,19},{19,11},{12,20... | collective-permute-start | bytes 1622024 | tf_op jit(solution)/shard_map/ppermute | solution.py:21
  3.0 29.4 %collective-permute-start.3 = (bf16[33,32,256]{2,1,0:T(8,128)(2,1)}, bf16[33,32,256]{2,1,0:T(8,128)(2,1)S(1)}, u32[]{:S(2)}, u32[]{:S(2)}) collective-permute-start(bf16[33,32,256]{2,1,0:T(8,128)(2,1)} %get-tuple-element.42), channel_id=1, source_target_pairs={{0,8},{16,24},{8,0},{24,16},{1,9},{17,25},{9,1},{25,17},{2,10},{18... | collective-permute-start | bytes 1622024 | tf_op jit(solution)/shard_map/ppermute | solution.py:21
  8.7 24.4 %collective-permute-start = (bf16[33,32,256]{2,1,0:T(8,128)(2,1)}, bf16[33,32,256]{2,1,0:T(8,128)(2,1)S(1)}, u32[]{:S(2)}, u32[]{:S(2)}) collective-permute-start(bf16[33,32,256]{2,1,0:T(8,128)(2,1)} %get-tuple-element.39), channel_id=1, source_target_pairs={{2,4},{3,5},{6,0},{7,1},{4,2},{5,3},{0,6},{1,7},{10,12},{11,13},{1... | collective-permute-start | bytes 1622024 | tf_op jit(solution)/shard_map/ppermute | solution.py:21
  12.3 23.6 %collective-permute-start.1 = (bf16[33,32,256]{2,1,0:T(8,128)(2,1)}, bf16[33,32,256]{2,1,0:T(8,128)(2,1)S(1)}, u32[]{:S(2)}, u32[]{:S(2)}) collective-permute-start(bf16[33,32,256]{2,1,0:T(8,128)(2,1)} %get-tuple-element.39), channel_id=1, source_target_pairs={{0,2},{1,3},{4,6},{5,7},{2,0},{3,1},{6,4},{7,5},{8,10},{9,11},{12,... | collective-permute-start | bytes 1622024 | tf_op jit(solution)/shard_map/ppermute | solution.py:21
  12.3 23.6 %collective-permute-start.5 = (bf16[32,64,256]{2,1,0:T(8,128)(2,1)}, bf16[32,64,256]{2,1,0:T(8,128)(2,1)S(1)}, u32[]{:S(2)}, u32[]{:S(2)}) collective-permute-start(bf16[32,64,256]{2,1,0:T(8,128)(2,1)} %refs_0_.1), channel_id=1, source_target_pairs={{0,1},{2,3},{4,5},{6,7},{1,0},{3,2},{5,4},{7,6},{8,9},{10,11},{12,... | collective-permute-start | bytes 3145736 | tf_op jit(solution)/shard_map/ppermute | solution.py:21
  13.8 1.2 %copy-start = (bf16[32,64,256]{2,1,0:T(8,128)(2,1)S(1)}, bf16[32,64,256]{2,1,0:T(8,128)(2,1)}, u32[]{:S(2)}) copy-start(bf16[32,64,256]{2,1,0:T(8,128)(2,1)} %refs_0_.1) | copy-start | bytes 3145732
  15.1 0.9 %copy-start.2 = (f32[4,32,256]{2,1,0:T(8,128)S(1)}, f32[4,32,256]{2,1,0:T(8,128)}, u32[]{:S(2)}) copy-start(f32[4,32,256]{2,1,0:T(8,128)} %rates_ref) | copy-start | bytes 393220
  16.0 20.0 %copy-start.1 = (bf16[32,64,256]{2,1,0:T(8,128)(2,1)S(1)}, bf16[32,64,256]{2,1,0:T(8,128)(2,1)}, u32[]{:S(2)}) copy-start(bf16[32,64,256]{2,1,0:T(8,128)(2,1)} %refs_0_.1) | copy-start | bytes 3145732
  32.6 3.4 %collective-permute-start.4 = (bf16[33,32,256]{2,1,0:T(8,128)(2,1)S(1)}, bf16[33,32,256]{2,1,0:T(8,128)(2,1)S(1)}, u32[]{:S(2)}, u32[]{:S(2)}) collective-permute-start(bf16[33,32,256]{2,1,0:T(8,128)(2,1)S(1)} %collective-permute-done.2.refs_3_.refs_6_), channel_id=1, source_target_pairs={{0,1},{2,3},{4,5},{6,7},{1,0},{3,2},{5,4},{7,6},{8,9},{10,11},{12,... | collective-permute-start | bytes 1622024 | tf_op jit(solution)/shard_map/ppermute | solution.py:21
  32.6 3.3 %collective-permute-start.6 = (bf16[33,32,256]{2,1,0:T(8,128)(2,1)S(1)}, bf16[33,32,256]{2,1,0:T(8,128)(2,1)S(1)}, u32[]{:S(2)}, u32[]{:S(2)}) collective-permute-start(bf16[33,32,256]{2,1,0:T(8,128)(2,1)S(1)} %collective-permute-done.3.refs_5_.refs_8_), channel_id=1, source_target_pairs={{0,1},{2,3},{4,5},{6,7},{1,0},{3,2},{5,4},{7,6},{8,9},{10,11},{12,... | collective-permute-start | bytes 1622024 | tf_op jit(solution)/shard_map/ppermute | solution.py:21
  33.1 8.3 %collective-permute-start.7 = (bf16[33,32,256]{2,1,0:T(8,128)(2,1)S(1)}, bf16[33,32,256]{2,1,0:T(8,128)(2,1)S(1)}, u32[]{:S(2)}, u32[]{:S(2)}) collective-permute-start(bf16[33,32,256]{2,1,0:T(8,128)(2,1)S(1)} %collective-permute-done.refs_3_.refs_2_), channel_id=1, source_target_pairs={{0,1},{2,3},{4,5},{6,7},{1,0},{3,2},{5,4},{7,6},{8,9},{10,11},{12,... | collective-permute-start | bytes 1622024 | tf_op jit(solution)/shard_map/ppermute | solution.py:21
  35.9 5.5 %collective-permute-start.8 = (bf16[33,32,256]{2,1,0:T(8,128)(2,1)S(1)}, bf16[33,32,256]{2,1,0:T(8,128)(2,1)S(1)}, u32[]{:S(2)}, u32[]{:S(2)}) collective-permute-start(bf16[33,32,256]{2,1,0:T(8,128)(2,1)S(1)} %collective-permute-done.1.refs_5_.refs_3_), channel_id=1, source_target_pairs={{0,1},{2,3},{4,5},{6,7},{1,0},{3,2},{5,4},{7,6},{8,9},{10,11},{12,... | collective-permute-start | bytes 1622024 | tf_op jit(solution)/shard_map/ppermute | solution.py:21
  38.5 16.7 %collective-permute-start.11 = (bf16[32,32,256]{2,1,0:T(8,128)(2,1)S(1)}, bf16[32,32,256]{2,1,0:T(8,128)(2,1)S(1)}, u32[]{:S(2)}, u32[]{:S(2)}) collective-permute-start(bf16[32,32,256]{2,1,0:T(8,128)(2,1)S(1)} %get-tuple-element.57), channel_id=1, source_target_pairs={{2,4},{3,5},{6,0},{7,1},{4,2},{5,3},{0,6},{1,7},{10,12},{11,13},{1... | collective-permute-start | bytes 1572872 | tf_op jit(solution)/shard_map/ppermute | solution.py:21
  41.4 24.6 %collective-permute-start.12 = (bf16[32,32,256]{2,1,0:T(8,128)(2,1)S(1)}, bf16[32,32,256]{2,1,0:T(8,128)(2,1)S(1)}, u32[]{:S(2)}, u32[]{:S(2)}) collective-permute-start(bf16[32,32,256]{2,1,0:T(8,128)(2,1)S(1)} %get-tuple-element.58), channel_id=1, source_target_pairs={{0,2},{1,3},{4,6},{5,7},{2,0},{3,1},{6,4},{7,5},{8,10},{9,11},{12,... | collective-permute-start | bytes 1572872 | tf_op jit(solution)/shard_map/ppermute | solution.py:21
  43.6 22.9 %collective-permute-start.9 = (bf16[32,32,256]{2,1,0:T(8,128)(2,1)S(1)}, bf16[32,32,256]{2,1,0:T(8,128)(2,1)S(1)}, u32[]{:S(2)}, u32[]{:S(2)}) collective-permute-start(bf16[32,32,256]{2,1,0:T(8,128)(2,1)S(1)} %get-tuple-element.54), channel_id=1, source_target_pairs={{8,16},{16,8},{9,17},{17,9},{10,18},{18,10},{11,19},{19,11},{12,20... | collective-permute-start | bytes 1572872 | tf_op jit(solution)/shard_map/ppermute | solution.py:21
  44.3 25.2 %collective-permute-start.10 = (bf16[32,32,256]{2,1,0:T(8,128)(2,1)S(1)}, bf16[32,32,256]{2,1,0:T(8,128)(2,1)S(1)}, u32[]{:S(2)}, u32[]{:S(2)}) collective-permute-start(bf16[32,32,256]{2,1,0:T(8,128)(2,1)S(1)} %get-tuple-element.55), channel_id=1, source_target_pairs={{0,8},{16,24},{8,0},{24,16},{1,9},{17,25},{9,1},{25,17},{2,10},{18... | collective-permute-start | bytes 1572872 | tf_op jit(solution)/shard_map/ppermute | solution.py:21
  69.9 3.1 %collective-permute-start.13 = (bf16[2,64,128]{2,1,0:T(8,128)(2,1)S(1)}, bf16[2,64,128]{2,1,0:T(8,128)(2,1)S(1)}, u32[]{:S(2)}, u32[]{:S(2)}) collective-permute-start(bf16[2,64,128]{2,1,0:T(8,128)(2,1)S(1)} %get-tuple-element.66), channel_id=1, source_target_pairs={{0,1},{2,3},{4,5},{6,7},{1,0},{3,2},{5,4},{7,6},{8,9},{10,11},{12,... | collective-permute-start | bytes 98312 | tf_op jit(solution)/shard_map/ppermute | solution.py:21
  70.0 5.3 %copy-start.4 = (s32[32]{0:T(128)S(1)}, s32[32]{0:T(128)}, u32[]{:S(2)}) copy-start(s32[32]{0:T(128)} %offset_ref.3) | copy-start | bytes 388
  70.0 5.3 %collective-permute-start.14 = (bf16[2,64,128]{2,1,0:T(8,128)(2,1)S(1)}, bf16[2,64,128]{2,1,0:T(8,128)(2,1)S(1)}, u32[]{:S(2)}, u32[]{:S(2)}) collective-permute-start(bf16[2,64,128]{2,1,0:T(8,128)(2,1)S(1)} %get-tuple-element.67), channel_id=1, source_target_pairs={{1,2},{3,4},{5,6},{7,0},{2,1},{4,3},{6,5},{0,7},{9,10},{11,12},{13... | collective-permute-start | bytes 98312 | tf_op jit(solution)/shard_map/ppermute | solution.py:21
  72.9 6.2 %copy-start.5 = (f32[32,256]{1,0:T(8,128)S(1)}, f32[32,256]{1,0:T(8,128)}, u32[]{:S(2)}) copy-start(f32[32,256]{1,0:T(8,128)} %param.19) | copy-start | bytes 98308
  76.1 6.9 %collective-permute-start.15 = (bf16[1,64,256]{2,1,0:T(8,128)(2,1)S(1)}, bf16[1,64,256]{2,1,0:T(8,128)(2,1)S(1)}, u32[]{:S(2)}, u32[]{:S(2)}) collective-permute-start(bf16[1,64,256]{2,1,0:T(8,128)(2,1)S(1)} %get-tuple-element.68), channel_id=1, source_target_pairs={{8,16},{16,8},{9,17},{17,9},{10,18},{18,10},{11,19},{19,11},{12,20... | collective-permute-start | bytes 98312 | tf_op jit(solution)/shard_map/ppermute | solution.py:21
  76.8 6.2 %collective-permute-start.16 = (bf16[1,64,256]{2,1,0:T(8,128)(2,1)S(1)}, bf16[1,64,256]{2,1,0:T(8,128)(2,1)S(1)}, u32[]{:S(2)}, u32[]{:S(2)}) collective-permute-start(bf16[1,64,256]{2,1,0:T(8,128)(2,1)S(1)} %get-tuple-element.69), channel_id=1, source_target_pairs={{0,8},{16,24},{8,0},{24,16},{1,9},{17,25},{9,1},{25,17},{2,10},{18... | collective-permute-start | bytes 98312 | tf_op jit(solution)/shard_map/ppermute | solution.py:21

commit v2 on v0

--- a/solution.py
+++ b/solution.py
@@ -416,8 +416,9 @@
 def combine_kernel(own0, a0, b0, own1, a1, b1, out_ref):
     rows, half = own0.shape[:2]
     for r in range(rows):
-        out_ref[r, :half] = own0[r] + a0[r].astype(jnp.float32) + b0[r].astype(jnp.float32)
-        out_ref[r, half:] = own1[r] + a1[r].astype(jnp.float32) + b1[r].astype(jnp.float32)
+        for first, parts in ((0, (own0, a0, b0)), (half, (own1, a1, b1))):
+            total = parts[0][r] + parts[1][r].astype(jnp.float32) + parts[2][r].astype(jnp.float32)
+            out_ref[r, first : first + half] = total.astype(out_ref.dtype)
 
 
 def combine(parts0, parts1):
@@ -428,7 +429,7 @@
         grid=(rows // step,),
         in_specs=[pl.BlockSpec((step, half, width), lambda t: (t, 0, 0))] * 6,
         out_specs=pl.BlockSpec((step, 2 * half, width), lambda t: (t, 0, 0)),
-        out_shape=jax.ShapeDtypeStruct((rows, 2 * half, width), jnp.float32),
+        out_shape=jax.ShapeDtypeStruct((rows, 2 * half, width), jnp.bfloat16),
         compiler_params=pltpu.CompilerParams(vmem_limit_bytes=VMEM_BYTES),
         cost_estimate=pl.CostEstimate(
             flops=4 * rows * half * width, bytes_accessed=24 * rows * half * width, transcendentals=0
@@ -450,9 +451,9 @@
     return [jnp.where(lane >= 128 + amount, turned[(t + 1) % count], turned[t]) for t in range(count)]
 
 
-def edge_tile(west_ref, east_ref, r):
+def edge_tile(one_ref, other_ref, r):
     per = 128 // 8
-    both = west_ref[r // per].astype(jnp.float32) + east_ref[r // per].astype(jnp.float32)
+    both = one_ref[r // per] + other_ref[r // per]
     return pltpu.roll(both, (125 - 8 * (r % per)) % 128, 1)
 
 
@@ -490,13 +491,13 @@
     )(lat, offset, remapped, remapped, one, other)
 
 
-def final_kernel(offset_ref, remap_ref, west_ref, east_ref, kappa_ref, local_ref, out_ref, outer_ref, edge_ref):
+def final_kernel(offset_ref, remap_ref, one_ref, other_ref, kappa_ref, local_ref, out_ref, outer_ref, edge_ref):
     rows, bins, width = remap_ref.shape
     count = width // 128
-    lane = lax.broadcasted_iota(jnp.int32, (8, 128), 1)
+    lane = lax.broadcasted_iota(jnp.int32, (16, 128), 1)
     spots = [slice(128 * t, 128 * t + 128) for t in range(count)]
     for r in range(rows):
-        edge_ref[r] = edge_tile(west_ref, east_ref, r)
+        edge_ref[r] = edge_tile(one_ref, other_ref, r)
 
     def moved(row, edge, amount):
         row = [jnp.where(lane < -amount, edge, row[0])] + row[1:]
@@ -504,10 +505,11 @@
         turned = [pltpu.roll(tile, (amount + 128) & 127, 1) for tile in row]
         before, after = lane < amount, lane >= 128 + amount
         return [
-            jnp.where(before, turned[t - 1], jnp.where(after, turned[(t + 1) % count], turned[t])) for t in range(count)
+            jnp.where(before, turned[t - 1], jnp.where(after, turned[(t + 1) % count], turned[t])).astype(jnp.float32)
+            for t in range(count)
         ]
 
-    pieces = [slice(8 * b, 8 * b + 8) for b in range(bins // 8)]
+    pieces = [slice(16 * b, 16 * b + 16) for b in range(bins // 16)]
     before, now, base = {}, {}, {}
     stores = []
     for r in range(rows):
@@ -558,7 +560,7 @@
             jax.ShapeDtypeStruct(local.shape, jnp.float32),
             jax.ShapeDtypeStruct((2, bins, width), jnp.float32),
         ],
-        scratch_shapes=[pltpu.VMEM((rows, tile, 128), jnp.float32)],
+        scratch_shapes=[pltpu.VMEM((rows, tile, 128), jnp.bfloat16)],
         compiler_params=pltpu.CompilerParams(vmem_limit_bytes=VMEM_BYTES),
         cost_estimate=pl.CostEstimate(flops=30 * remapped.size, bytes_accessed=12 * remapped.size, transcendentals=0),
         name="final",
@@ -617,8 +619,8 @@
     beside = swap_core(conc)
     rates, meta = lax.optimization_barrier((agg_rates, meta))
     local = local_terms(conc, rates, toeplitz, settle)
+    lat1, lat2, local = lax.optimization_barrier((lat1, lat2, local))
     terms = decoded(flags, [lat1, meta, lat2], lat_slots, rows, half, entries)
-    lat1, lat2, local, terms = lax.optimization_barrier((lat1, lat2, local, terms))
 
     to_lon1, own1, to_lon2 = lon_sums(
         flags,

time: 82.1 us -> 85 us (1.035)
  Pallas kernels: 15.1 us -> 17.6 us
    pallas_call x2, Pallas kernels: 4.4 us -> 6.3 us  [sums_call(): pl.pallas_call(kernel, in_specs=[in_smem()] * smem + [in_place()] * (len(...]
  transfers between devices with their start and end apart: 17 -> 17, of which waited for: 6 -> 6; matrix products, arithmetic and copies ran while one was open for 2% -> 2% of each run, Pallas kernels for 13% -> 16%
where the time goes in v2:
time: 85 us; the launch traced here: 83.7 us
  waiting for transfers between devices  37.5 us (44%)
  starting transfers between devices  24.8 us (29%)
  Pallas kernels  17.6 us (21%)
  local copies, waits for them, and re-layouts  3.68 us (4%)
    ppermute x17, waiting for transfers between devices, exchange(): lax.ppermute(value, axis, [(i, j) for i, j in pairs] + [(j, i) for i, j i...  37.5 us
    ppermute x17, starting transfers between devices, exchange(): lax.ppermute(value, axis, [(i, j) for i, j in pairs] + [(j, i) for i, j i...  24.8 us
    pallas_call x2, Pallas kernels, sums_call(): pl.pallas_call(kernel, in_specs=[in_smem()] * smem + [in_place()] * (len(...  6.3 us
    pallas_call x1, Pallas kernels, final(): pl.pallas_call(final_kernel, grid=(bins // tile,), in_specs=[in_smem(), b...  3.6 us
    pallas_call x1, Pallas kernels, messages(): pl.pallas_call(messages_kernel, in_specs=[in_place()] * 5, out_specs=[pl....  2.29 us
    unnamed x12, local copies, waits for them, and re-layouts  2.14 us
    pallas_call x1, Pallas kernels, local_terms(): pl.pallas_call(growth_kernel, grid=(rows // step,), in_specs=[pl.BlockSpe...  1.81 us
  transfers between devices with their start and end apart: 17, of which 6 were waited for; matrix products, arithmetic and copies ran while one was open for 2% of the time, Pallas kernels for 16%

profile of v2, /device:TPU:0, one launch (start us, length us, event | category | flops | bytes accessed | tf_op | source)
XLA Modules:
  0.0 83.7 jit_solution(13930000696507801985)
XLA Ops:
  0.0 2.3 %messages.1 = (bf16[33,32,256]{2,1,0:T(8,128)(2,1)}, bf16[33,32,256]{2,1,0:T(8,128)(2,1)}, bf16[1,32,256]{2,1,0:T(8,128)(2,1)}) custom-call(bf16[32,64,256]{2,1,0:T(8,128)(2,1)} %refs_0_.1, s32[4,32]{1,0:T(4,128)} %bitcast.13, s32[4,32]{1,0:T(4,128)} %bitcast.14, f32[4,32]{1,0:T(4,128)} %bitcast.15, s32[1,32]{1,0:T(1,128)} %count_hbm.1), custom_call_target="tpu_custom_call" | custom-call | bytes 2097152 | tf_op jit(solution)/shard_map/messages/pallas_call | solution.py:150
  2.3 3.0 %collective-permute-start.2 = (bf16[33,32,256]{2,1,0:T(8,128)(2,1)}, bf16[33,32,256]{2,1,0:T(8,128)(2,1)}, u32[]{:S(2)}, u32[]{:S(2)}) collective-permute-start(bf16[33,32,256]{2,1,0:T(8,128)(2,1)} %get-tuple-element.40), channel_id=1, source_target_pairs={{0,8},{16,24},{8,0},{24,16},{1,9},{17,25},{9,1},{25,17},{2,10},{18... | collective-permute-start | bytes 1622024 | tf_op jit(solution)/shard_map/ppermute | solution.py:21
  5.3 1.5 %collective-permute-start.3 = (bf16[33,32,256]{2,1,0:T(8,128)(2,1)}, bf16[33,32,256]{2,1,0:T(8,128)(2,1)}, u32[]{:S(2)}, u32[]{:S(2)}) collective-permute-start(bf16[33,32,256]{2,1,0:T(8,128)(2,1)} %get-tuple-element.40), channel_id=1, source_target_pairs={{8,16},{16,8},{9,17},{17,9},{10,18},{18,10},{11,19},{19,11},{12,20... | collective-permute-start | bytes 1622024 | tf_op jit(solution)/shard_map/ppermute | solution.py:21
  6.8 1.6 %collective-permute-start = (bf16[33,32,256]{2,1,0:T(8,128)(2,1)}, bf16[33,32,256]{2,1,0:T(8,128)(2,1)}, u32[]{:S(2)}, u32[]{:S(2)}) collective-permute-start(bf16[33,32,256]{2,1,0:T(8,128)(2,1)} %get-tuple-element.37), channel_id=1, source_target_pairs={{0,2},{1,3},{4,6},{5,7},{2,0},{3,1},{6,4},{7,5},{8,10},{9,11},{12,... | collective-permute-start | bytes 1622024 | tf_op jit(solution)/shard_map/ppermute | solution.py:21
  8.3 2.5 %collective-permute-start.1 = (bf16[33,32,256]{2,1,0:T(8,128)(2,1)}, bf16[33,32,256]{2,1,0:T(8,128)(2,1)}, u32[]{:S(2)}, u32[]{:S(2)}) collective-permute-start(bf16[33,32,256]{2,1,0:T(8,128)(2,1)} %get-tuple-element.37), channel_id=1, source_target_pairs={{2,4},{3,5},{6,0},{7,1},{4,2},{5,3},{0,6},{1,7},{10,12},{11,13},{1... | collective-permute-start | bytes 1622024 | tf_op jit(solution)/shard_map/ppermute | solution.py:21
  10.8 0.8 rev.3
  12.4 1.2 %copy-done = bf16[32,64,256]{2,1,0:T(8,128)(2,1)S(1)} copy-done((bf16[32,64,256]{2,1,0:T(8,128)(2,1)S(1)}, bf16[32,64,256]{2,1,0:T(8,128)(2,1)}, u32[]{:S(2)}) %copy-start) | copy-done | bytes 1048600
  13.6 0.9 %copy-done.2 = f32[4,32,256]{2,1,0:T(8,128)S(1)} copy-done((f32[4,32,256]{2,1,0:T(8,128)S(1)}, f32[4,32,256]{2,1,0:T(8,128)}, u32[]{:S(2)}) %copy-start.2) | copy-done | bytes 131096
  14.5 1.8 %growth.1.local_ref = f32[32,64,256]{2,1,0:T(8,128)S(1)} custom-call(f32[4,128]{1,0:T(4,128)S(1)} %pad_convert_fusion.flip_ref, f32[64,1]{1,0:T(8,128)S(1)} %copy.12.settle_ref, bf16[32,64,256]{2,1,0:T(8,128)(2,1)S(1)} %copy-done, f32[4,32,256]{2,1,0:T(8,128)S(1)} %copy-done.2), custom_call_target="tpu_custom_call" | custom-call | flops 268435456 | bytes 4194304 | tf_op jit(solution)/shard_map/growth/pallas_call | solution.py:90
  16.3 2.4 %collective-permute-done.2.refs_6_.refs_3_ = bf16[33,32,256]{2,1,0:T(8,128)(2,1)} collective-permute-done((bf16[33,32,256]{2,1,0:T(8,128)(2,1)}, bf16[33,32,256]{2,1,0:T(8,128)(2,1)}, u32[]{:S(2)}, u32[]{:S(2)}) %collective-permute-start.2) | collective-permute-done | bytes 540704 | tf_op jit(solution)/shard_map/ppermute | solution.py:21
  19.2 2.1 %collective-permute-done.refs_3_.refs_2_ = bf16[33,32,256]{2,1,0:T(8,128)(2,1)} collective-permute-done((bf16[33,32,256]{2,1,0:T(8,128)(2,1)}, bf16[33,32,256]{2,1,0:T(8,128)(2,1)}, u32[]{:S(2)}, u32[]{:S(2)}) %collective-permute-start) | collective-permute-done | bytes 540704 | tf_op jit(solution)/shard_map/ppermute | solution.py:21
  21.4 13.2 %collective-permute-done.1.refs_5_.refs_3_ = bf16[33,32,256]{2,1,0:T(8,128)(2,1)} collective-permute-done((bf16[33,32,256]{2,1,0:T(8,128)(2,1)}, bf16[33,32,256]{2,1,0:T(8,128)(2,1)}, u32[]{:S(2)}, u32[]{:S(2)}) %collective-permute-start.1) | collective-permute-done | bytes 540704 | tf_op jit(solution)/shard_map/ppermute | solution.py:21
  34.5 0.8 decode.1
  35.4 2.9 %lon_sums.1 = (bf16[32,32,256]{2,1,0:T(8,128)(2,1)S(1)}, f32[32,32,256]{2,1,0:T(8,128)S(1)}, bf16[32,32,256]{2,1,0:T(8,128)(2,1)S(1)}) custom-call(s32[1]{0:T(128)} %bitcast.1.refs_0_.core_ref, s32[1]{0:T(128)} %bitcast.2.refs_1_.chip_ref, s32[1]{0:T(128)} %bitcast.refs_2_.lat_ref, bf16[33,32,256]{2,1,0:T(8,128)(2,1)} %collective-permute-done.refs_3_.refs_2_, ...), custom_call_target="tpu_custom_call" | custom-call | flops 6291456 | bytes 4718592 | tf_op jit(solution)/shard_map/lon_sums/pallas_call | solution.py:341
  38.9 2.6 %collective-permute-start.12 = (bf16[32,32,256]{2,1,0:T(8,128)(2,1)S(1)}, bf16[32,32,256]{2,1,0:T(8,128)(2,1)S(1)}, u32[]{:S(2)}, u32[]{:S(2)}) collective-permute-start(bf16[32,32,256]{2,1,0:T(8,128)(2,1)S(1)} %get-tuple-element.54), channel_id=1, source_target_pairs={{2,4},{3,5},{6,0},{7,1},{4,2},{5,3},{0,6},{1,7},{10,12},{11,13},{1... | collective-permute-start | bytes 1572872 | tf_op jit(solution)/shard_map/ppermute | solution.py:21
  41.6 3.4 %lat_sums.1 = (bf16[32,32,256]{2,1,0:T(8,128)(2,1)S(1)}, f32[32,32,256]{2,1,0:T(8,128)S(1)}, bf16[32,32,256]{2,1,0:T(8,128)(2,1)S(1)}) custom-call(s32[1]{0:T(128)} %bitcast.1.refs_0_.core_ref, s32[1]{0:T(128)} %bitcast.2.refs_1_.chip_ref, s32[16,128]{1,0:T(8,128)S(1)} %get-tuple-element.47.index_ref, f32[16,128]{1,0:T(8,128)S(1)} %get-tuple-element.48.weight_ref, ...), custom_call_target="tpu_custom_call" | custom-call | flops 6291456 | bytes 4718592 | tf_op jit(solution)/shard_map/lat_sums/pallas_call | solution.py:341
  45.0 3.4 %collective-permute-start.9 = (bf16[32,32,256]{2,1,0:T(8,128)(2,1)S(1)}, bf16[32,32,256]{2,1,0:T(8,128)(2,1)S(1)}, u32[]{:S(2)}, u32[]{:S(2)}) collective-permute-start(bf16[32,32,256]{2,1,0:T(8,128)(2,1)S(1)} %get-tuple-element.50), channel_id=1, source_target_pairs={{0,8},{16,24},{8,0},{24,16},{1,9},{17,25},{9,1},{25,17},{2,10},{18... | collective-permute-start | bytes 1572872 | tf_op jit(solution)/shard_map/ppermute | solution.py:21
  49.1 3.7 %collective-permute-done.11.refs_1_.refs_4_.a1 = bf16[32,32,256]{2,1,0:T(8,128)(2,1)S(1)} collective-permute-done((bf16[32,32,256]{2,1,0:T(8,128)(2,1)S(1)}, bf16[32,32,256]{2,1,0:T(8,128)(2,1)S(1)}, u32[]{:S(2)}, u32[]{:S(2)}) %collective-permute-start.11) | collective-permute-done | bytes 524320 | tf_op jit(solution)/shard_map/ppermute | solution.py:21
  52.8 12.5 %collective-permute-done.12.refs_2_.refs_5_.b1 = bf16[32,32,256]{2,1,0:T(8,128)(2,1)S(1)} collective-permute-done((bf16[32,32,256]{2,1,0:T(8,128)(2,1)S(1)}, bf16[32,32,256]{2,1,0:T(8,128)(2,1)S(1)}, u32[]{:S(2)}, u32[]{:S(2)}) %collective-permute-start.12) | collective-permute-done | bytes 524320 | tf_op jit(solution)/shard_map/ppermute | solution.py:21
  66.3 1.3 %collective-permute-start.14 = (bf16[2,64,128]{2,1,0:T(8,128)(2,1)S(1)}, bf16[2,64,128]{2,1,0:T(8,128)(2,1)S(1)}, u32[]{:S(2)}, u32[]{:S(2)}) collective-permute-start(bf16[2,64,128]{2,1,0:T(8,128)(2,1)S(1)} %get-tuple-element.63), channel_id=1, source_target_pairs={{1,2},{3,4},{5,6},{7,0},{2,1},{4,3},{6,5},{0,7},{9,10},{11,12},{13... | collective-permute-start | bytes 98312 | tf_op jit(solution)/shard_map/ppermute | solution.py:21
  68.0 3.5 %collective-permute-done.14.other_ref = bf16[2,64,128]{2,1,0:T(8,128)(2,1)S(1)} collective-permute-done((bf16[2,64,128]{2,1,0:T(8,128)(2,1)S(1)}, bf16[2,64,128]{2,1,0:T(8,128)(2,1)S(1)}, u32[]{:S(2)}, u32[]{:S(2)}) %collective-permute-start.14) | collective-permute-done | bytes 32800 | tf_op jit(solution)/shard_map/ppermute | solution.py:21
  71.5 0.8 %outer_rows.1 = (bf16[1,64,256]{2,1,0:T(8,128)(2,1)S(1)}, bf16[1,64,256]{2,1,0:T(8,128)(2,1)S(1)}) custom-call(s32[1]{0:T(128)} %bitcast.refs_2_.lat_ref, s32[32]{0:T(128)S(1)} %copy-done.4, bf16[32,64,256]{2,1,0:T(8,128)(2,1)S(1)} %combine.1.first_row.last_row.remap_ref, bf16[32,64,256]{2,1,0:T(8,128)(2,1)S(1)} %combine.1.first_row.last_row.remap_ref, ...), custom_call_target="tpu_custom_call" | custom-call | flops 327680 | bytes 196608 | tf_op jit(solution)/shard_map/outer_rows/pallas_call | solution.py:482
  72.3 6.4 %collective-permute-start.15 = (bf16[1,64,256]{2,1,0:T(8,128)(2,1)S(1)}, bf16[1,64,256]{2,1,0:T(8,128)(2,1)S(1)}, u32[]{:S(2)}, u32[]{:S(2)}) collective-permute-start(bf16[1,64,256]{2,1,0:T(8,128)(2,1)S(1)} %get-tuple-element.64), channel_id=1, source_target_pairs={{0,8},{16,24},{8,0},{24,16},{1,9},{17,25},{9,1},{25,17},{2,10},{18... | collective-permute-start | bytes 98312 | tf_op jit(solution)/shard_map/ppermute | solution.py:21
  79.4 3.6 %final.1 = (f32[32,64,256]{2,1,0:T(8,128)}, f32[2,64,256]{2,1,0:T(8,128)S(1)}) custom-call(s32[32]{0:T(128)S(1)} %copy-done.4, bf16[32,64,256]{2,1,0:T(8,128)(2,1)S(1)} %combine.1.first_row.last_row.remap_ref, bf16[2,64,128]{2,1,0:T(8,128)(2,1)S(1)} %collective-permute-done.13.one_ref, bf16[2,64,128]{2,1,0:T(8,128)(2,1)S(1)} %collective-permute-done.14.other_ref, ...), custom_call_target="tpu_custom_call" | custom-call | flops 15728640 | bytes 6291456 | tf_op jit(solution)/shard_map/final/pallas_call | solution.py:554
  (37 shorter events, 5.3 us)
Async XLA Ops:
  2.3 32.2 %copy-start.3 = (bf16[1,32,256]{2,1,0:T(8,128)(2,1)S(1)}, bf16[1,32,256]{2,1,0:T(8,128)(2,1)}, u32[]{:S(2)}) copy-start(bf16[1,32,256]{2,1,0:T(8,128)(2,1)} %get-tuple-element.39.refs_4_) | copy-start | bytes 49156
  2.3 16.4 %collective-permute-start.2 = (bf16[33,32,256]{2,1,0:T(8,128)(2,1)}, bf16[33,32,256]{2,1,0:T(8,128)(2,1)}, u32[]{:S(2)}, u32[]{:S(2)}) collective-permute-start(bf16[33,32,256]{2,1,0:T(8,128)(2,1)} %get-tuple-element.40), channel_id=1, source_target_pairs={{0,8},{16,24},{8,0},{24,16},{1,9},{17,25},{9,1},{25,17},{2,10},{18... | collective-permute-start | bytes 1622024 | tf_op jit(solution)/shard_map/ppermute | solution.py:21
  5.3 13.4 %collective-permute-start.3 = (bf16[33,32,256]{2,1,0:T(8,128)(2,1)}, bf16[33,32,256]{2,1,0:T(8,128)(2,1)}, u32[]{:S(2)}, u32[]{:S(2)}) collective-permute-start(bf16[33,32,256]{2,1,0:T(8,128)(2,1)} %get-tuple-element.40), channel_id=1, source_target_pairs={{8,16},{16,8},{9,17},{17,9},{10,18},{18,10},{11,19},{19,11},{12,20... | collective-permute-start | bytes 1622024 | tf_op jit(solution)/shard_map/ppermute | solution.py:21
  6.8 14.6 %collective-permute-start = (bf16[33,32,256]{2,1,0:T(8,128)(2,1)}, bf16[33,32,256]{2,1,0:T(8,128)(2,1)}, u32[]{:S(2)}, u32[]{:S(2)}) collective-permute-start(bf16[33,32,256]{2,1,0:T(8,128)(2,1)} %get-tuple-element.37), channel_id=1, source_target_pairs={{0,2},{1,3},{4,6},{5,7},{2,0},{3,1},{6,4},{7,5},{8,10},{9,11},{12,... | collective-permute-start | bytes 1622024 | tf_op jit(solution)/shard_map/ppermute | solution.py:21
  8.3 26.2 %collective-permute-start.1 = (bf16[33,32,256]{2,1,0:T(8,128)(2,1)}, bf16[33,32,256]{2,1,0:T(8,128)(2,1)}, u32[]{:S(2)}, u32[]{:S(2)}) collective-permute-start(bf16[33,32,256]{2,1,0:T(8,128)(2,1)} %get-tuple-element.37), channel_id=1, source_target_pairs={{2,4},{3,5},{6,0},{7,1},{4,2},{5,3},{0,6},{1,7},{10,12},{11,13},{1... | collective-permute-start | bytes 1622024 | tf_op jit(solution)/shard_map/ppermute | solution.py:21
  10.8 24.5 %collective-permute-start.5 = (bf16[32,64,256]{2,1,0:T(8,128)(2,1)}, bf16[32,64,256]{2,1,0:T(8,128)(2,1)}, u32[]{:S(2)}, u32[]{:S(2)}) collective-permute-start(bf16[32,64,256]{2,1,0:T(8,128)(2,1)} %refs_0_.1), channel_id=1, source_target_pairs={{0,1},{2,3},{4,5},{6,7},{1,0},{3,2},{5,4},{7,6},{8,9},{10,11},{12,... | collective-permute-start | bytes 3145736 | tf_op jit(solution)/shard_map/ppermute | solution.py:21
  12.3 1.2 %copy-start = (bf16[32,64,256]{2,1,0:T(8,128)(2,1)S(1)}, bf16[32,64,256]{2,1,0:T(8,128)(2,1)}, u32[]{:S(2)}) copy-start(bf16[32,64,256]{2,1,0:T(8,128)(2,1)} %refs_0_.1) | copy-start | bytes 3145732
  13.6 0.9 %copy-start.2 = (f32[4,32,256]{2,1,0:T(8,128)S(1)}, f32[4,32,256]{2,1,0:T(8,128)}, u32[]{:S(2)}) copy-start(f32[4,32,256]{2,1,0:T(8,128)} %rates_ref) | copy-start | bytes 393220
  14.5 20.9 %copy-start.1 = (bf16[32,64,256]{2,1,0:T(8,128)(2,1)S(1)}, bf16[32,64,256]{2,1,0:T(8,128)(2,1)}, u32[]{:S(2)}) copy-start(bf16[32,64,256]{2,1,0:T(8,128)(2,1)} %refs_0_.1) | copy-start | bytes 3145732
  18.7 16.6 %collective-permute-start.4 = (bf16[33,32,256]{2,1,0:T(8,128)(2,1)}, bf16[33,32,256]{2,1,0:T(8,128)(2,1)}, u32[]{:S(2)}, u32[]{:S(2)}) collective-permute-start(bf16[33,32,256]{2,1,0:T(8,128)(2,1)} %collective-permute-done.2.refs_6_.refs_3_), channel_id=1, source_target_pairs={{0,1},{2,3},{4,5},{6,7},{1,0},{3,2},{5,4},{7,6},{8,9},{10,11},{12,... | collective-permute-start | bytes 1622024 | tf_op jit(solution)/shard_map/ppermute | solution.py:21
  18.7 16.6 %collective-permute-start.6 = (bf16[33,32,256]{2,1,0:T(8,128)(2,1)}, bf16[33,32,256]{2,1,0:T(8,128)(2,1)}, u32[]{:S(2)}, u32[]{:S(2)}) collective-permute-start(bf16[33,32,256]{2,1,0:T(8,128)(2,1)} %collective-permute-done.3.refs_8_.refs_5_), channel_id=1, source_target_pairs={{0,1},{2,3},{4,5},{6,7},{1,0},{3,2},{5,4},{7,6},{8,9},{10,11},{12,... | collective-permute-start | bytes 1622024 | tf_op jit(solution)/shard_map/ppermute | solution.py:21
  21.4 20.2 %collective-permute-start.7 = (bf16[33,32,256]{2,1,0:T(8,128)(2,1)}, bf16[33,32,256]{2,1,0:T(8,128)(2,1)}, u32[]{:S(2)}, u32[]{:S(2)}) collective-permute-start(bf16[33,32,256]{2,1,0:T(8,128)(2,1)} %collective-permute-done.refs_3_.refs_2_), channel_id=1, source_target_pairs={{0,1},{2,3},{4,5},{6,7},{1,0},{3,2},{5,4},{7,6},{8,9},{10,11},{12,... | collective-permute-start | bytes 1622024 | tf_op jit(solution)/shard_map/ppermute | solution.py:21
  34.5 7.0 %collective-permute-start.8 = (bf16[33,32,256]{2,1,0:T(8,128)(2,1)}, bf16[33,32,256]{2,1,0:T(8,128)(2,1)}, u32[]{:S(2)}, u32[]{:S(2)}) collective-permute-start(bf16[33,32,256]{2,1,0:T(8,128)(2,1)} %collective-permute-done.1.refs_5_.refs_3_), channel_id=1, source_target_pairs={{0,1},{2,3},{4,5},{6,7},{1,0},{3,2},{5,4},{7,6},{8,9},{10,11},{12,... | collective-permute-start | bytes 1622024 | tf_op jit(solution)/shard_map/ppermute | solution.py:21
  38.3 14.5 %collective-permute-start.11 = (bf16[32,32,256]{2,1,0:T(8,128)(2,1)S(1)}, bf16[32,32,256]{2,1,0:T(8,128)(2,1)S(1)}, u32[]{:S(2)}, u32[]{:S(2)}) collective-permute-start(bf16[32,32,256]{2,1,0:T(8,128)(2,1)S(1)} %get-tuple-element.53), channel_id=1, source_target_pairs={{0,2},{1,3},{4,6},{5,7},{2,0},{3,1},{6,4},{7,5},{8,10},{9,11},{12,... | collective-permute-start | bytes 1572872 | tf_op jit(solution)/shard_map/ppermute | solution.py:21
  38.9 26.3 %collective-permute-start.12 = (bf16[32,32,256]{2,1,0:T(8,128)(2,1)S(1)}, bf16[32,32,256]{2,1,0:T(8,128)(2,1)S(1)}, u32[]{:S(2)}, u32[]{:S(2)}) collective-permute-start(bf16[32,32,256]{2,1,0:T(8,128)(2,1)S(1)} %get-tuple-element.54), channel_id=1, source_target_pairs={{2,4},{3,5},{6,0},{7,1},{4,2},{5,3},{0,6},{1,7},{10,12},{11,13},{1... | collective-permute-start | bytes 1572872 | tf_op jit(solution)/shard_map/ppermute | solution.py:21
  45.0 20.7 %collective-permute-start.9 = (bf16[32,32,256]{2,1,0:T(8,128)(2,1)S(1)}, bf16[32,32,256]{2,1,0:T(8,128)(2,1)S(1)}, u32[]{:S(2)}, u32[]{:S(2)}) collective-permute-start(bf16[32,32,256]{2,1,0:T(8,128)(2,1)S(1)} %get-tuple-element.50), channel_id=1, source_target_pairs={{0,8},{16,24},{8,0},{24,16},{1,9},{17,25},{9,1},{25,17},{2,10},{18... | collective-permute-start | bytes 1572872 | tf_op jit(solution)/shard_map/ppermute | solution.py:21
  48.4 17.3 %collective-permute-start.10 = (bf16[32,32,256]{2,1,0:T(8,128)(2,1)S(1)}, bf16[32,32,256]{2,1,0:T(8,128)(2,1)S(1)}, u32[]{:S(2)}, u32[]{:S(2)}) collective-permute-start(bf16[32,32,256]{2,1,0:T(8,128)(2,1)S(1)} %get-tuple-element.51), channel_id=1, source_target_pairs={{8,16},{16,8},{9,17},{17,9},{10,18},{18,10},{11,19},{19,11},{12,20... | collective-permute-start | bytes 1572872 | tf_op jit(solution)/shard_map/ppermute | solution.py:21
  66.2 1.8 %collective-permute-start.13 = (bf16[2,64,128]{2,1,0:T(8,128)(2,1)S(1)}, bf16[2,64,128]{2,1,0:T(8,128)(2,1)S(1)}, u32[]{:S(2)}, u32[]{:S(2)}) collective-permute-start(bf16[2,64,128]{2,1,0:T(8,128)(2,1)S(1)} %get-tuple-element.62), channel_id=1, source_target_pairs={{0,1},{2,3},{4,5},{6,7},{1,0},{3,2},{5,4},{7,6},{8,9},{10,11},{12,... | collective-permute-start | bytes 98312 | tf_op jit(solution)/shard_map/ppermute | solution.py:21
  66.2 5.2 %copy-start.4 = (s32[32]{0:T(128)S(1)}, s32[32]{0:T(128)}, u32[]{:S(2)}) copy-start(s32[32]{0:T(128)} %offset_ref.3) | copy-start | bytes 388
  66.3 5.2 %collective-permute-start.14 = (bf16[2,64,128]{2,1,0:T(8,128)(2,1)S(1)}, bf16[2,64,128]{2,1,0:T(8,128)(2,1)S(1)}, u32[]{:S(2)}, u32[]{:S(2)}) collective-permute-start(bf16[2,64,128]{2,1,0:T(8,128)(2,1)S(1)} %get-tuple-element.63), channel_id=1, source_target_pairs={{1,2},{3,4},{5,6},{7,0},{2,1},{4,3},{6,5},{0,7},{9,10},{11,12},{13... | collective-permute-start | bytes 98312 | tf_op jit(solution)/shard_map/ppermute | solution.py:21
  67.9 11.5 %copy-start.5 = (f32[32,256]{1,0:T(8,128)S(1)}, f32[32,256]{1,0:T(8,128)}, u32[]{:S(2)}) copy-start(f32[32,256]{1,0:T(8,128)} %param.19) | copy-start | bytes 98308
  72.3 10.7 %collective-permute-start.15 = (bf16[1,64,256]{2,1,0:T(8,128)(2,1)S(1)}, bf16[1,64,256]{2,1,0:T(8,128)(2,1)S(1)}, u32[]{:S(2)}, u32[]{:S(2)}) collective-permute-start(bf16[1,64,256]{2,1,0:T(8,128)(2,1)S(1)} %get-tuple-element.64), channel_id=1, source_target_pairs={{0,8},{16,24},{8,0},{24,16},{1,9},{17,25},{9,1},{25,17},{2,10},{18... | collective-permute-start | bytes 98312 | tf_op jit(solution)/shard_map/ppermute | solution.py:21
  78.7 4.3 %collective-permute-start.16 = (bf16[1,64,256]{2,1,0:T(8,128)(2,1)S(1)}, bf16[1,64,256]{2,1,0:T(8,128)(2,1)S(1)}, u32[]{:S(2)}, u32[]{:S(2)}) collective-permute-start(bf16[1,64,256]{2,1,0:T(8,128)(2,1)S(1)} %get-tuple-element.65), channel_id=1, source_target_pairs={{8,16},{16,8},{9,17},{17,9},{10,18},{18,10},{11,19},{19,11},{12,20... | collective-permute-start | bytes 98312 | tf_op jit(solution)/shard_map/ppermute | solution.py:21

commit v3 on v0

--- a/solution.py
+++ b/solution.py
@@ -463,25 +463,25 @@
     end = offset_ref.shape[0] - 1
     odd = lat_ref[0] == 1
     for out_ref, first in ((outs[0], odd), (outs[1], jnp.logical_not(odd))):
-        offset = jnp.where(first, offset_ref[0], offset_ref[end])
+        offset = jnp.broadcast_to(jnp.where(first, offset_ref[0], offset_ref[end]), (bins, 128))
         row = [jnp.where(first, first_row[0, :, at], last_row[0, :, at]) for at in spots]
         edge = jnp.where(first, edge_tile(one_ref, other_ref, 0), edge_tile(one_ref, other_ref, end))
-        for amount in range(-REACH, REACH + 1):
-
-            @pl.when(offset == amount)
-            def _(out_ref=out_ref, row=row, edge=edge, amount=amount):
-                for at, tile in zip(spots, shifted_by(row, edge, amount, lane)):
-                    out_ref[0, :, at] = tile.astype(out_ref.dtype)
+        result = row
+        for amount in (-2, -1, 1, 2):
+            moved = shifted_by(row, edge, amount, lane)
+            result = [jnp.where(offset == amount, tile, kept) for tile, kept in zip(moved, result)]
+        for at, tile in zip(spots, result):
+            out_ref[0, :, at] = tile.astype(out_ref.dtype)
 
 
 def outer_rows(lat, offset, remapped, one, other):
     rows, bins, width = remapped.shape
     row = lambda at: pl.BlockSpec((1, bins, width), lambda t: (at, 0, 0))
-    whole = pl.BlockSpec(one.shape, lambda t: (0, 0, 0))
+    whole = lambda array: pl.BlockSpec(array.shape, lambda t: (0, 0, 0))
     return pl.pallas_call(
         rows_kernel,
         grid=(1,),
-        in_specs=[in_smem()] * 2 + [row(0), row(rows - 1), whole, whole],
+        in_specs=[in_smem(), whole(offset), row(0), row(rows - 1), whole(one), whole(other)],
         out_specs=[row(0), row(0)],
         out_shape=[jax.ShapeDtypeStruct((1, bins, width), jnp.bfloat16)] * 2,
         compiler_params=pltpu.CompilerParams(vmem_limit_bytes=VMEM_BYTES),
@@ -490,13 +490,15 @@
     )(lat, offset, remapped, remapped, one, other)
 
 
-def final_kernel(offset_ref, remap_ref, west_ref, east_ref, kappa_ref, local_ref, out_ref, outer_ref, edge_ref):
+def final_kernel(
+    offset_ref, remap_ref, one_ref, other_ref, kappa_ref, local_ref, out_ref, outer_ref, edge_ref, sums_ref, sems
+):
     rows, bins, width = remap_ref.shape
     count = width // 128
     lane = lax.broadcasted_iota(jnp.int32, (8, 128), 1)
     spots = [slice(128 * t, 128 * t + 128) for t in range(count)]
     for r in range(rows):
-        edge_ref[r] = edge_tile(west_ref, east_ref, r)
+        edge_ref[r] = edge_tile(one_ref, other_ref, r)
 
     def moved(row, edge, amount):
         row = [jnp.where(lane < -amount, edge, row[0])] + row[1:]
@@ -507,62 +509,75 @@
             jnp.where(before, turned[t - 1], jnp.where(after, turned[(t + 1) % count], turned[t])) for t in range(count)
         ]
 
-    pieces = [slice(8 * b, 8 * b + 8) for b in range(bins // 8)]
-    before, now, base = {}, {}, {}
-    stores = []
-    for r in range(rows):
-        amount = offset_ref[r]
-        kappa = [kappa_ref[r, :, spot] for spot in spots]
-        above = [kappa_ref[max(r - 1, 0), :, spot] for spot in spots]
+    copies = []
+    for half in range(2):
+        first = half * bins // 2
+        pieces = [slice(b, b + 8) for b in range(first, first + bins // 2, 8)]
+        before, now, base = {}, {}, {}
+        stores = []
+        sent = 1
+        for r in range(rows):
+            amount = offset_ref[r]
+            kappa = [kappa_ref[r, :, spot] for spot in spots]
+            above = [kappa_ref[max(r - 1, 0), :, spot] for spot in spots]
+            for at in pieces:
+                row = [remap_ref[r, at, spot] for spot in spots]
+                edge = edge_ref[r, at]
+                center = moved(row, edge, amount)
+                east = moved(row, edge, amount - 1)
+                west = moved(row, edge, amount + 1)
+                key = at.start
+                fresh = []
+                for t, spot in enumerate(spots):
+                    around = kappa[t] * (east[t] + west[t] - 4.0 * center[t])
+                    fresh.append(local_ref[r, at, spot] + center[t] + around)
+                    if r == 1:
+                        stores.append((r - 1, at, spot, base[key][t] + above[t] * center[t]))
+                    elif r:
+                        stores.append((r - 1, at, spot, base[key][t] + above[t] * (before[key][t] + center[t])))
+                if r:
+                    before[key] = now[key]
+                now[key], base[key] = center, fresh
+            if r % 2:
+                for which, at, spot, value in stores:
+                    if which:
+                        sums_ref[which, at, spot] = value
+                    else:
+                        outer_ref[0, at, spot] = value
+                stores = []
+            if r % 8 == 7:
+                block = (pl.ds(sent, r - sent), pl.ds(first, bins // 2))
+                copy = pltpu.make_async_copy(sums_ref.at[block], out_ref.at[block], sems.at[len(copies)])
+                copy.start()
+                copies.append(copy)
+                sent = r
         for at in pieces:
-            row = [remap_ref[r, at, spot] for spot in spots]
-            edge = edge_ref[r, at]
-            center = moved(row, edge, amount)
-            east = moved(row, edge, amount - 1)
-            west = moved(row, edge, amount + 1)
-            key = at.start
-            fresh = []
             for t, spot in enumerate(spots):
-                around = kappa[t] * (east[t] + west[t] - 4.0 * center[t])
-                fresh.append(local_ref[r, at, spot] + center[t] + around)
-                if r == 1:
-                    stores.append((r - 1, at, spot, base[key][t] + above[t] * center[t]))
-                elif r:
-                    stores.append((r - 1, at, spot, base[key][t] + above[t] * (before[key][t] + center[t])))
-            if r:
-                before[key] = now[key]
-            now[key], base[key] = center, fresh
-        if r % 2:
-            for which, at, spot, value in stores:
-                if which:
-                    out_ref[which, at, spot] = value
-                else:
-                    outer_ref[0, at, spot] = value
-            stores = []
-    for at in pieces:
-        for t, spot in enumerate(spots):
-            outer_ref[1, at, spot] = base[at.start][t] + kappa_ref[rows - 1, :, spot] * before[at.start][t]
-
-
-def final(offset, remapped, west, east, kappa, local):
+                outer_ref[1, at, spot] = base[at.start][t] + kappa_ref[rows - 1, :, spot] * before[at.start][t]
+    for copy in copies:
+        copy.wait()
+
+
+def final(offset, remapped, one, other, kappa, local):
     rows, bins, width = remapped.shape
-    tile = bins // 2
-    block = pl.BlockSpec((rows, tile, width), lambda t: (0, t, 0))
-    packed = pl.BlockSpec((west.shape[0], tile, 128), lambda t: (0, t, 0))
+    vmem = pl.BlockSpec(memory_space=pltpu.VMEM)
     return pl.pallas_call(
         final_kernel,
-        grid=(bins // tile,),
-        in_specs=[in_smem(), block, packed, packed, pl.BlockSpec(kappa.shape, lambda t: (0, 0, 0)), block],
-        out_specs=[block, pl.BlockSpec((2, tile, width), lambda t: (0, t, 0))],
+        in_specs=[in_smem()] + [vmem] * 5,
+        out_specs=[in_place(), vmem],
         out_shape=[
             jax.ShapeDtypeStruct(local.shape, jnp.float32),
             jax.ShapeDtypeStruct((2, bins, width), jnp.float32),
         ],
-        scratch_shapes=[pltpu.VMEM((rows, tile, 128), jnp.float32)],
-        compiler_params=pltpu.CompilerParams(vmem_limit_bytes=VMEM_BYTES),
+        scratch_shapes=[
+            pltpu.VMEM((rows, bins, 128), jnp.float32),
+            pltpu.VMEM((rows, bins, width), jnp.float32),
+            pltpu.SemaphoreType.DMA((2 * (rows // 8),)),
+        ],
+        compiler_params=pltpu.CompilerParams(vmem_limit_bytes=TABLE_BYTES),
         cost_estimate=pl.CostEstimate(flops=30 * remapped.size, bytes_accessed=12 * remapped.size, transcendentals=0),
         name="final",
-    )(offset, remapped, west, east, kappa, local)
+    )(offset, remapped, one, other, kappa, local)
 
 
 def halo_kernel(lat_ref, one_ref, other_ref, kappa_ref, outer_ref, _, out_ref, sums_ref, sems):
@@ -618,7 +633,8 @@
     rates, meta = lax.optimization_barrier((agg_rates, meta))
     local = local_terms(conc, rates, toeplitz, settle)
     terms = decoded(flags, [lat1, meta, lat2], lat_slots, rows, half, entries)
-    lat1, lat2, local, terms = lax.optimization_barrier((lat1, lat2, local, terms))
+    spread = jnp.broadcast_to(zonal_offset[:, None, None], (rows, 1, 128))
+    lat1, lat2, local, terms, spread = lax.optimization_barrier((lat1, lat2, local, terms, spread))
 
     to_lon1, own1, to_lon2 = lon_sums(
         flags,
@@ -650,7 +666,7 @@
     to_core, to_across = edges(flags[0], parts0, earlier)
     one, other = swap_core(to_core), swap_across(to_across)
     remapped = combine(parts0, parts1)
-    row1, row2 = outer_rows(flags[2], zonal_offset, remapped, one, other)
+    row1, row2 = outer_rows(flags[2], spread, remapped, one, other)
     row1, row2 = swap_lat(row1, 0), swap_lat(row2, 1)
     partial, outer = final(zonal_offset, remapped, one, other, kappa, local)
     return add_halo(flags[2], row1, row2, kappa, outer, partial)

time: 82.1 us -> 81.1 us (0.988)
  Pallas kernels: 15.1 us -> 14.1 us
    pallas_call x2, Pallas kernels: 4.64 us -> 3.54 us  [the longest x1 3.34 us: final(): pl.pallas_call(final_kernel, in_specs=[in_smem()] + [vmem] * 5, out_specs...]
where the time goes in v3:
time: 81.1 us; the launch traced here: 80 us
  waiting for transfers between devices  37.4 us (46%)
  starting transfers between devices  24.4 us (30%)
  Pallas kernels  14.1 us (17%)
  local copies, waits for them, and re-layouts  3.76 us (5%)
    ppermute x17, waiting for transfers between devices, exchange(): lax.ppermute(value, axis, [(i, j) for i, j in pairs] + [(j, i) for i, j i...  37.4 us
    ppermute x17, starting transfers between devices, exchange(): lax.ppermute(value, axis, [(i, j) for i, j in pairs] + [(j, i) for i, j i...  24.4 us
    pallas_call x2, Pallas kernels, sums_call(): pl.pallas_call(kernel, in_specs=[in_smem()] * smem + [in_place()] * (len(...  4.4 us
    pallas_call x1, Pallas kernels, final(): pl.pallas_call(final_kernel, in_specs=[in_smem()] + [vmem] * 5, out_specs...  3.34 us
    pallas_call x1, Pallas kernels, messages(): pl.pallas_call(messages_kernel, in_specs=[in_place()] * 5, out_specs=[pl....  2.29 us
    unnamed x12, local copies, waits for them, and re-layouts  2.14 us
    pallas_call x1, Pallas kernels, local_terms(): pl.pallas_call(growth_kernel, grid=(rows // step,), in_specs=[pl.BlockSpe...  1.81 us
  transfers between devices with their start and end apart: 17, of which 6 were waited for; matrix products, arithmetic and copies ran while one was open for 2% of the time, Pallas kernels for 13%

profile of v3, /device:TPU:0, one launch (start us, length us, event | category | flops | bytes accessed | tf_op | source)
XLA Modules:
  0.0 80.0 jit_solution(13345771011197526175)
XLA Ops:
  0.0 2.3 %messages.1 = (bf16[33,32,256]{2,1,0:T(8,128)(2,1)}, bf16[33,32,256]{2,1,0:T(8,128)(2,1)}, bf16[1,32,256]{2,1,0:T(8,128)(2,1)}) custom-call(bf16[32,64,256]{2,1,0:T(8,128)(2,1)} %refs_0_.1, s32[4,32]{1,0:T(4,128)} %bitcast.13, s32[4,32]{1,0:T(4,128)} %bitcast.14, f32[4,32]{1,0:T(4,128)} %bitcast.15, s32[1,32]{1,0:T(1,128)} %count_hbm.1), custom_call_target="tpu_custom_call" | custom-call | bytes 2097152 | tf_op jit(solution)/shard_map/messages/pallas_call | solution.py:150
  2.3 3.0 %collective-permute-start = (bf16[33,32,256]{2,1,0:T(8,128)(2,1)}, bf16[33,32,256]{2,1,0:T(8,128)(2,1)S(1)}, u32[]{:S(2)}, u32[]{:S(2)}) collective-permute-start(bf16[33,32,256]{2,1,0:T(8,128)(2,1)} %get-tuple-element.40), channel_id=1, source_target_pairs={{0,8},{16,24},{8,0},{24,16},{1,9},{17,25},{9,1},{25,17},{2,10},{18... | collective-permute-start | bytes 1622024 | tf_op jit(solution)/shard_map/ppermute | solution.py:21
  6.0 1.6 %collective-permute-start.2 = (bf16[33,32,256]{2,1,0:T(8,128)(2,1)}, bf16[33,32,256]{2,1,0:T(8,128)(2,1)S(1)}, u32[]{:S(2)}, u32[]{:S(2)}) collective-permute-start(bf16[33,32,256]{2,1,0:T(8,128)(2,1)} %get-tuple-element.47), channel_id=1, source_target_pairs={{0,2},{1,3},{4,6},{5,7},{2,0},{3,1},{6,4},{7,5},{8,10},{9,11},{12,... | collective-permute-start | bytes 1622024 | tf_op jit(solution)/shard_map/ppermute | solution.py:21
  7.6 2.5 %collective-permute-start.3 = (bf16[33,32,256]{2,1,0:T(8,128)(2,1)}, bf16[33,32,256]{2,1,0:T(8,128)(2,1)S(1)}, u32[]{:S(2)}, u32[]{:S(2)}) collective-permute-start(bf16[33,32,256]{2,1,0:T(8,128)(2,1)} %get-tuple-element.47), channel_id=1, source_target_pairs={{2,4},{3,5},{6,0},{7,1},{4,2},{5,3},{0,6},{1,7},{10,12},{11,13},{1... | collective-permute-start | bytes 1622024 | tf_op jit(solution)/shard_map/ppermute | solution.py:21
  10.1 0.8 rev.3
  10.9 0.7 copy.12.settle_ref
  11.7 1.2 %copy-done = bf16[32,64,256]{2,1,0:T(8,128)(2,1)S(1)} copy-done((bf16[32,64,256]{2,1,0:T(8,128)(2,1)S(1)}, bf16[32,64,256]{2,1,0:T(8,128)(2,1)}, u32[]{:S(2)}) %copy-start) | copy-done | bytes 1048600
  12.9 0.9 %copy-done.2 = f32[4,32,256]{2,1,0:T(8,128)S(1)} copy-done((f32[4,32,256]{2,1,0:T(8,128)S(1)}, f32[4,32,256]{2,1,0:T(8,128)}, u32[]{:S(2)}) %copy-start.2) | copy-done | bytes 131096
  13.8 1.8 %growth.1.local_ref = f32[32,64,256]{2,1,0:T(8,128)S(1)} custom-call(f32[4,128]{1,0:T(4,128)S(1)} %pad_convert_fusion.flip_ref, f32[64,1]{1,0:T(8,128)S(1)} %copy.12.settle_ref, bf16[32,64,256]{2,1,0:T(8,128)(2,1)S(1)} %copy-done, f32[4,32,256]{2,1,0:T(8,128)S(1)} %copy-done.2), custom_call_target="tpu_custom_call" | custom-call | flops 268435456 | bytes 4194304 | tf_op jit(solution)/shard_map/growth/pallas_call | solution.py:90
  15.6 3.0 %collective-permute-done.refs_3_.refs_6_ = bf16[33,32,256]{2,1,0:T(8,128)(2,1)S(1)} collective-permute-done((bf16[33,32,256]{2,1,0:T(8,128)(2,1)}, bf16[33,32,256]{2,1,0:T(8,128)(2,1)S(1)}, u32[]{:S(2)}, u32[]{:S(2)}) %collective-permute-start) | collective-permute-done | bytes 540704 | tf_op jit(solution)/shard_map/ppermute | solution.py:21
  19.5 1.2 %collective-permute-done.2.refs_3_.refs_2_ = bf16[33,32,256]{2,1,0:T(8,128)(2,1)S(1)} collective-permute-done((bf16[33,32,256]{2,1,0:T(8,128)(2,1)}, bf16[33,32,256]{2,1,0:T(8,128)(2,1)S(1)}, u32[]{:S(2)}, u32[]{:S(2)}) %collective-permute-start.2) | collective-permute-done | bytes 540704 | tf_op jit(solution)/shard_map/ppermute | solution.py:21
  20.7 13.0 %collective-permute-done.3.refs_5_.refs_3_ = bf16[33,32,256]{2,1,0:T(8,128)(2,1)S(1)} collective-permute-done((bf16[33,32,256]{2,1,0:T(8,128)(2,1)}, bf16[33,32,256]{2,1,0:T(8,128)(2,1)S(1)}, u32[]{:S(2)}, u32[]{:S(2)}) %collective-permute-start.3) | collective-permute-done | bytes 540704 | tf_op jit(solution)/shard_map/ppermute | solution.py:21
  33.8 2.3 %lon_sums.1 = (bf16[32,32,256]{2,1,0:T(8,128)(2,1)S(1)}, f32[32,32,256]{2,1,0:T(8,128)S(1)}, bf16[32,32,256]{2,1,0:T(8,128)(2,1)S(1)}) custom-call(s32[1]{0:T(128)} %bitcast.8.refs_0_.core_ref, s32[1]{0:T(128)} %bitcast.9.refs_1_.chip_ref, s32[1]{0:T(128)} %bitcast.refs_2_.lat_ref, bf16[33,32,256]{2,1,0:T(8,128)(2,1)S(1)} %collective-permute-done.2.refs_3_.refs_2_, ...), custom_call_target="tpu_custom_call" | custom-call | flops 6291456 | bytes 4718592 | tf_op jit(solution)/shard_map/lon_sums/pallas_call | solution.py:341
  36.1 0.8 %collective-permute-start.11 = (bf16[32,32,256]{2,1,0:T(8,128)(2,1)S(1)}, bf16[32,32,256]{2,1,0:T(8,128)(2,1)S(1)}, u32[]{:S(2)}, u32[]{:S(2)}) collective-permute-start(bf16[32,32,256]{2,1,0:T(8,128)(2,1)S(1)} %get-tuple-element.59), channel_id=1, source_target_pairs={{0,2},{1,3},{4,6},{5,7},{2,0},{3,1},{6,4},{7,5},{8,10},{9,11},{12,... | collective-permute-start | bytes 1572872 | tf_op jit(solution)/shard_map/ppermute | solution.py:21
  36.9 2.6 %collective-permute-start.12 = (bf16[32,32,256]{2,1,0:T(8,128)(2,1)S(1)}, bf16[32,32,256]{2,1,0:T(8,128)(2,1)S(1)}, u32[]{:S(2)}, u32[]{:S(2)}) collective-permute-start(bf16[32,32,256]{2,1,0:T(8,128)(2,1)S(1)} %get-tuple-element.60), channel_id=1, source_target_pairs={{2,4},{3,5},{6,0},{7,1},{4,2},{5,3},{0,6},{1,7},{10,12},{11,13},{1... | collective-permute-start | bytes 1572872 | tf_op jit(solution)/shard_map/ppermute | solution.py:21
  39.5 2.1 %lat_sums.1 = (bf16[32,32,256]{2,1,0:T(8,128)(2,1)S(1)}, f32[32,32,256]{2,1,0:T(8,128)S(1)}, bf16[32,32,256]{2,1,0:T(8,128)(2,1)S(1)}) custom-call(s32[1]{0:T(128)} %bitcast.8.refs_0_.core_ref, s32[1]{0:T(128)} %bitcast.9.refs_1_.chip_ref, s32[16,128]{1,0:T(8,128)S(1)} %get-tuple-element.53.index_ref, f32[16,128]{1,0:T(8,128)S(1)} %get-tuple-element.54.weight_ref, ...), custom_call_target="tpu_custom_call" | custom-call | flops 6291456 | bytes 4718592 | tf_op jit(solution)/shard_map/lat_sums/pallas_call | solution.py:341
  41.6 4.0 %collective-permute-start.9 = (bf16[32,32,256]{2,1,0:T(8,128)(2,1)S(1)}, bf16[32,32,256]{2,1,0:T(8,128)(2,1)S(1)}, u32[]{:S(2)}, u32[]{:S(2)}) collective-permute-start(bf16[32,32,256]{2,1,0:T(8,128)(2,1)S(1)} %get-tuple-element.56), channel_id=1, source_target_pairs={{0,8},{16,24},{8,0},{24,16},{1,9},{17,25},{9,1},{25,17},{2,10},{18... | collective-permute-start | bytes 1572872 | tf_op jit(solution)/shard_map/ppermute | solution.py:21
  46.2 4.3 %collective-permute-done.11.refs_1_.refs_4_.a1 = bf16[32,32,256]{2,1,0:T(8,128)(2,1)S(1)} collective-permute-done((bf16[32,32,256]{2,1,0:T(8,128)(2,1)S(1)}, bf16[32,32,256]{2,1,0:T(8,128)(2,1)S(1)}, u32[]{:S(2)}, u32[]{:S(2)}) %collective-permute-start.11) | collective-permute-done | bytes 524320 | tf_op jit(solution)/shard_map/ppermute | solution.py:21
  50.5 12.5 %collective-permute-done.12.refs_2_.refs_5_.b1 = bf16[32,32,256]{2,1,0:T(8,128)(2,1)S(1)} collective-permute-done((bf16[32,32,256]{2,1,0:T(8,128)(2,1)S(1)}, bf16[32,32,256]{2,1,0:T(8,128)(2,1)S(1)}, u32[]{:S(2)}, u32[]{:S(2)}) %collective-permute-start.12) | collective-permute-done | bytes 524320 | tf_op jit(solution)/shard_map/ppermute | solution.py:21
  64.0 1.5 %collective-permute-start.14 = (bf16[2,64,128]{2,1,0:T(8,128)(2,1)S(1)}, bf16[2,64,128]{2,1,0:T(8,128)(2,1)S(1)}, u32[]{:S(2)}, u32[]{:S(2)}) collective-permute-start(bf16[2,64,128]{2,1,0:T(8,128)(2,1)S(1)} %get-tuple-element.69), channel_id=1, source_target_pairs={{1,2},{3,4},{5,6},{7,0},{2,1},{4,3},{6,5},{0,7},{9,10},{11,12},{13... | collective-permute-start | bytes 98312 | tf_op jit(solution)/shard_map/ppermute | solution.py:21
  65.9 3.3 %collective-permute-done.14.other_ref = bf16[2,64,128]{2,1,0:T(8,128)(2,1)S(1)} collective-permute-done((bf16[2,64,128]{2,1,0:T(8,128)(2,1)S(1)}, bf16[2,64,128]{2,1,0:T(8,128)(2,1)S(1)}, u32[]{:S(2)}, u32[]{:S(2)}) %collective-permute-start.14) | collective-permute-done | bytes 32800 | tf_op jit(solution)/shard_map/ppermute | solution.py:21
  69.4 5.8 %collective-permute-start.15 = (bf16[1,64,256]{2,1,0:T(8,128)(2,1)S(1)}, bf16[1,64,256]{2,1,0:T(8,128)(2,1)S(1)}, u32[]{:S(2)}, u32[]{:S(2)}) collective-permute-start(bf16[1,64,256]{2,1,0:T(8,128)(2,1)S(1)} %get-tuple-element.70), channel_id=1, source_target_pairs={{0,8},{16,24},{8,0},{24,16},{1,9},{17,25},{9,1},{25,17},{2,10},{18... | collective-permute-start | bytes 98312 | tf_op jit(solution)/shard_map/ppermute | solution.py:21
  75.9 3.3 %final.1 = (f32[32,64,256]{2,1,0:T(8,128)}, f32[2,64,256]{2,1,0:T(8,128)S(1)}) custom-call(s32[32]{0:T(128)S(1)} %copy-done.4, f32[32,64,256]{2,1,0:T(8,128)S(1)} %combine.1.first_row.last_row.remap_ref, bf16[2,64,128]{2,1,0:T(8,128)(2,1)S(1)} %collective-permute-done.13.one_ref, bf16[2,64,128]{2,1,0:T(8,128)(2,1)S(1)} %collective-permute-done.14.other_ref, ...), custom_call_target="tpu_custom_call" | custom-call | flops 15728640 | bytes 6291456 | tf_op jit(solution)/shard_map/final/pallas_call | solution.py:564
  79.3 0.7 add_halo.1
  (38 shorter events, 4.4 us)
Async XLA Ops:
  2.3 16.3 %copy-start.3 = (bf16[1,32,256]{2,1,0:T(8,128)(2,1)S(1)}, bf16[1,32,256]{2,1,0:T(8,128)(2,1)}, u32[]{:S(2)}) copy-start(bf16[1,32,256]{2,1,0:T(8,128)(2,1)} %get-tuple-element.43.refs_4_) | copy-start | bytes 49156
  2.3 16.3 %collective-permute-start = (bf16[33,32,256]{2,1,0:T(8,128)(2,1)}, bf16[33,32,256]{2,1,0:T(8,128)(2,1)S(1)}, u32[]{:S(2)}, u32[]{:S(2)}) collective-permute-start(bf16[33,32,256]{2,1,0:T(8,128)(2,1)} %get-tuple-element.40), channel_id=1, source_target_pairs={{0,8},{16,24},{8,0},{24,16},{1,9},{17,25},{9,1},{25,17},{2,10},{18... | collective-permute-start | bytes 1622024 | tf_op jit(solution)/shard_map/ppermute | solution.py:21
  5.3 13.3 %collective-permute-start.1 = (bf16[33,32,256]{2,1,0:T(8,128)(2,1)}, bf16[33,32,256]{2,1,0:T(8,128)(2,1)S(1)}, u32[]{:S(2)}, u32[]{:S(2)}) collective-permute-start(bf16[33,32,256]{2,1,0:T(8,128)(2,1)} %get-tuple-element.40), channel_id=1, source_target_pairs={{8,16},{16,8},{9,17},{17,9},{10,18},{18,10},{11,19},{19,11},{12,20... | collective-permute-start | bytes 1622024 | tf_op jit(solution)/shard_map/ppermute | solution.py:21
  6.0 14.7 %collective-permute-start.2 = (bf16[33,32,256]{2,1,0:T(8,128)(2,1)}, bf16[33,32,256]{2,1,0:T(8,128)(2,1)S(1)}, u32[]{:S(2)}, u32[]{:S(2)}) collective-permute-start(bf16[33,32,256]{2,1,0:T(8,128)(2,1)} %get-tuple-element.47), channel_id=1, source_target_pairs={{0,2},{1,3},{4,6},{5,7},{2,0},{3,1},{6,4},{7,5},{8,10},{9,11},{12,... | collective-permute-start | bytes 1622024 | tf_op jit(solution)/shard_map/ppermute | solution.py:21
  7.6 26.1 %collective-permute-start.3 = (bf16[33,32,256]{2,1,0:T(8,128)(2,1)}, bf16[33,32,256]{2,1,0:T(8,128)(2,1)S(1)}, u32[]{:S(2)}, u32[]{:S(2)}) collective-permute-start(bf16[33,32,256]{2,1,0:T(8,128)(2,1)} %get-tuple-element.47), channel_id=1, source_target_pairs={{2,4},{3,5},{6,0},{7,1},{4,2},{5,3},{0,6},{1,7},{10,12},{11,13},{1... | collective-permute-start | bytes 1622024 | tf_op jit(solution)/shard_map/ppermute | solution.py:21
  10.1 23.6 %collective-permute-start.5 = (bf16[32,64,256]{2,1,0:T(8,128)(2,1)}, bf16[32,64,256]{2,1,0:T(8,128)(2,1)S(1)}, u32[]{:S(2)}, u32[]{:S(2)}) collective-permute-start(bf16[32,64,256]{2,1,0:T(8,128)(2,1)} %refs_0_.1), channel_id=1, source_target_pairs={{0,1},{2,3},{4,5},{6,7},{1,0},{3,2},{5,4},{7,6},{8,9},{10,11},{12,... | collective-permute-start | bytes 3145736 | tf_op jit(solution)/shard_map/ppermute | solution.py:21
  11.6 1.2 %copy-start = (bf16[32,64,256]{2,1,0:T(8,128)(2,1)S(1)}, bf16[32,64,256]{2,1,0:T(8,128)(2,1)}, u32[]{:S(2)}) copy-start(bf16[32,64,256]{2,1,0:T(8,128)(2,1)} %refs_0_.1) | copy-start | bytes 3145732
  12.9 0.9 %copy-start.2 = (f32[4,32,256]{2,1,0:T(8,128)S(1)}, f32[4,32,256]{2,1,0:T(8,128)}, u32[]{:S(2)}) copy-start(f32[4,32,256]{2,1,0:T(8,128)} %rates_ref) | copy-start | bytes 393220
  13.8 5.0 %copy-start.4 = (s32[32]{0:T(128)S(1)}, s32[32]{0:T(128)}, u32[]{:S(2)}) copy-start(s32[32]{0:T(128)} %offset_ref.1) | copy-start | bytes 388
  13.8 20.0 %copy-start.1 = (bf16[32,64,256]{2,1,0:T(8,128)(2,1)S(1)}, bf16[32,64,256]{2,1,0:T(8,128)(2,1)}, u32[]{:S(2)}) copy-start(bf16[32,64,256]{2,1,0:T(8,128)(2,1)} %refs_0_.1) | copy-start | bytes 3145732
  18.9 14.9 %collective-permute-start.4 = (bf16[33,32,256]{2,1,0:T(8,128)(2,1)S(1)}, bf16[33,32,256]{2,1,0:T(8,128)(2,1)S(1)}, u32[]{:S(2)}, u32[]{:S(2)}) collective-permute-start(bf16[33,32,256]{2,1,0:T(8,128)(2,1)S(1)} %collective-permute-done.refs_3_.refs_6_), channel_id=1, source_target_pairs={{0,1},{2,3},{4,5},{6,7},{1,0},{3,2},{5,4},{7,6},{8,9},{10,11},{12,... | collective-permute-start | bytes 1622024 | tf_op jit(solution)/shard_map/ppermute | solution.py:21
  19.0 14.8 %collective-permute-start.6 = (bf16[33,32,256]{2,1,0:T(8,128)(2,1)S(1)}, bf16[33,32,256]{2,1,0:T(8,128)(2,1)S(1)}, u32[]{:S(2)}, u32[]{:S(2)}) collective-permute-start(bf16[33,32,256]{2,1,0:T(8,128)(2,1)S(1)} %collective-permute-done.1.refs_5_.refs_8_), channel_id=1, source_target_pairs={{0,1},{2,3},{4,5},{6,7},{1,0},{3,2},{5,4},{7,6},{8,9},{10,11},{12,... | collective-permute-start | bytes 1622024 | tf_op jit(solution)/shard_map/ppermute | solution.py:21
  20.7 18.8 %collective-permute-start.7 = (bf16[33,32,256]{2,1,0:T(8,128)(2,1)S(1)}, bf16[33,32,256]{2,1,0:T(8,128)(2,1)S(1)}, u32[]{:S(2)}, u32[]{:S(2)}) collective-permute-start(bf16[33,32,256]{2,1,0:T(8,128)(2,1)S(1)} %collective-permute-done.2.refs_3_.refs_2_), channel_id=1, source_target_pairs={{0,1},{2,3},{4,5},{6,7},{1,0},{3,2},{5,4},{7,6},{8,9},{10,11},{12,... | collective-permute-start | bytes 1622024 | tf_op jit(solution)/shard_map/ppermute | solution.py:21
  33.7 5.7 %collective-permute-start.8 = (bf16[33,32,256]{2,1,0:T(8,128)(2,1)S(1)}, bf16[33,32,256]{2,1,0:T(8,128)(2,1)S(1)}, u32[]{:S(2)}, u32[]{:S(2)}) collective-permute-start(bf16[33,32,256]{2,1,0:T(8,128)(2,1)S(1)} %collective-permute-done.3.refs_5_.refs_3_), channel_id=1, source_target_pairs={{0,1},{2,3},{4,5},{6,7},{1,0},{3,2},{5,4},{7,6},{8,9},{10,11},{12,... | collective-permute-start | bytes 1622024 | tf_op jit(solution)/shard_map/ppermute | solution.py:21
  36.1 14.4 %collective-permute-start.11 = (bf16[32,32,256]{2,1,0:T(8,128)(2,1)S(1)}, bf16[32,32,256]{2,1,0:T(8,128)(2,1)S(1)}, u32[]{:S(2)}, u32[]{:S(2)}) collective-permute-start(bf16[32,32,256]{2,1,0:T(8,128)(2,1)S(1)} %get-tuple-element.59), channel_id=1, source_target_pairs={{0,2},{1,3},{4,6},{5,7},{2,0},{3,1},{6,4},{7,5},{8,10},{9,11},{12,... | collective-permute-start | bytes 1572872 | tf_op jit(solution)/shard_map/ppermute | solution.py:21
  36.9 26.1 %collective-permute-start.12 = (bf16[32,32,256]{2,1,0:T(8,128)(2,1)S(1)}, bf16[32,32,256]{2,1,0:T(8,128)(2,1)S(1)}, u32[]{:S(2)}, u32[]{:S(2)}) collective-permute-start(bf16[32,32,256]{2,1,0:T(8,128)(2,1)S(1)} %get-tuple-element.60), channel_id=1, source_target_pairs={{2,4},{3,5},{6,0},{7,1},{4,2},{5,3},{0,6},{1,7},{10,12},{11,13},{1... | collective-permute-start | bytes 1572872 | tf_op jit(solution)/shard_map/ppermute | solution.py:21
  41.6 21.9 %collective-permute-start.9 = (bf16[32,32,256]{2,1,0:T(8,128)(2,1)S(1)}, bf16[32,32,256]{2,1,0:T(8,128)(2,1)S(1)}, u32[]{:S(2)}, u32[]{:S(2)}) collective-permute-start(bf16[32,32,256]{2,1,0:T(8,128)(2,1)S(1)} %get-tuple-element.56), channel_id=1, source_target_pairs={{0,8},{16,24},{8,0},{24,16},{1,9},{17,25},{9,1},{25,17},{2,10},{18... | collective-permute-start | bytes 1572872 | tf_op jit(solution)/shard_map/ppermute | solution.py:21
  45.6 17.9 %collective-permute-start.10 = (bf16[32,32,256]{2,1,0:T(8,128)(2,1)S(1)}, bf16[32,32,256]{2,1,0:T(8,128)(2,1)S(1)}, u32[]{:S(2)}, u32[]{:S(2)}) collective-permute-start(bf16[32,32,256]{2,1,0:T(8,128)(2,1)S(1)} %get-tuple-element.57), channel_id=1, source_target_pairs={{8,16},{16,8},{9,17},{17,9},{10,18},{18,10},{11,19},{19,11},{12,20... | collective-permute-start | bytes 1572872 | tf_op jit(solution)/shard_map/ppermute | solution.py:21
  63.9 2.0 %collective-permute-start.13 = (bf16[2,64,128]{2,1,0:T(8,128)(2,1)S(1)}, bf16[2,64,128]{2,1,0:T(8,128)(2,1)S(1)}, u32[]{:S(2)}, u32[]{:S(2)}) collective-permute-start(bf16[2,64,128]{2,1,0:T(8,128)(2,1)S(1)} %get-tuple-element.68), channel_id=1, source_target_pairs={{0,1},{2,3},{4,5},{6,7},{1,0},{3,2},{5,4},{7,6},{8,9},{10,11},{12,... | collective-permute-start | bytes 98312 | tf_op jit(solution)/shard_map/ppermute | solution.py:21
  64.0 5.2 %collective-permute-start.14 = (bf16[2,64,128]{2,1,0:T(8,128)(2,1)S(1)}, bf16[2,64,128]{2,1,0:T(8,128)(2,1)S(1)}, u32[]{:S(2)}, u32[]{:S(2)}) collective-permute-start(bf16[2,64,128]{2,1,0:T(8,128)(2,1)S(1)} %get-tuple-element.69), channel_id=1, source_target_pairs={{1,2},{3,4},{5,6},{7,0},{2,1},{4,3},{6,5},{0,7},{9,10},{11,12},{13... | collective-permute-start | bytes 98312 | tf_op jit(solution)/shard_map/ppermute | solution.py:21
  65.9 10.0 %copy-start.5 = (f32[32,256]{1,0:T(8,128)S(1)}, f32[32,256]{1,0:T(8,128)}, u32[]{:S(2)}) copy-start(f32[32,256]{1,0:T(8,128)} %param.19) | copy-start | bytes 98308
  69.4 9.9 %collective-permute-start.15 = (bf16[1,64,256]{2,1,0:T(8,128)(2,1)S(1)}, bf16[1,64,256]{2,1,0:T(8,128)(2,1)S(1)}, u32[]{:S(2)}, u32[]{:S(2)}) collective-permute-start(bf16[1,64,256]{2,1,0:T(8,128)(2,1)S(1)} %get-tuple-element.70), channel_id=1, source_target_pairs={{0,8},{16,24},{8,0},{24,16},{1,9},{17,25},{9,1},{25,17},{2,10},{18... | collective-permute-start | bytes 98312 | tf_op jit(solution)/shard_map/ppermute | solution.py:21
  75.2 4.1 %collective-permute-start.16 = (bf16[1,64,256]{2,1,0:T(8,128)(2,1)S(1)}, bf16[1,64,256]{2,1,0:T(8,128)(2,1)S(1)}, u32[]{:S(2)}, u32[]{:S(2)}) collective-permute-start(bf16[1,64,256]{2,1,0:T(8,128)(2,1)S(1)} %get-tuple-element.71), channel_id=1, source_target_pairs={{8,16},{16,8},{9,17},{17,9},{10,18},{18,10},{11,19},{19,11},{12,20... | collective-permute-start | bytes 98312 | tf_op jit(solution)/shard_map/ppermute | solution.py:21

commit v4 on v3

--- a/solution.py
+++ b/solution.py
@@ -491,14 +491,18 @@
 
 
 def final_kernel(
-    offset_ref, remap_ref, one_ref, other_ref, kappa_ref, local_ref, out_ref, outer_ref, edge_ref, sums_ref, sems
+    spread_ref, remap_ref, one_ref, other_ref, kappa_ref, local_ref, out_ref, outer_ref,
+    offset_ref, edge_ref, sums_ref, sems,
 ):
     rows, bins, width = remap_ref.shape
+    offsets = pltpu.make_async_copy(spread_ref, offset_ref, sems.at[sems.shape[0] - 1])
+    offsets.start()
     count = width // 128
     lane = lax.broadcasted_iota(jnp.int32, (8, 128), 1)
     spots = [slice(128 * t, 128 * t + 128) for t in range(count)]
     for r in range(rows):
         edge_ref[r] = edge_tile(one_ref, other_ref, r)
+    offsets.wait()
 
     def moved(row, edge, amount):
         row = [jnp.where(lane < -amount, edge, row[0])] + row[1:]
@@ -517,7 +521,7 @@
         stores = []
         sent = 1
         for r in range(rows):
-            amount = offset_ref[r]
+            amount = offset_ref[r, 0, 0]
             kappa = [kappa_ref[r, :, spot] for spot in spots]
             above = [kappa_ref[max(r - 1, 0), :, spot] for spot in spots]
             for at in pieces:
@@ -558,26 +562,27 @@
         copy.wait()
 
 
-def final(offset, remapped, one, other, kappa, local):
+def final(spread, remapped, one, other, kappa, local):
     rows, bins, width = remapped.shape
     vmem = pl.BlockSpec(memory_space=pltpu.VMEM)
     return pl.pallas_call(
         final_kernel,
-        in_specs=[in_smem()] + [vmem] * 5,
+        in_specs=[vmem] * 6,
         out_specs=[in_place(), vmem],
         out_shape=[
             jax.ShapeDtypeStruct(local.shape, jnp.float32),
             jax.ShapeDtypeStruct((2, bins, width), jnp.float32),
         ],
         scratch_shapes=[
+            pltpu.SMEM(spread.shape, jnp.int32),
             pltpu.VMEM((rows, bins, 128), jnp.float32),
             pltpu.VMEM((rows, bins, width), jnp.float32),
-            pltpu.SemaphoreType.DMA((2 * (rows // 8),)),
+            pltpu.SemaphoreType.DMA((2 * (rows // 8) + 1,)),
         ],
         compiler_params=pltpu.CompilerParams(vmem_limit_bytes=TABLE_BYTES),
         cost_estimate=pl.CostEstimate(flops=30 * remapped.size, bytes_accessed=12 * remapped.size, transcendentals=0),
         name="final",
-    )(offset, remapped, one, other, kappa, local)
+    )(spread, remapped, one, other, kappa, local)
 
 
 def halo_kernel(lat_ref, one_ref, other_ref, kappa_ref, outer_ref, _, out_ref, sums_ref, sems):
@@ -632,15 +637,17 @@
     beside = swap_core(conc)
     rates, meta = lax.optimization_barrier((agg_rates, meta))
     local = local_terms(conc, rates, toeplitz, settle)
+    spread = jnp.broadcast_to(zonal_offset[:, None, None], (rows, 1, 128))
+    lat1, local, spread = lax.optimization_barrier((lat1, local, spread))
+    beside_lat1, beside_lat2 = swap_core(lat1), swap_core(lat2)
     terms = decoded(flags, [lat1, meta, lat2], lat_slots, rows, half, entries)
-    spread = jnp.broadcast_to(zonal_offset[:, None, None], (rows, 1, 128))
-    lat1, lat2, local, terms, spread = lax.optimization_barrier((lat1, lat2, local, terms, spread))
+    lon1, lon2, terms = lax.optimization_barrier((lon1, lon2, terms))
 
     to_lon1, own1, to_lon2 = lon_sums(
         flags,
         [lon1, meta, lon2],
         lon_slots,
-        [(lat1, 0), (conc, half), (lat2, 0), (swap_core(lat1), 0), (beside, half), (swap_core(lat2), 0)],
+        [(lat1, 0), (conc, half), (lat2, 0), (beside_lat1, 0), (beside, half), (beside_lat2, 0)],
         rows,
         half,
         entries,
@@ -668,7 +675,7 @@
     remapped = combine(parts0, parts1)
     row1, row2 = outer_rows(flags[2], spread, remapped, one, other)
     row1, row2 = swap_lat(row1, 0), swap_lat(row2, 1)
-    partial, outer = final(zonal_offset, remapped, one, other, kappa, local)
+    partial, outer = final(spread, remapped, one, other, kappa, local)
     return add_halo(flags[2], row1, row2, kappa, outer, partial)
 
 

time: 81.1 us -> 83.3 us (1.027)
  Pallas kernels: 14.1 us -> 16.7 us
  waiting for transfers between devices: 37.4 us -> 35.8 us
  starting transfers between devices: 24.4 us -> 25.4 us
    pallas_call x2, Pallas kernels: 4.4 us -> 6.24 us  [sums_call(): pl.pallas_call(kernel, in_specs=[in_smem()] * smem + [in_place()] * (len(...]
    ppermute x17, waiting for transfers between devices: 37.4 us -> 35.8 us  [exchange(): lax.ppermute(value, axis, [(i, j) for i, j in pairs] + [(j, i) for i, j i...]
    ppermute x17, starting transfers between devices: 24.4 us -> 25.4 us  [exchange(): lax.ppermute(value, axis, [(i, j) for i, j in pairs] + [(j, i) for i, j i...]
  transfers between devices with their start and end apart: 17 -> 17, of which waited for: 6 -> 6; matrix products, arithmetic and copies ran while one was open for 2% -> 2% of each run, Pallas kernels for 13% -> 16%
where the time goes in v4:
time: 83.3 us; the launch traced here: 82 us
  waiting for transfers between devices  35.8 us (43%)
  starting transfers between devices  25.4 us (30%)
  Pallas kernels  16.7 us (20%)
  local copies, waits for them, and re-layouts  3.76 us (5%)
    ppermute x17, waiting for transfers between devices, exchange(): lax.ppermute(value, axis, [(i, j) for i, j in pairs] + [(j, i) for i, j i...  35.8 us
    ppermute x17, starting transfers between devices, exchange(): lax.ppermute(value, axis, [(i, j) for i, j in pairs] + [(j, i) for i, j i...  25.4 us
    pallas_call x2, Pallas kernels, sums_call(): pl.pallas_call(kernel, in_specs=[in_smem()] * smem + [in_place()] * (len(...  6.24 us
    pallas_call x1, Pallas kernels, final(): pl.pallas_call(final_kernel, in_specs=[vmem] * 6, out_specs=[in_place(),...  3.52 us
    pallas_call x1, Pallas kernels, messages(): pl.pallas_call(messages_kernel, in_specs=[in_place()] * 5, out_specs=[pl....  2.3 us
    unnamed x12, local copies, waits for them, and re-layouts  2.14 us
    pallas_call x1, Pallas kernels, local_terms(): pl.pallas_call(growth_kernel, grid=(rows // step,), in_specs=[pl.BlockSpe...  1.81 us
  transfers between devices with their start and end apart: 17, of which 6 were waited for; matrix products, arithmetic and copies ran while one was open for 2% of the time, Pallas kernels for 16%

profile of v4, /device:TPU:0, one launch (start us, length us, event | category | flops | bytes accessed | tf_op | source)
XLA Modules:
  0.0 82.0 jit_solution(11966648021516998988)
XLA Ops:
  0.0 2.3 %messages.1 = (bf16[33,32,256]{2,1,0:T(8,128)(2,1)}, bf16[33,32,256]{2,1,0:T(8,128)(2,1)}, bf16[1,32,256]{2,1,0:T(8,128)(2,1)}) custom-call(bf16[32,64,256]{2,1,0:T(8,128)(2,1)} %refs_0_.1, s32[4,32]{1,0:T(4,128)} %bitcast.13, s32[4,32]{1,0:T(4,128)} %bitcast.14, f32[4,32]{1,0:T(4,128)} %bitcast.15, s32[1,32]{1,0:T(1,128)} %count_hbm.1), custom_call_target="tpu_custom_call" | custom-call | bytes 2097152 | tf_op jit(solution)/shard_map/messages/pallas_call | solution.py:150
  2.3 3.0 %collective-permute-start = (bf16[33,32,256]{2,1,0:T(8,128)(2,1)}, bf16[33,32,256]{2,1,0:T(8,128)(2,1)}, u32[]{:S(2)}, u32[]{:S(2)}) collective-permute-start(bf16[33,32,256]{2,1,0:T(8,128)(2,1)} %get-tuple-element.41), channel_id=1, source_target_pairs={{0,8},{16,24},{8,0},{24,16},{1,9},{17,25},{9,1},{25,17},{2,10},{18... | collective-permute-start | bytes 1622024 | tf_op jit(solution)/shard_map/ppermute | solution.py:21
  5.3 1.5 %collective-permute-start.3 = (bf16[33,32,256]{2,1,0:T(8,128)(2,1)}, bf16[33,32,256]{2,1,0:T(8,128)(2,1)}, u32[]{:S(2)}, u32[]{:S(2)}) collective-permute-start(bf16[33,32,256]{2,1,0:T(8,128)(2,1)} %get-tuple-element.41), channel_id=1, source_target_pairs={{8,16},{16,8},{9,17},{17,9},{10,18},{18,10},{11,19},{19,11},{12,20... | collective-permute-start | bytes 1622024 | tf_op jit(solution)/shard_map/ppermute | solution.py:21
  6.8 1.6 %collective-permute-start.1 = (bf16[33,32,256]{2,1,0:T(8,128)(2,1)}, bf16[33,32,256]{2,1,0:T(8,128)(2,1)}, u32[]{:S(2)}, u32[]{:S(2)}) collective-permute-start(bf16[33,32,256]{2,1,0:T(8,128)(2,1)} %get-tuple-element.45), channel_id=1, source_target_pairs={{0,2},{1,3},{4,6},{5,7},{2,0},{3,1},{6,4},{7,5},{8,10},{9,11},{12,... | collective-permute-start | bytes 1622024 | tf_op jit(solution)/shard_map/ppermute | solution.py:21
  8.4 2.5 %collective-permute-start.2 = (bf16[33,32,256]{2,1,0:T(8,128)(2,1)}, bf16[33,32,256]{2,1,0:T(8,128)(2,1)}, u32[]{:S(2)}, u32[]{:S(2)}) collective-permute-start(bf16[33,32,256]{2,1,0:T(8,128)(2,1)} %get-tuple-element.45), channel_id=1, source_target_pairs={{2,4},{3,5},{6,0},{7,1},{4,2},{5,3},{0,6},{1,7},{10,12},{11,13},{1... | collective-permute-start | bytes 1622024 | tf_op jit(solution)/shard_map/ppermute | solution.py:21
  10.8 0.8 rev.3
  11.6 0.7 copy.12.settle_ref
  12.4 1.2 %copy-done = bf16[32,64,256]{2,1,0:T(8,128)(2,1)S(1)} copy-done((bf16[32,64,256]{2,1,0:T(8,128)(2,1)S(1)}, bf16[32,64,256]{2,1,0:T(8,128)(2,1)}, u32[]{:S(2)}) %copy-start) | copy-done | bytes 1048600
  13.6 0.9 %copy-done.2 = f32[4,32,256]{2,1,0:T(8,128)S(1)} copy-done((f32[4,32,256]{2,1,0:T(8,128)S(1)}, f32[4,32,256]{2,1,0:T(8,128)}, u32[]{:S(2)}) %copy-start.2) | copy-done | bytes 131096
  14.5 1.8 %growth.1.local_ref = f32[32,64,256]{2,1,0:T(8,128)S(1)} custom-call(f32[4,128]{1,0:T(4,128)S(1)} %pad_convert_fusion.flip_ref, f32[64,1]{1,0:T(8,128)S(1)} %copy.12.settle_ref, bf16[32,64,256]{2,1,0:T(8,128)(2,1)S(1)} %copy-done, f32[4,32,256]{2,1,0:T(8,128)S(1)} %copy-done.2), custom_call_target="tpu_custom_call" | custom-call | flops 268435456 | bytes 4194304 | tf_op jit(solution)/shard_map/growth/pallas_call | solution.py:90
  16.3 2.4 %collective-permute-done.refs_3_.refs_6_ = bf16[33,32,256]{2,1,0:T(8,128)(2,1)} collective-permute-done((bf16[33,32,256]{2,1,0:T(8,128)(2,1)}, bf16[33,32,256]{2,1,0:T(8,128)(2,1)}, u32[]{:S(2)}, u32[]{:S(2)}) %collective-permute-start) | collective-permute-done | bytes 540704 | tf_op jit(solution)/shard_map/ppermute | solution.py:21
  19.4 0.8 decode.1
  20.3 1.1 %collective-permute-done.1.refs_3_.refs_2_ = bf16[33,32,256]{2,1,0:T(8,128)(2,1)} collective-permute-done((bf16[33,32,256]{2,1,0:T(8,128)(2,1)}, bf16[33,32,256]{2,1,0:T(8,128)(2,1)}, u32[]{:S(2)}, u32[]{:S(2)}) %collective-permute-start.1) | collective-permute-done | bytes 540704 | tf_op jit(solution)/shard_map/ppermute | solution.py:21
  21.4 13.2 %collective-permute-done.2.refs_5_.refs_3_ = bf16[33,32,256]{2,1,0:T(8,128)(2,1)} collective-permute-done((bf16[33,32,256]{2,1,0:T(8,128)(2,1)}, bf16[33,32,256]{2,1,0:T(8,128)(2,1)}, u32[]{:S(2)}, u32[]{:S(2)}) %collective-permute-start.2) | collective-permute-done | bytes 540704 | tf_op jit(solution)/shard_map/ppermute | solution.py:21
  35.1 3.0 %lon_sums.1 = (bf16[32,32,256]{2,1,0:T(8,128)(2,1)S(1)}, f32[32,32,256]{2,1,0:T(8,128)S(1)}, bf16[32,32,256]{2,1,0:T(8,128)(2,1)S(1)}) custom-call(s32[1]{0:T(128)} %bitcast.8.refs_0_.core_ref, s32[1]{0:T(128)} %bitcast.9.refs_1_.chip_ref, s32[1]{0:T(128)} %bitcast.refs_2_.lat_ref, bf16[33,32,256]{2,1,0:T(8,128)(2,1)} %collective-permute-done.1.refs_3_.refs_2_, ...), custom_call_target="tpu_custom_call" | custom-call | flops 6291456 | bytes 4718592 | tf_op jit(solution)/shard_map/lon_sums/pallas_call | solution.py:341
  38.7 2.6 %collective-permute-start.12 = (bf16[32,32,256]{2,1,0:T(8,128)(2,1)S(1)}, bf16[32,32,256]{2,1,0:T(8,128)(2,1)S(1)}, u32[]{:S(2)}, u32[]{:S(2)}) collective-permute-start(bf16[32,32,256]{2,1,0:T(8,128)(2,1)S(1)} %get-tuple-element.62), channel_id=1, source_target_pairs={{2,4},{3,5},{6,0},{7,1},{4,2},{5,3},{0,6},{1,7},{10,12},{11,13},{1... | collective-permute-start | bytes 1572872 | tf_op jit(solution)/shard_map/ppermute | solution.py:21
  41.3 3.3 %lat_sums.1 = (bf16[32,32,256]{2,1,0:T(8,128)(2,1)S(1)}, f32[32,32,256]{2,1,0:T(8,128)S(1)}, bf16[32,32,256]{2,1,0:T(8,128)(2,1)S(1)}) custom-call(s32[1]{0:T(128)} %bitcast.8.refs_0_.core_ref, s32[1]{0:T(128)} %bitcast.9.refs_1_.chip_ref, s32[16,128]{1,0:T(8,128)S(1)} %get-tuple-element.55.index_ref, f32[16,128]{1,0:T(8,128)S(1)} %get-tuple-element.56.weight_ref, ...), custom_call_target="tpu_custom_call" | custom-call | flops 6291456 | bytes 4718592 | tf_op jit(solution)/shard_map/lat_sums/pallas_call | solution.py:341
  44.6 3.3 %collective-permute-start.9 = (bf16[32,32,256]{2,1,0:T(8,128)(2,1)S(1)}, bf16[32,32,256]{2,1,0:T(8,128)(2,1)S(1)}, u32[]{:S(2)}, u32[]{:S(2)}) collective-permute-start(bf16[32,32,256]{2,1,0:T(8,128)(2,1)S(1)} %get-tuple-element.58), channel_id=1, source_target_pairs={{0,8},{16,24},{8,0},{24,16},{1,9},{17,25},{9,1},{25,17},{2,10},{18... | collective-permute-start | bytes 1572872 | tf_op jit(solution)/shard_map/ppermute | solution.py:21
  48.6 3.2 %collective-permute-done.11.refs_1_.refs_4_.a1 = bf16[32,32,256]{2,1,0:T(8,128)(2,1)S(1)} collective-permute-done((bf16[32,32,256]{2,1,0:T(8,128)(2,1)S(1)}, bf16[32,32,256]{2,1,0:T(8,128)(2,1)S(1)}, u32[]{:S(2)}, u32[]{:S(2)}) %collective-permute-start.11) | collective-permute-done | bytes 524320 | tf_op jit(solution)/shard_map/ppermute | solution.py:21
  51.9 12.4 %collective-permute-done.12.refs_2_.refs_5_.b1 = bf16[32,32,256]{2,1,0:T(8,128)(2,1)S(1)} collective-permute-done((bf16[32,32,256]{2,1,0:T(8,128)(2,1)S(1)}, bf16[32,32,256]{2,1,0:T(8,128)(2,1)S(1)}, u32[]{:S(2)}, u32[]{:S(2)}) %collective-permute-start.12) | collective-permute-done | bytes 524320 | tf_op jit(solution)/shard_map/ppermute | solution.py:21
  65.2 1.4 %collective-permute-start.14 = (bf16[2,64,128]{2,1,0:T(8,128)(2,1)S(1)}, bf16[2,64,128]{2,1,0:T(8,128)(2,1)S(1)}, u32[]{:S(2)}, u32[]{:S(2)}) collective-permute-start(bf16[2,64,128]{2,1,0:T(8,128)(2,1)S(1)} %get-tuple-element.71), channel_id=1, source_target_pairs={{1,2},{3,4},{5,6},{7,0},{2,1},{4,3},{6,5},{0,7},{9,10},{11,12},{13... | collective-permute-start | bytes 98312 | tf_op jit(solution)/shard_map/ppermute | solution.py:21
  67.0 3.4 %collective-permute-done.14.other_ref = bf16[2,64,128]{2,1,0:T(8,128)(2,1)S(1)} collective-permute-done((bf16[2,64,128]{2,1,0:T(8,128)(2,1)S(1)}, bf16[2,64,128]{2,1,0:T(8,128)(2,1)S(1)}, u32[]{:S(2)}, u32[]{:S(2)}) %collective-permute-start.14) | collective-permute-done | bytes 32800 | tf_op jit(solution)/shard_map/ppermute | solution.py:21
  70.6 6.4 %collective-permute-start.15 = (bf16[1,64,256]{2,1,0:T(8,128)(2,1)S(1)}, bf16[1,64,256]{2,1,0:T(8,128)(2,1)S(1)}, u32[]{:S(2)}, u32[]{:S(2)}) collective-permute-start(bf16[1,64,256]{2,1,0:T(8,128)(2,1)S(1)} %get-tuple-element.72), channel_id=1, source_target_pairs={{0,8},{16,24},{8,0},{24,16},{1,9},{17,25},{9,1},{25,17},{2,10},{18... | collective-permute-start | bytes 98312 | tf_op jit(solution)/shard_map/ppermute | solution.py:21
  77.7 3.5 %final.1 = (f32[32,64,256]{2,1,0:T(8,128)}, f32[2,64,256]{2,1,0:T(8,128)S(1)}) custom-call(s32[32,1,128]{2,1,0:T(1,128)S(1)} %broadcast_in_dim.13.offset_ref.spread_ref, f32[32,64,256]{2,1,0:T(8,128)S(1)} %combine.1.first_row.last_row.remap_ref, bf16[2,64,128]{2,1,0:T(8,128)(2,1)S(1)} %collective-permute-done.13.one_ref, ...), custom_call_target="tpu_custom_call" | custom-call | flops 15728640 | bytes 6291456 | tf_op jit(solution)/shard_map/final/pallas_call | solution.py:568
  (38 shorter events, 5.4 us)
Async XLA Ops:
  0.0 18.8 %copy-start.5 = (s32[32]{0:T(128)S(1)}, s32[32]{0:T(128)}, u32[]{:S(2)}) copy-start(s32[32]{0:T(128)} %param.15) | copy-start | bytes 388
  2.3 17.1 %copy-start.3 = (bf16[1,32,256]{2,1,0:T(8,128)(2,1)S(1)}, bf16[1,32,256]{2,1,0:T(8,128)(2,1)}, u32[]{:S(2)}) copy-start(bf16[1,32,256]{2,1,0:T(8,128)(2,1)} %get-tuple-element.47.refs_4_) | copy-start | bytes 49156
  2.3 16.4 %collective-permute-start = (bf16[33,32,256]{2,1,0:T(8,128)(2,1)}, bf16[33,32,256]{2,1,0:T(8,128)(2,1)}, u32[]{:S(2)}, u32[]{:S(2)}) collective-permute-start(bf16[33,32,256]{2,1,0:T(8,128)(2,1)} %get-tuple-element.41), channel_id=1, source_target_pairs={{0,8},{16,24},{8,0},{24,16},{1,9},{17,25},{9,1},{25,17},{2,10},{18... | collective-permute-start | bytes 1622024 | tf_op jit(solution)/shard_map/ppermute | solution.py:21
  5.3 13.6 %collective-permute-start.3 = (bf16[33,32,256]{2,1,0:T(8,128)(2,1)}, bf16[33,32,256]{2,1,0:T(8,128)(2,1)}, u32[]{:S(2)}, u32[]{:S(2)}) collective-permute-start(bf16[33,32,256]{2,1,0:T(8,128)(2,1)} %get-tuple-element.41), channel_id=1, source_target_pairs={{8,16},{16,8},{9,17},{17,9},{10,18},{18,10},{11,19},{19,11},{12,20... | collective-permute-start | bytes 1622024 | tf_op jit(solution)/shard_map/ppermute | solution.py:21
  6.8 14.6 %collective-permute-start.1 = (bf16[33,32,256]{2,1,0:T(8,128)(2,1)}, bf16[33,32,256]{2,1,0:T(8,128)(2,1)}, u32[]{:S(2)}, u32[]{:S(2)}) collective-permute-start(bf16[33,32,256]{2,1,0:T(8,128)(2,1)} %get-tuple-element.45), channel_id=1, source_target_pairs={{0,2},{1,3},{4,6},{5,7},{2,0},{3,1},{6,4},{7,5},{8,10},{9,11},{12,... | collective-permute-start | bytes 1622024 | tf_op jit(solution)/shard_map/ppermute | solution.py:21
  8.4 26.2 %collective-permute-start.2 = (bf16[33,32,256]{2,1,0:T(8,128)(2,1)}, bf16[33,32,256]{2,1,0:T(8,128)(2,1)}, u32[]{:S(2)}, u32[]{:S(2)}) collective-permute-start(bf16[33,32,256]{2,1,0:T(8,128)(2,1)} %get-tuple-element.45), channel_id=1, source_target_pairs={{2,4},{3,5},{6,0},{7,1},{4,2},{5,3},{0,6},{1,7},{10,12},{11,13},{1... | collective-permute-start | bytes 1622024 | tf_op jit(solution)/shard_map/ppermute | solution.py:21
  10.8 24.2 %collective-permute-start.5 = (bf16[32,64,256]{2,1,0:T(8,128)(2,1)}, bf16[32,64,256]{2,1,0:T(8,128)(2,1)}, u32[]{:S(2)}, u32[]{:S(2)}) collective-permute-start(bf16[32,64,256]{2,1,0:T(8,128)(2,1)} %refs_0_.1), channel_id=1, source_target_pairs={{0,1},{2,3},{4,5},{6,7},{1,0},{3,2},{5,4},{7,6},{8,9},{10,11},{12,... | collective-permute-start | bytes 3145736 | tf_op jit(solution)/shard_map/ppermute | solution.py:21
  12.4 1.2 %copy-start = (bf16[32,64,256]{2,1,0:T(8,128)(2,1)S(1)}, bf16[32,64,256]{2,1,0:T(8,128)(2,1)}, u32[]{:S(2)}) copy-start(bf16[32,64,256]{2,1,0:T(8,128)(2,1)} %refs_0_.1) | copy-start | bytes 3145732
  13.6 0.9 %copy-start.2 = (f32[4,32,256]{2,1,0:T(8,128)S(1)}, f32[4,32,256]{2,1,0:T(8,128)}, u32[]{:S(2)}) copy-start(f32[4,32,256]{2,1,0:T(8,128)} %rates_ref) | copy-start | bytes 393220
  14.5 20.6 %copy-start.1 = (bf16[32,64,256]{2,1,0:T(8,128)(2,1)S(1)}, bf16[32,64,256]{2,1,0:T(8,128)(2,1)}, u32[]{:S(2)}) copy-start(bf16[32,64,256]{2,1,0:T(8,128)(2,1)} %refs_0_.1) | copy-start | bytes 3145732
  18.8 16.2 %collective-permute-start.4 = (bf16[33,32,256]{2,1,0:T(8,128)(2,1)}, bf16[33,32,256]{2,1,0:T(8,128)(2,1)}, u32[]{:S(2)}, u32[]{:S(2)}) collective-permute-start(bf16[33,32,256]{2,1,0:T(8,128)(2,1)} %collective-permute-done.refs_3_.refs_6_), channel_id=1, source_target_pairs={{0,1},{2,3},{4,5},{6,7},{1,0},{3,2},{5,4},{7,6},{8,9},{10,11},{12,... | collective-permute-start | bytes 1622024 | tf_op jit(solution)/shard_map/ppermute | solution.py:21
  18.9 16.1 %collective-permute-start.6 = (bf16[33,32,256]{2,1,0:T(8,128)(2,1)}, bf16[33,32,256]{2,1,0:T(8,128)(2,1)}, u32[]{:S(2)}, u32[]{:S(2)}) collective-permute-start(bf16[33,32,256]{2,1,0:T(8,128)(2,1)} %collective-permute-done.3.refs_5_.refs_8_), channel_id=1, source_target_pairs={{0,1},{2,3},{4,5},{6,7},{1,0},{3,2},{5,4},{7,6},{8,9},{10,11},{12,... | collective-permute-start | bytes 1622024 | tf_op jit(solution)/shard_map/ppermute | solution.py:21
  34.6 6.8 %collective-permute-start.7 = (bf16[33,32,256]{2,1,0:T(8,128)(2,1)}, bf16[33,32,256]{2,1,0:T(8,128)(2,1)S(1)}, u32[]{:S(2)}, u32[]{:S(2)}) collective-permute-start(bf16[33,32,256]{2,1,0:T(8,128)(2,1)} %collective-permute-done.1.refs_3_.refs_2_), channel_id=1, source_target_pairs={{0,1},{2,3},{4,5},{6,7},{1,0},{3,2},{5,4},{7,6},{8,9},{10,11},{12,... | collective-permute-start | bytes 1622024 | tf_op jit(solution)/shard_map/ppermute | solution.py:21
  34.6 6.8 %collective-permute-start.8 = (bf16[33,32,256]{2,1,0:T(8,128)(2,1)}, bf16[33,32,256]{2,1,0:T(8,128)(2,1)S(1)}, u32[]{:S(2)}, u32[]{:S(2)}) collective-permute-start(bf16[33,32,256]{2,1,0:T(8,128)(2,1)} %collective-permute-done.2.refs_5_.refs_3_), channel_id=1, source_target_pairs={{0,1},{2,3},{4,5},{6,7},{1,0},{3,2},{5,4},{7,6},{8,9},{10,11},{12,... | collective-permute-start | bytes 1622024 | tf_op jit(solution)/shard_map/ppermute | solution.py:21
  38.0 13.8 %collective-permute-start.11 = (bf16[32,32,256]{2,1,0:T(8,128)(2,1)S(1)}, bf16[32,32,256]{2,1,0:T(8,128)(2,1)S(1)}, u32[]{:S(2)}, u32[]{:S(2)}) collective-permute-start(bf16[32,32,256]{2,1,0:T(8,128)(2,1)S(1)} %get-tuple-element.61), channel_id=1, source_target_pairs={{0,2},{1,3},{4,6},{5,7},{2,0},{3,1},{6,4},{7,5},{8,10},{9,11},{12,... | collective-permute-start | bytes 1572872 | tf_op jit(solution)/shard_map/ppermute | solution.py:21
  38.7 25.6 %collective-permute-start.12 = (bf16[32,32,256]{2,1,0:T(8,128)(2,1)S(1)}, bf16[32,32,256]{2,1,0:T(8,128)(2,1)S(1)}, u32[]{:S(2)}, u32[]{:S(2)}) collective-permute-start(bf16[32,32,256]{2,1,0:T(8,128)(2,1)S(1)} %get-tuple-element.62), channel_id=1, source_target_pairs={{2,4},{3,5},{6,0},{7,1},{4,2},{5,3},{0,6},{1,7},{10,12},{11,13},{1... | collective-permute-start | bytes 1572872 | tf_op jit(solution)/shard_map/ppermute | solution.py:21
  44.6 20.0 %collective-permute-start.9 = (bf16[32,32,256]{2,1,0:T(8,128)(2,1)S(1)}, bf16[32,32,256]{2,1,0:T(8,128)(2,1)S(1)}, u32[]{:S(2)}, u32[]{:S(2)}) collective-permute-start(bf16[32,32,256]{2,1,0:T(8,128)(2,1)S(1)} %get-tuple-element.58), channel_id=1, source_target_pairs={{0,8},{16,24},{8,0},{24,16},{1,9},{17,25},{9,1},{25,17},{2,10},{18... | collective-permute-start | bytes 1572872 | tf_op jit(solution)/shard_map/ppermute | solution.py:21
  47.9 16.8 %collective-permute-start.10 = (bf16[32,32,256]{2,1,0:T(8,128)(2,1)S(1)}, bf16[32,32,256]{2,1,0:T(8,128)(2,1)S(1)}, u32[]{:S(2)}, u32[]{:S(2)}) collective-permute-start(bf16[32,32,256]{2,1,0:T(8,128)(2,1)S(1)} %get-tuple-element.59), channel_id=1, source_target_pairs={{8,16},{16,8},{9,17},{17,9},{10,18},{18,10},{11,19},{19,11},{12,20... | collective-permute-start | bytes 1572872 | tf_op jit(solution)/shard_map/ppermute | solution.py:21
  65.1 1.9 %collective-permute-start.13 = (bf16[2,64,128]{2,1,0:T(8,128)(2,1)S(1)}, bf16[2,64,128]{2,1,0:T(8,128)(2,1)S(1)}, u32[]{:S(2)}, u32[]{:S(2)}) collective-permute-start(bf16[2,64,128]{2,1,0:T(8,128)(2,1)S(1)} %get-tuple-element.70), channel_id=1, source_target_pairs={{0,1},{2,3},{4,5},{6,7},{1,0},{3,2},{5,4},{7,6},{8,9},{10,11},{12,... | collective-permute-start | bytes 98312 | tf_op jit(solution)/shard_map/ppermute | solution.py:21
  65.2 5.2 %collective-permute-start.14 = (bf16[2,64,128]{2,1,0:T(8,128)(2,1)S(1)}, bf16[2,64,128]{2,1,0:T(8,128)(2,1)S(1)}, u32[]{:S(2)}, u32[]{:S(2)}) collective-permute-start(bf16[2,64,128]{2,1,0:T(8,128)(2,1)S(1)} %get-tuple-element.71), channel_id=1, source_target_pairs={{1,2},{3,4},{5,6},{7,0},{2,1},{4,3},{6,5},{0,7},{9,10},{11,12},{13... | collective-permute-start | bytes 98312 | tf_op jit(solution)/shard_map/ppermute | solution.py:21
  67.0 10.7 %copy-start.4 = (f32[32,256]{1,0:T(8,128)S(1)}, f32[32,256]{1,0:T(8,128)}, u32[]{:S(2)}) copy-start(f32[32,256]{1,0:T(8,128)} %param.19) | copy-start | bytes 98308
  70.6 10.7 %collective-permute-start.15 = (bf16[1,64,256]{2,1,0:T(8,128)(2,1)S(1)}, bf16[1,64,256]{2,1,0:T(8,128)(2,1)S(1)}, u32[]{:S(2)}, u32[]{:S(2)}) collective-permute-start(bf16[1,64,256]{2,1,0:T(8,128)(2,1)S(1)} %get-tuple-element.72), channel_id=1, source_target_pairs={{0,8},{16,24},{8,0},{24,16},{1,9},{17,25},{9,1},{25,17},{2,10},{18... | collective-permute-start | bytes 98312 | tf_op jit(solution)/shard_map/ppermute | solution.py:21
  77.0 4.2 %collective-permute-start.16 = (bf16[1,64,256]{2,1,0:T(8,128)(2,1)S(1)}, bf16[1,64,256]{2,1,0:T(8,128)(2,1)S(1)}, u32[]{:S(2)}, u32[]{:S(2)}) collective-permute-start(bf16[1,64,256]{2,1,0:T(8,128)(2,1)S(1)} %get-tuple-element.73), channel_id=1, source_target_pairs={{8,16},{16,8},{9,17},{17,9},{10,18},{18,10},{11,19},{19,11},{12,20... | collective-permute-start | bytes 98312 | tf_op jit(solution)/shard_map/ppermute | solution.py:21

commit v5 on v3

--- a/solution.py
+++ b/solution.py
@@ -666,10 +666,11 @@
     to_core, to_across = edges(flags[0], parts0, earlier)
     one, other = swap_core(to_core), swap_across(to_across)
     remapped = combine(parts0, parts1)
-    row1, row2 = outer_rows(flags[2], spread, remapped, one, other)
-    row1, row2 = swap_lat(row1, 0), swap_lat(row2, 1)
+    lat = ((my_lat + 1) % 2).astype(jnp.int32).reshape(1)
+    row1, row2 = outer_rows(lat, spread, remapped, one, other)
+    row1, row2 = swap_lat(row1, 1), swap_lat(row2, 0)
     partial, outer = final(zonal_offset, remapped, one, other, kappa, local)
-    return add_halo(flags[2], row1, row2, kappa, outer, partial)
+    return add_halo(lat, row1, row2, kappa, outer, partial)
 
 
 def solution(mesh):

time: 81.1 us -> 87.6 us (1.080)
  starting transfers between devices: 24.4 us -> 30.5 us
  waiting for transfers between devices: 37.4 us -> 31.8 us
  local copies, waits for them, and re-layouts: 3.76 us -> 8.93 us
  Pallas kernels: 14.1 us -> 15.6 us
    ppermute x17, starting transfers between devices: 24.4 us -> 30.5 us  [exchange(): lax.ppermute(value, axis, [(i, j) for i, j in pairs] + [(j, i) for i, j i...]
    ppermute x17, waiting for transfers between devices: 37.4 us -> 31.8 us  [exchange(): lax.ppermute(value, axis, [(i, j) for i, j in pairs] + [(j, i) for i, j i...]
    unnamed x12 -> x28, local copies, waits for them, and re-layouts: 2.14 us -> 7.31 us
    pallas_call x2, Pallas kernels: 4.4 us -> 6.02 us  [sums_call(): pl.pallas_call(kernel, in_specs=[in_smem()] * smem + [in_place()] * (len(...]
  transfers between devices with their start and end apart: 17 -> 17, of which waited for: 6 -> 6; matrix products, arithmetic and copies ran while one was open for 2% -> 2% of each run, Pallas kernels for 13% -> 14%
where the time goes in v5:
time: 87.6 us; the launch traced here: 87.1 us
  waiting for transfers between devices  31.8 us (36%)
  starting transfers between devices  30.5 us (35%)
  Pallas kernels  15.6 us (18%)
  local copies, waits for them, and re-layouts  8.93 us (10%)
    ppermute x17, waiting for transfers between devices, exchange(): lax.ppermute(value, axis, [(i, j) for i, j in pairs] + [(j, i) for i, j i...  31.8 us
    ppermute x17, starting transfers between devices, exchange(): lax.ppermute(value, axis, [(i, j) for i, j in pairs] + [(j, i) for i, j i...  30.5 us
    unnamed x28, local copies, waits for them, and re-layouts  7.31 us
    pallas_call x2, Pallas kernels, sums_call(): pl.pallas_call(kernel, in_specs=[in_smem()] * smem + [in_place()] * (len(...  6.02 us
    pallas_call x1, Pallas kernels, final(): pl.pallas_call(final_kernel, in_specs=[in_smem()] + [vmem] * 5, out_specs...  3.3 us
    pallas_call x1, Pallas kernels, messages(): pl.pallas_call(messages_kernel, in_specs=[in_place()] * 5, out_specs=[pl....  2.29 us
    pallas_call x1, Pallas kernels, local_terms(): pl.pallas_call(growth_kernel, grid=(rows // step,), in_specs=[pl.BlockSpe...  1.81 us
  transfers between devices with their start and end apart: 17, of which 6 were waited for; matrix products, arithmetic and copies ran while one was open for 2% of the time, Pallas kernels for 14%

profile of v5, /device:TPU:0, one launch (start us, length us, event | category | flops | bytes accessed | tf_op | source)
XLA Modules:
  0.0 87.1 jit_solution(7039096444205120309)
XLA Ops:
  0.0 2.3 %messages.1 = (bf16[33,32,256]{2,1,0:T(8,128)(2,1)}, bf16[33,32,256]{2,1,0:T(8,128)(2,1)}, bf16[1,32,256]{2,1,0:T(8,128)(2,1)}) custom-call(bf16[32,64,256]{2,1,0:T(8,128)(2,1)} %refs_0_.1, s32[4,32]{1,0:T(4,128)} %bitcast.14, s32[4,32]{1,0:T(4,128)} %bitcast.15, f32[4,32]{1,0:T(4,128)} %bitcast.16, s32[1,32]{1,0:T(1,128)} %count_hbm.1), custom_call_target="tpu_custom_call" | custom-call | bytes 2097152 | tf_op jit(solution)/shard_map/messages/pallas_call | solution.py:150
  2.3 3.0 %collective-permute-start = (bf16[33,32,256]{2,1,0:T(8,128)(2,1)}, bf16[33,32,256]{2,1,0:T(8,128)(2,1)S(1)}, u32[]{:S(2)}, u32[]{:S(2)}) collective-permute-start(bf16[33,32,256]{2,1,0:T(8,128)(2,1)} %get-tuple-element.40), channel_id=1, source_target_pairs={{0,8},{16,24},{8,0},{24,16},{1,9},{17,25},{9,1},{25,17},{2,10},{18... | collective-permute-start | bytes 1622024 | tf_op jit(solution)/shard_map/ppermute | solution.py:21
  6.0 1.6 %collective-permute-start.2 = (bf16[33,32,256]{2,1,0:T(8,128)(2,1)}, bf16[33,32,256]{2,1,0:T(8,128)(2,1)}, u32[]{:S(2)}, u32[]{:S(2)}) collective-permute-start(bf16[33,32,256]{2,1,0:T(8,128)(2,1)} %get-tuple-element.47), channel_id=1, source_target_pairs={{0,2},{1,3},{4,6},{5,7},{2,0},{3,1},{6,4},{7,5},{8,10},{9,11},{12,... | collective-permute-start | bytes 1622024 | tf_op jit(solution)/shard_map/ppermute | solution.py:21
  7.6 2.5 %collective-permute-start.3 = (bf16[33,32,256]{2,1,0:T(8,128)(2,1)}, bf16[33,32,256]{2,1,0:T(8,128)(2,1)}, u32[]{:S(2)}, u32[]{:S(2)}) collective-permute-start(bf16[33,32,256]{2,1,0:T(8,128)(2,1)} %get-tuple-element.47), channel_id=1, source_target_pairs={{2,4},{3,5},{6,0},{7,1},{4,2},{5,3},{0,6},{1,7},{10,12},{11,13},{1... | collective-permute-start | bytes 1622024 | tf_op jit(solution)/shard_map/ppermute | solution.py:21
  11.7 1.2 %copy-done = bf16[32,64,256]{2,1,0:T(8,128)(2,1)S(1)} copy-done((bf16[32,64,256]{2,1,0:T(8,128)(2,1)S(1)}, bf16[32,64,256]{2,1,0:T(8,128)(2,1)}, u32[]{:S(2)}) %copy-start) | copy-done | bytes 1048600
  12.9 0.9 %copy-done.10 = f32[4,32,256]{2,1,0:T(8,128)S(1)} copy-done((f32[4,32,256]{2,1,0:T(8,128)S(1)}, f32[4,32,256]{2,1,0:T(8,128)}, u32[]{:S(2)}) %copy-start.10) | copy-done | bytes 131096
  13.8 1.8 %growth.1.local_ref = f32[32,64,256]{2,1,0:T(8,128)S(1)} custom-call(f32[4,128]{1,0:T(4,128)S(1)} %pad_convert_fusion.flip_ref, f32[64,1]{1,0:T(8,128)S(1)} %copy.12.settle_ref, bf16[32,64,256]{2,1,0:T(8,128)(2,1)S(1)} %copy-done, f32[4,32,256]{2,1,0:T(8,128)S(1)} %copy-done.10), custom_call_target="tpu_custom_call" | custom-call | flops 268435456 | bytes 4194304 | tf_op jit(solution)/shard_map/growth/pallas_call | solution.py:90
  15.6 1.3 %copy-done.2 = f32[32,64,256]{2,1,0:T(8,128)} copy-done((f32[32,64,256]{2,1,0:T(8,128)}, f32[32,64,256]{2,1,0:T(8,128)S(1)}, u32[]{:S(2)}) %copy-start.2) | copy-done | bytes 2097176
  16.9 1.7 %collective-permute-done.refs_3_.refs_6_ = bf16[33,32,256]{2,1,0:T(8,128)(2,1)S(1)} collective-permute-done((bf16[33,32,256]{2,1,0:T(8,128)(2,1)}, bf16[33,32,256]{2,1,0:T(8,128)(2,1)S(1)}, u32[]{:S(2)}, u32[]{:S(2)}) %collective-permute-start) | collective-permute-done | bytes 540704 | tf_op jit(solution)/shard_map/ppermute | solution.py:21
  19.5 1.2 %collective-permute-done.2.refs_3_.refs_2_ = bf16[33,32,256]{2,1,0:T(8,128)(2,1)} collective-permute-done((bf16[33,32,256]{2,1,0:T(8,128)(2,1)}, bf16[33,32,256]{2,1,0:T(8,128)(2,1)}, u32[]{:S(2)}, u32[]{:S(2)}) %collective-permute-start.2) | collective-permute-done | bytes 540704 | tf_op jit(solution)/shard_map/ppermute | solution.py:21
  20.7 13.2 %collective-permute-done.3.refs_5_.refs_3_ = bf16[33,32,256]{2,1,0:T(8,128)(2,1)} collective-permute-done((bf16[33,32,256]{2,1,0:T(8,128)(2,1)}, bf16[33,32,256]{2,1,0:T(8,128)(2,1)}, u32[]{:S(2)}, u32[]{:S(2)}) %collective-permute-start.3) | collective-permute-done | bytes 540704 | tf_op jit(solution)/shard_map/ppermute | solution.py:21
  33.9 2.8 %lon_sums.1 = (bf16[32,32,256]{2,1,0:T(8,128)(2,1)S(1)}, f32[32,32,256]{2,1,0:T(8,128)S(1)}, bf16[32,32,256]{2,1,0:T(8,128)(2,1)S(1)}) custom-call(s32[1]{0:T(128)} %bitcast.8.refs_0_.core_ref, s32[1]{0:T(128)} %bitcast.9.refs_1_.chip_ref, s32[1]{0:T(128)} %bitcast.10.refs_2_, bf16[33,32,256]{2,1,0:T(8,128)(2,1)} %collective-permute-done.2.refs_3_.refs_2_, ...), custom_call_target="tpu_custom_call" | custom-call | flops 6291456 | bytes 4718592 | tf_op jit(solution)/shard_map/lon_sums/pallas_call | solution.py:341
  37.5 2.7 %collective-permute-start.12 = (bf16[32,32,256]{2,1,0:T(8,128)(2,1)S(1)}, bf16[32,32,256]{2,1,0:T(8,128)(2,1)S(1)}, u32[]{:S(2)}, u32[]{:S(2)}) collective-permute-start(bf16[32,32,256]{2,1,0:T(8,128)(2,1)S(1)} %get-tuple-element.60), channel_id=1, source_target_pairs={{2,4},{3,5},{6,0},{7,1},{4,2},{5,3},{0,6},{1,7},{10,12},{11,13},{1... | collective-permute-start | bytes 1572872 | tf_op jit(solution)/shard_map/ppermute | solution.py:21
  40.2 1.2 %copy-done.9 = bf16[32,64,256]{2,1,0:T(8,128)(2,1)S(1)} copy-done((bf16[32,64,256]{2,1,0:T(8,128)(2,1)S(1)}, bf16[32,64,256]{2,1,0:T(8,128)(2,1)}, u32[]{:S(2)}) %copy-start.9) | copy-done | bytes 1048600
  41.5 3.2 %lat_sums.1 = (bf16[32,32,256]{2,1,0:T(8,128)(2,1)S(1)}, f32[32,32,256]{2,1,0:T(8,128)S(1)}, bf16[32,32,256]{2,1,0:T(8,128)(2,1)S(1)}) custom-call(s32[1]{0:T(128)} %bitcast.8.refs_0_.core_ref, s32[1]{0:T(128)} %bitcast.9.refs_1_.chip_ref, s32[16,128]{1,0:T(8,128)S(1)} %get-tuple-element.53.index_ref, f32[16,128]{1,0:T(8,128)S(1)} %get-tuple-element.54.weight_ref, ...), custom_call_target="tpu_custom_call" | custom-call | flops 6291456 | bytes 4718592 | tf_op jit(solution)/shard_map/lat_sums/pallas_call | solution.py:341
  44.6 4.0 %collective-permute-start.9 = (bf16[32,32,256]{2,1,0:T(8,128)(2,1)S(1)}, bf16[32,32,256]{2,1,0:T(8,128)(2,1)S(1)}, u32[]{:S(2)}, u32[]{:S(2)}) collective-permute-start(bf16[32,32,256]{2,1,0:T(8,128)(2,1)S(1)} %get-tuple-element.56), channel_id=1, source_target_pairs={{0,8},{16,24},{8,0},{24,16},{1,9},{17,25},{9,1},{25,17},{2,10},{18... | collective-permute-start | bytes 1572872 | tf_op jit(solution)/shard_map/ppermute | solution.py:21
  49.3 2.0 %collective-permute-done.11.refs_1_.refs_4_.a1 = bf16[32,32,256]{2,1,0:T(8,128)(2,1)S(1)} collective-permute-done((bf16[32,32,256]{2,1,0:T(8,128)(2,1)S(1)}, bf16[32,32,256]{2,1,0:T(8,128)(2,1)S(1)}, u32[]{:S(2)}, u32[]{:S(2)}) %collective-permute-start.11) | collective-permute-done | bytes 524320 | tf_op jit(solution)/shard_map/ppermute | solution.py:21
  51.3 12.4 %collective-permute-done.12.refs_2_.refs_5_.b1 = bf16[32,32,256]{2,1,0:T(8,128)(2,1)S(1)} collective-permute-done((bf16[32,32,256]{2,1,0:T(8,128)(2,1)S(1)}, bf16[32,32,256]{2,1,0:T(8,128)(2,1)S(1)}, u32[]{:S(2)}, u32[]{:S(2)}) %collective-permute-start.12) | collective-permute-done | bytes 524320 | tf_op jit(solution)/shard_map/ppermute | solution.py:21
  65.1 1.4 %collective-permute-start.14 = (bf16[2,64,128]{2,1,0:T(8,128)(2,1)S(1)}, bf16[2,64,128]{2,1,0:T(8,128)(2,1)S(1)}, u32[]{:S(2)}, u32[]{:S(2)}) collective-permute-start(bf16[2,64,128]{2,1,0:T(8,128)(2,1)S(1)} %get-tuple-element.69), channel_id=1, source_target_pairs={{1,2},{3,4},{5,6},{7,0},{2,1},{4,3},{6,5},{0,7},{9,10},{11,12},{13... | collective-permute-start | bytes 98312 | tf_op jit(solution)/shard_map/ppermute | solution.py:21
  66.5 1.0 %copy-done.5 = bf16[32,32,256]{2,1,0:T(8,128)(2,1)S(1)} copy-done((bf16[32,32,256]{2,1,0:T(8,128)(2,1)S(1)}, bf16[32,32,256]{2,1,0:T(8,128)(2,1)}, u32[]{:S(2)}) %copy-start.5) | copy-done | bytes 524312
  67.5 1.0 %copy-done.7 = bf16[32,32,256]{2,1,0:T(8,128)(2,1)S(1)} copy-done((bf16[32,32,256]{2,1,0:T(8,128)(2,1)S(1)}, bf16[32,32,256]{2,1,0:T(8,128)(2,1)}, u32[]{:S(2)}) %copy-start.7) | copy-done | bytes 524312
  68.9 1.3 %collective-permute-done.14.other_ref = bf16[2,64,128]{2,1,0:T(8,128)(2,1)S(1)} collective-permute-done((bf16[2,64,128]{2,1,0:T(8,128)(2,1)S(1)}, bf16[2,64,128]{2,1,0:T(8,128)(2,1)S(1)}, u32[]{:S(2)}, u32[]{:S(2)}) %collective-permute-start.14) | collective-permute-done | bytes 32800 | tf_op jit(solution)/shard_map/ppermute | solution.py:21
  71.3 11.8 %collective-permute-start.16 = (bf16[1,64,256]{2,1,0:T(8,128)(2,1)S(1)}, bf16[1,64,256]{2,1,0:T(8,128)(2,1)S(1)}, u32[]{:S(2)}, u32[]{:S(2)}) collective-permute-start(bf16[1,64,256]{2,1,0:T(8,128)(2,1)S(1)} %get-tuple-element.71), channel_id=1, source_target_pairs={{0,8},{16,24},{8,0},{24,16},{1,9},{17,25},{9,1},{25,17},{2,10},{18... | collective-permute-start | bytes 98312 | tf_op jit(solution)/shard_map/ppermute | solution.py:21
  83.1 3.3 %final.1 = (f32[32,64,256]{2,1,0:T(8,128)}, f32[2,64,256]{2,1,0:T(8,128)S(1)}) custom-call(s32[32]{0:T(128)S(1)} %copy-done.12, f32[32,64,256]{2,1,0:T(8,128)S(1)} %combine.1.first_row.last_row.remap_ref, bf16[2,64,128]{2,1,0:T(8,128)(2,1)S(1)} %collective-permute-done.13.one_ref, bf16[2,64,128]{2,1,0:T(8,128)(2,1)S(1)} %collective-permute-done.14.other_ref, ...), custom_call_target="tpu_custom_call" | custom-call | flops 15728640 | bytes 6291456 | tf_op jit(solution)/shard_map/final/pallas_call | solution.py:564
  (54 shorter events, 7.9 us)
Async XLA Ops:
  2.3 16.3 %copy-start.11 = (bf16[1,32,256]{2,1,0:T(8,128)(2,1)S(1)}, bf16[1,32,256]{2,1,0:T(8,128)(2,1)}, u32[]{:S(2)}) copy-start(bf16[1,32,256]{2,1,0:T(8,128)(2,1)} %get-tuple-element.43.refs_4_) | copy-start | bytes 49156
  2.3 16.3 %collective-permute-start = (bf16[33,32,256]{2,1,0:T(8,128)(2,1)}, bf16[33,32,256]{2,1,0:T(8,128)(2,1)S(1)}, u32[]{:S(2)}, u32[]{:S(2)}) collective-permute-start(bf16[33,32,256]{2,1,0:T(8,128)(2,1)} %get-tuple-element.40), channel_id=1, source_target_pairs={{0,8},{16,24},{8,0},{24,16},{1,9},{17,25},{9,1},{25,17},{2,10},{18... | collective-permute-start | bytes 1622024 | tf_op jit(solution)/shard_map/ppermute | solution.py:21
  5.3 13.3 %collective-permute-start.1 = (bf16[33,32,256]{2,1,0:T(8,128)(2,1)}, bf16[33,32,256]{2,1,0:T(8,128)(2,1)S(1)}, u32[]{:S(2)}, u32[]{:S(2)}) collective-permute-start(bf16[33,32,256]{2,1,0:T(8,128)(2,1)} %get-tuple-element.40), channel_id=1, source_target_pairs={{8,16},{16,8},{9,17},{17,9},{10,18},{18,10},{11,19},{19,11},{12,20... | collective-permute-start | bytes 1622024 | tf_op jit(solution)/shard_map/ppermute | solution.py:21
  6.0 14.7 %collective-permute-start.2 = (bf16[33,32,256]{2,1,0:T(8,128)(2,1)}, bf16[33,32,256]{2,1,0:T(8,128)(2,1)}, u32[]{:S(2)}, u32[]{:S(2)}) collective-permute-start(bf16[33,32,256]{2,1,0:T(8,128)(2,1)} %get-tuple-element.47), channel_id=1, source_target_pairs={{0,2},{1,3},{4,6},{5,7},{2,0},{3,1},{6,4},{7,5},{8,10},{9,11},{12,... | collective-permute-start | bytes 1622024 | tf_op jit(solution)/shard_map/ppermute | solution.py:21
  7.6 26.2 %collective-permute-start.3 = (bf16[33,32,256]{2,1,0:T(8,128)(2,1)}, bf16[33,32,256]{2,1,0:T(8,128)(2,1)}, u32[]{:S(2)}, u32[]{:S(2)}) collective-permute-start(bf16[33,32,256]{2,1,0:T(8,128)(2,1)} %get-tuple-element.47), channel_id=1, source_target_pairs={{2,4},{3,5},{6,0},{7,1},{4,2},{5,3},{0,6},{1,7},{10,12},{11,13},{1... | collective-permute-start | bytes 1622024 | tf_op jit(solution)/shard_map/ppermute | solution.py:21
  10.1 23.7 %collective-permute-start.5 = (bf16[32,64,256]{2,1,0:T(8,128)(2,1)}, bf16[32,64,256]{2,1,0:T(8,128)(2,1)S(1)}, u32[]{:S(2)}, u32[]{:S(2)}) collective-permute-start(bf16[32,64,256]{2,1,0:T(8,128)(2,1)} %refs_0_.1), channel_id=1, source_target_pairs={{0,1},{2,3},{4,5},{6,7},{1,0},{3,2},{5,4},{7,6},{8,9},{10,11},{12,... | collective-permute-start | bytes 3145736 | tf_op jit(solution)/shard_map/ppermute | solution.py:21
  13.8 5.0 %copy-start.12 = (s32[32]{0:T(128)S(1)}, s32[32]{0:T(128)}, u32[]{:S(2)}) copy-start(s32[32]{0:T(128)} %offset_ref.1) | copy-start | bytes 388
  13.8 20.1 %copy-start.1 = (bf16[32,64,256]{2,1,0:T(8,128)(2,1)S(1)}, bf16[32,64,256]{2,1,0:T(8,128)(2,1)}, u32[]{:S(2)}) copy-start(bf16[32,64,256]{2,1,0:T(8,128)(2,1)} %refs_0_.1) | copy-start | bytes 3145732
  15.6 1.3 %copy-start.2 = (f32[32,64,256]{2,1,0:T(8,128)}, f32[32,64,256]{2,1,0:T(8,128)S(1)}, u32[]{:S(2)}) copy-start(f32[32,64,256]{2,1,0:T(8,128)S(1)} %growth.1.local_ref) | copy-start | bytes 6291460
  18.9 15.0 %collective-permute-start.4 = (bf16[33,32,256]{2,1,0:T(8,128)(2,1)S(1)}, bf16[33,32,256]{2,1,0:T(8,128)(2,1)S(1)}, u32[]{:S(2)}, u32[]{:S(2)}) collective-permute-start(bf16[33,32,256]{2,1,0:T(8,128)(2,1)S(1)} %collective-permute-done.refs_3_.refs_6_), channel_id=1, source_target_pairs={{0,1},{2,3},{4,5},{6,7},{1,0},{3,2},{5,4},{7,6},{8,9},{10,11},{12,... | collective-permute-start | bytes 1622024 | tf_op jit(solution)/shard_map/ppermute | solution.py:21
  19.0 14.9 %collective-permute-start.6 = (bf16[33,32,256]{2,1,0:T(8,128)(2,1)S(1)}, bf16[33,32,256]{2,1,0:T(8,128)(2,1)S(1)}, u32[]{:S(2)}, u32[]{:S(2)}) collective-permute-start(bf16[33,32,256]{2,1,0:T(8,128)(2,1)S(1)} %collective-permute-done.1.refs_5_.refs_8_), channel_id=1, source_target_pairs={{0,1},{2,3},{4,5},{6,7},{1,0},{3,2},{5,4},{7,6},{8,9},{10,11},{12,... | collective-permute-start | bytes 1622024 | tf_op jit(solution)/shard_map/ppermute | solution.py:21
  20.7 19.5 %collective-permute-start.7 = (bf16[33,32,256]{2,1,0:T(8,128)(2,1)}, bf16[33,32,256]{2,1,0:T(8,128)(2,1)S(1)}, u32[]{:S(2)}, u32[]{:S(2)}) collective-permute-start(bf16[33,32,256]{2,1,0:T(8,128)(2,1)} %collective-permute-done.2.refs_3_.refs_2_), channel_id=1, source_target_pairs={{0,1},{2,3},{4,5},{6,7},{1,0},{3,2},{5,4},{7,6},{8,9},{10,11},{12,... | collective-permute-start | bytes 1622024 | tf_op jit(solution)/shard_map/ppermute | solution.py:21
  33.8 6.4 %collective-permute-start.8 = (bf16[33,32,256]{2,1,0:T(8,128)(2,1)}, bf16[33,32,256]{2,1,0:T(8,128)(2,1)S(1)}, u32[]{:S(2)}, u32[]{:S(2)}) collective-permute-start(bf16[33,32,256]{2,1,0:T(8,128)(2,1)} %collective-permute-done.3.refs_5_.refs_3_), channel_id=1, source_target_pairs={{0,1},{2,3},{4,5},{6,7},{1,0},{3,2},{5,4},{7,6},{8,9},{10,11},{12,... | collective-permute-start | bytes 1622024 | tf_op jit(solution)/shard_map/ppermute | solution.py:21
  33.8 2.9 %copy-start.8 = (bf16[32,64,256]{2,1,0:T(8,128)(2,1)}, bf16[32,64,256]{2,1,0:T(8,128)(2,1)S(1)}, u32[]{:S(2)}) copy-start(bf16[32,64,256]{2,1,0:T(8,128)(2,1)S(1)} %collective-permute-done.5.refs_10_.refs_1_) | copy-start | bytes 3145732
  36.7 14.5 %collective-permute-start.11 = (bf16[32,32,256]{2,1,0:T(8,128)(2,1)S(1)}, bf16[32,32,256]{2,1,0:T(8,128)(2,1)S(1)}, u32[]{:S(2)}, u32[]{:S(2)}) collective-permute-start(bf16[32,32,256]{2,1,0:T(8,128)(2,1)S(1)} %get-tuple-element.59), channel_id=1, source_target_pairs={{0,2},{1,3},{4,6},{5,7},{2,0},{3,1},{6,4},{7,5},{8,10},{9,11},{12,... | collective-permute-start | bytes 1572872 | tf_op jit(solution)/shard_map/ppermute | solution.py:21
  37.5 26.2 %collective-permute-start.12 = (bf16[32,32,256]{2,1,0:T(8,128)(2,1)S(1)}, bf16[32,32,256]{2,1,0:T(8,128)(2,1)S(1)}, u32[]{:S(2)}, u32[]{:S(2)}) collective-permute-start(bf16[32,32,256]{2,1,0:T(8,128)(2,1)S(1)} %get-tuple-element.60), channel_id=1, source_target_pairs={{2,4},{3,5},{6,0},{7,1},{4,2},{5,3},{0,6},{1,7},{10,12},{11,13},{1... | collective-permute-start | bytes 1572872 | tf_op jit(solution)/shard_map/ppermute | solution.py:21
  44.6 19.5 %collective-permute-start.9 = (bf16[32,32,256]{2,1,0:T(8,128)(2,1)S(1)}, bf16[32,32,256]{2,1,0:T(8,128)(2,1)S(1)}, u32[]{:S(2)}, u32[]{:S(2)}) collective-permute-start(bf16[32,32,256]{2,1,0:T(8,128)(2,1)S(1)} %get-tuple-element.56), channel_id=1, source_target_pairs={{0,8},{16,24},{8,0},{24,16},{1,9},{17,25},{9,1},{25,17},{2,10},{18... | collective-permute-start | bytes 1572872 | tf_op jit(solution)/shard_map/ppermute | solution.py:21
  48.6 15.5 %collective-permute-start.10 = (bf16[32,32,256]{2,1,0:T(8,128)(2,1)S(1)}, bf16[32,32,256]{2,1,0:T(8,128)(2,1)S(1)}, u32[]{:S(2)}, u32[]{:S(2)}) collective-permute-start(bf16[32,32,256]{2,1,0:T(8,128)(2,1)S(1)} %get-tuple-element.57), channel_id=1, source_target_pairs={{8,16},{16,8},{9,17},{17,9},{10,18},{18,10},{11,19},{19,11},{12,20... | collective-permute-start | bytes 1572872 | tf_op jit(solution)/shard_map/ppermute | solution.py:21
  65.1 3.8 %collective-permute-start.13 = (bf16[2,64,128]{2,1,0:T(8,128)(2,1)S(1)}, bf16[2,64,128]{2,1,0:T(8,128)(2,1)S(1)}, u32[]{:S(2)}, u32[]{:S(2)}) collective-permute-start(bf16[2,64,128]{2,1,0:T(8,128)(2,1)S(1)} %get-tuple-element.68), channel_id=1, source_target_pairs={{0,1},{2,3},{4,5},{6,7},{1,0},{3,2},{5,4},{7,6},{8,9},{10,11},{12,... | collective-permute-start | bytes 98312 | tf_op jit(solution)/shard_map/ppermute | solution.py:21
  65.1 5.1 %collective-permute-start.14 = (bf16[2,64,128]{2,1,0:T(8,128)(2,1)S(1)}, bf16[2,64,128]{2,1,0:T(8,128)(2,1)S(1)}, u32[]{:S(2)}, u32[]{:S(2)}) collective-permute-start(bf16[2,64,128]{2,1,0:T(8,128)(2,1)S(1)} %get-tuple-element.69), channel_id=1, source_target_pairs={{1,2},{3,4},{5,6},{7,0},{2,1},{4,3},{6,5},{0,7},{9,10},{11,12},{13... | collective-permute-start | bytes 98312 | tf_op jit(solution)/shard_map/ppermute | solution.py:21
  70.2 12.8 %copy-start.13 = (f32[32,256]{1,0:T(8,128)S(1)}, f32[32,256]{1,0:T(8,128)}, u32[]{:S(2)}) copy-start(f32[32,256]{1,0:T(8,128)} %param.19) | copy-start | bytes 98308
  70.2 12.8 %copy-start.3 = (f32[32,64,256]{2,1,0:T(8,128)S(1)}, f32[32,64,256]{2,1,0:T(8,128)}, u32[]{:S(2)}) copy-start(f32[32,64,256]{2,1,0:T(8,128)} %copy-done.2) | copy-start | bytes 6291460
  70.5 16.0 %collective-permute-start.15 = (bf16[1,64,256]{2,1,0:T(8,128)(2,1)S(1)}, bf16[1,64,256]{2,1,0:T(8,128)(2,1)S(1)}, u32[]{:S(2)}, u32[]{:S(2)}) collective-permute-start(bf16[1,64,256]{2,1,0:T(8,128)(2,1)S(1)} %get-tuple-element.70), channel_id=1, source_target_pairs={{8,16},{16,8},{9,17},{17,9},{10,18},{18,10},{11,19},{19,11},{12,20... | collective-permute-start | bytes 98312 | tf_op jit(solution)/shard_map/ppermute | solution.py:21
  71.3 15.2 %collective-permute-start.16 = (bf16[1,64,256]{2,1,0:T(8,128)(2,1)S(1)}, bf16[1,64,256]{2,1,0:T(8,128)(2,1)S(1)}, u32[]{:S(2)}, u32[]{:S(2)}) collective-permute-start(bf16[1,64,256]{2,1,0:T(8,128)(2,1)S(1)} %get-tuple-element.71), channel_id=1, source_target_pairs={{0,8},{16,24},{8,0},{24,16},{1,9},{17,25},{9,1},{25,17},{2,10},{18... | collective-permute-start | bytes 98312 | tf_op jit(solution)/shard_map/ppermute | solution.py:21
  (7 other events, 7.2 us)
